TPU v7x, 512 devices: a whole 4x4x16 slice. The times are simulated.
512 devices in a mesh: grid: 2 (over core), lat: 8 (over z_lo), lon: 32 (over x, y, z_hi).
Axes of the slice: x: 4, y: 4, z: 16 (z_hi: 2, z_lo: 8; z = z_hi * 8 + z_lo), core: 2. Of those that a mesh axis runs over, the one named last changes fastest.
Arguments:
- velocity: float32 [2, 3, 8, 1024, 1024], P('grid', None, None, 'lon', 'lat'), may hold values from -6 to 6
- magnetic: float32 [2, 3, 8, 1024, 1024], P('grid', None, None, 'lon', 'lat'), may hold values from -6 to 6
- pair_rows: int32 [2, 8, 32, 32], P('grid', 'lat', 'lon'), may hold values from 0 to 16, as said below
- send_cell: int32 [2, 8, 32, 512], P('grid', 'lat', 'lon'), may hold values from 0 to 4095
- send_weight: float32 [2, 8, 32, 512], P('grid', 'lat', 'lon'), may hold values from 0.25 to 1
- cycle_slot: int32 [2, 8, 32, 512], P('grid', 'lat', 'lon'), may hold values from 0 to 127
Outputs:
- new_velocity: float32 [2, 3, 8, 1024, 1024], P('grid', None, None, 'lon', 'lat')
- new_magnetic: float32 [2, 3, 8, 1024, 1024], P('grid', None, None, 'lon', 'lat')
- cycle_values: float32 [2, 8, 32, 48, 128], P('grid', 'lat', 'lon')
Inputs may be any that keep to these rules, and one draw needn't show every extreme that they name: `pair_rows`: at most 16 rows go from one donor block to one longitude block; the first and the last longitude block receive exactly 16 from every donor block. `send_cell`: A cell of the donor block.
All inputs are finite; a program needn't handle non-finite values.
Results may differ from a plain program's by a relative error of at most 0.0001.
Values sent between devices are 32-bit elements; how exact they have to be, the bound alone decides.
No kernel may reach another device: no remote copies, remote signals or barrier semaphores. Data moves between devices by JAX's collectives and lax.ppermute only.
A program may use at most 64 MiB of HBM per device.

v0:
```python
import math

import jax
import jax.numpy as jnp
from jax import lax
from jax.sharding import PartitionSpec as P

CAP = 16
CYCLE = 128


inner_radius = 0.6
smag_const = 0.2
aniso_weight = 0.8
turb_prandtl = 0.7
courant = 0.2
sym_index = ((0, 1, 2), (1, 3, 4), (2, 4, 5))
flux_pairs = ((0, 0), (0, 1), (0, 2), (1, 1), (1, 2), (2, 2))


def from_partner(block, axis, distance):
    count = lax.axis_size(axis)
    route = []
    for low in range(count):
        high = low | 1 << distance
        if high != low and high < count:
            route += [(low, high), (high, low)]
    return lax.ppermute(block, axis, route)


def with_halo(block, sides, width):
    for axis, dim in sides:
        count = lax.axis_size(axis)
        forward = [(i, i + 1) for i in range(count - 1)]
        backward = [(target, source) for source, target in forward]
        low = lax.ppermute(
            lax.slice_in_dim(block, block.shape[dim] - width, None, axis=dim), axis, forward
        )
        high = lax.ppermute(lax.slice_in_dim(block, 0, width, axis=dim), axis, backward)
        block = jnp.concatenate([low, block, high], axis=dim)
    return block


def coefficients(theta_index, total_t, total_p, levels):
    theta_step = 0.5 * math.pi / total_t
    phi_step = 1.5 * math.pi / total_p
    spacing = inner_radius * theta_step
    radius = inner_radius + (jnp.arange(levels, dtype=jnp.float32) + 0.5) * spacing
    theta = 0.25 * math.pi + (theta_index.astype(jnp.float32) + 0.5) * theta_step
    coef_theta = (0.5 / (theta_step * radius))[:, None, None]
    coef_phi = 0.5 / (phi_step * radius[:, None, None] * jnp.sin(theta)[None, None, :])
    return (coef_theta, coef_phi, spacing, courant * spacing)


def radial(field, spacing):
    inner = (field[:, 2:] - field[:, :-2]) * (0.5 / spacing)
    lower = (field[:, 1:2] - field[:, :1]) * (1.0 / spacing)
    upper = (field[:, -1:] - field[:, -2:-1]) * (1.0 / spacing)
    return jnp.concatenate([lower, inner, upper], axis=1)


def derivatives(padded, coefs):
    coef_theta, coef_phi, spacing, time_step = coefs
    center = padded[:, :, 1:-1, 1:-1]
    along_theta = (padded[:, :, 1:-1, 2:] - padded[:, :, 1:-1, :-2]) * coef_theta
    along_phi = (padded[:, :, 2:, 1:-1] - padded[:, :, :-2, 1:-1]) * coef_phi
    return (center, (radial(center, spacing), along_theta, along_phi))


def fluxes(padded, coefs):
    spacing = coefs[2]
    center, grads = derivatives(padded, coefs)
    speed = center[0:3]
    field = center[3:6]
    grad_u = [[grads[col][row] for col in range(3)] for row in range(3)]
    grad_b = [[grads[col][row + 3] for col in range(3)] for row in range(3)]
    strain = [[0.5 * (grad_u[row][col] + grad_u[col][row]) for col in range(3)] for row in range(3)]
    magnitude = jnp.sqrt(
        2.0 * sum((strain[row][col] * strain[row][col] for row in range(3) for col in range(3)))
    )
    viscous = (smag_const * spacing) ** 2 * magnitude
    field_sq = field[0] * field[0] + field[1] * field[1] + field[2] * field[2]
    scaling = 1.0 / jnp.sqrt(field_sq + 1.0)
    unit = [field[comp] * scaling for comp in range(3)]
    aligned = sum(
        (unit[row] * strain[row][col] * unit[col] for row in range(3) for col in range(3))
    )
    parts = []
    for row, col in flux_pairs:
        value = speed[row] * speed[col] - field[row] * field[col]
        value = value - 2.0 * viscous * (
            strain[row][col] - aniso_weight * unit[row] * unit[col] * aligned
        )
        if row == col:
            value = value + 0.5 * field_sq
        parts.append(value)
    current = [
        grad_b[2][1] - grad_b[1][2],
        grad_b[0][2] - grad_b[2][0],
        grad_b[1][0] - grad_b[0][1],
    ]
    cross = [
        speed[1] * field[2] - speed[2] * field[1],
        speed[2] * field[0] - speed[0] * field[2],
        speed[0] * field[1] - speed[1] * field[0],
    ]
    for comp in range(3):
        parts.append(cross[comp] - viscous / turb_prandtl * current[comp])
    return jnp.stack(parts)


def advance(state, flux_pad, coefs):
    time_step = coefs[3]
    unused, grads = derivatives(flux_pad, coefs)
    result = []
    for row in range(3):
        spread = (
            grads[0][sym_index[row][0]] + grads[1][sym_index[row][1]] + grads[2][sym_index[row][2]]
        )
        result.append(state[row] - time_step * spread)
    curls = [grads[1][8] - grads[2][7], grads[2][6] - grads[0][8], grads[0][7] - grads[1][6]]
    for row in range(3):
        result.append(state[row + 3] + time_step * curls[row])
    return jnp.stack(result)


def route_lon(payload):
    return (
        lax.all_to_all(payload[0], "lon", split_axis=1, concat_axis=1, tiled=True),
        lax.all_to_all(payload[1], "lon", split_axis=1, concat_axis=1, tiled=True),
    )


def route_grid(payload):
    return from_partner((payload[0], payload[1]), "grid", 0)


def local(velocity, magnetic, pair_rows, send_cell, send_weight, cycle_slot):
    state = jnp.concatenate([velocity[0], magnetic[0]], axis=0)
    levels, cells_p, cells_t = (state.shape[1], state.shape[2], state.shape[3])
    total_t = cells_t * lax.axis_size("lat")
    total_p = cells_p * lax.axis_size("lon")
    first_t = lax.axis_index("lat") * cells_t
    own_t = first_t + jnp.arange(cells_t, dtype=jnp.int32)
    coefs = coefficients(own_t, total_t, total_p, levels)
    padded = with_halo(state, (("lat", 3), ("lon", 2)), 1)
    flux = fluxes(padded, coefs)
    flux_pad = with_halo(flux, (("lat", 3), ("lon", 2)), 1)
    updated = advance(state, flux_pad, coefs)
    flat = updated.reshape(6 * levels, cells_p * cells_t)
    cells = send_cell[0, 0, 0]
    slots_total = cells.shape[0]
    bucket_pos = jnp.arange(slots_total, dtype=jnp.int32) % CAP
    counts = jnp.repeat(pair_rows[0, 0, 0], CAP, total_repeat_length=slots_total)
    scale = jnp.where(bucket_pos < counts, send_weight[0, 0, 0], jnp.float32(0.0))
    values = jnp.take(flat, cells, axis=1) * scale[None]
    slots = cycle_slot[0, 0, 0][None]
    values, slots = route_lon((values, slots))
    values, slots = route_grid((values, slots))
    onehot = (slots[0][:, None] == jnp.arange(CYCLE, dtype=jnp.int32)[None, :]).astype(jnp.float32)
    cycle = jnp.dot(values, onehot, precision=lax.Precision.HIGHEST)
    return (updated[0:3][None], updated[3:6][None], cycle[None, None, None])


def solution(mesh):
    placed = (
        P("grid", None, None, "lon", "lat"),
        P("grid", None, None, "lon", "lat"),
        P("grid", "lat", "lon", None),
        P("grid", "lat", "lon", None),
        P("grid", "lat", "lon", None),
        P("grid", "lat", "lon", None),
    )
    return jax.shard_map(
        local,
        mesh=mesh,
        in_specs=placed,
        out_specs=(
            P("grid", None, None, "lon", "lat"),
            P("grid", None, None, "lon", "lat"),
            P("grid", "lat", "lon", None, None),
        ),
        check_vma=False,
    )
```

profile of v0, /device:TPU:1, one launch (start us, length us, event | category | flops | bytes accessed | tf_op | source)
XLA Modules:
  0.0 183.9 jit_solution(16304200002593426648)
XLA Ops:
  0.6 1.7 fusion.6
  2.3 0.9 copy.194
  3.3 1.3 collective-permute-start
  4.6 1.0 copy.195
  5.5 5.6 %collective-permute-start.1 = (f32[6,8,32,1]{2,1,3,0:T(8,128)}, f32[6,8,32,1]{2,1,3,0:T(8,128)}, u32[]{:S(2)}, u32[]{:S(2)}) collective-permute-start(f32[6,8,32,1]{2,1,3,0:T(8,128)} %copy.195), channel_id=1, source_target_pairs={{0,32},{32,64},{64,96},{96,128},{128,160},{160,192},{192,224},{1,3... | collective-permute-start | bytes 18440 | tf_op jit(solution)/shard_map/ppermute | solution.py:36
  13.0 20.1 %all-to-all-start.1 = ((s32[1,32,16]{2,0,1:T(1,128)}), s32[1,32,16]{2,0,1:T(1,128)S(1)}, u32[]{:S(2)}, u32[]{:S(2)}) async-start(s32[1,32,16]{2,0,1:T(1,128)} %bitcast.50), calls=%async_computation.1 | async-start | bytes 32768 | tf_op jit(solution)/shard_map/all_to_all | solution.py:130
  36.2 4.3 %compare_select_fusion.4 = (s32[512,1]{0,1:T(1,128)S(1)}, s32[512,1]{0,1:T(1,128)S(1)}) fusion(s32[]{:T(128)} %bitcast.41, s32[]{:T(128)} %bitcast.42, s32[]{:T(128)} %bitcast.43, s32[]{:T(128)} %bitcast.44, s32[]{:T(128)} %bitcast.45, s32[]{:T(128)} %bitcast.47, s32[]{:T(128)} %bitcast.46, s32[512,1]{0,1:T(1,128)S(1)} %bitcast.216, s32[512,1]{0,1:T(1,128)S(1)} %bitcast.215), kind=kLoop, calls=%fused_computation.238 | loop fusion | flops 7168 | bytes 8220 | tf_op jit(solution)/shard_map/jit(_take)/gather | solution.py:154
  40.6 15.9 %select_select_fusion = s32[512]{0:T(512)S(1)} fusion(pred[512]{0:T(512)(128)(4,1)S(1)} %get-tuple-element.42, pred[512]{0:T(512)(128)(4,1)S(1)} %get-tuple-element.41, pred[512]{0:T(512)(128)(4,1)S(1)} %get-tuple-element.40, pred[512]{0:T(512)(128)(4,1)S(1)} %get-tuple-element.39, pred[512]{0:T(512)(128)(4,1)S(1)} %get-tuple-element.38, ...), kind=kLoop, calls=%fused_computation.248 | loop fusion | flops 12800 | bytes 16996 | tf_op jit(solution)/shard_map/jit(_take)/gather | solution.py:154
  61.8 1.1 copy.156
  62.9 1.1 copy.158
  64.2 1.3 collective-permute-start.2
  65.5 12.7 %collective-permute-start.3 = (f32[6,8,1,130]{3,1,2,0:T(8,128)S(1)}, f32[6,8,1,130]{3,1,2,0:T(8,128)S(1)}, u32[]{:S(2)}, u32[]{:S(2)}) collective-permute-start(f32[6,8,1,130]{3,1,2,0:T(8,128)S(1)} %get-tuple-element.58), channel_id=1, source_target_pairs={{0,1},{1,2},{2,3},{3,4},{4,5},{5,6},{6,7},{7,8},{8,9},{9,10},{10,1... | collective-permute-start | bytes 74888 | tf_op jit(solution)/shard_map/ppermute | solution.py:36
  78.2 1.1 collective-permute-done.3
  79.3 1.1 fusion.10
  84.6 1.4 fusion.106
  86.0 1.8 copy.171
  87.8 1.3 collective-permute-start.4
  89.1 1.1 copy.173
  90.2 4.6 %collective-permute-start.5 = (f32[9,8,32,1]{2,1,3,0:T(8,128)}, f32[9,8,32,1]{2,1,3,0:T(8,128)}, u32[]{:S(2)}, u32[]{:S(2)}) collective-permute-start(f32[9,8,32,1]{2,1,3,0:T(8,128)} %copy.173), channel_id=1, source_target_pairs={{0,32},{32,64},{64,96},{96,128},{128,160},{160,192},{192,224},{1,3... | collective-permute-start | bytes 27656 | tf_op jit(solution)/shard_map/ppermute | solution.py:36
  95.7 2.3 %copy.174 = f32[9,8,32,1]{3,1,2,0:T(8,128)} copy(f32[9,8,32,1]{2,1,3,0:T(8,128)} %collective-permute-done.5) | data formatting | bytes 18432 | tf_op jit(solution)/shard_map/ppermute | solution.py:36
  98.0 0.9 pad_maximum_fusion.27
  98.9 1.3 collective-permute-start.6
  100.3 13.9 %collective-permute-start.7 = (f32[9,8,1,130]{3,1,2,0:T(8,128)S(1)}, f32[9,8,1,130]{3,1,2,0:T(8,128)S(1)}, u32[]{:S(2)}, u32[]{:S(2)}) collective-permute-start(f32[9,8,1,130]{3,1,2,0:T(8,128)S(1)} %get-tuple-element.54), channel_id=1, source_target_pairs={{0,1},{1,2},{2,3},{3,4},{4,5},{5,6},{6,7},{7,8},{8,9},{9,10},{10,1... | collective-permute-start | bytes 112328 | tf_op jit(solution)/shard_map/ppermute | solution.py:36
  114.4 1.3 collective-permute-done.7
  115.7 1.6 fusion.3
  120.1 1.3 gather_fusion
  121.4 0.9 fusion.111
  123.2 30.7 %all-to-all-start = ((f32[32,1,768]{2,1,0:T(1,128)}), f32[32,1,768]{2,1,0:T(1,128)S(1)}, u32[]{:S(2)}, u32[]{:S(2)}) async-start(f32[32,1,768]{2,1,0:T(1,128)} %reshape.983), calls=%async_computation | async-start | bytes 196608 | tf_op jit(solution)/shard_map/all_to_all | solution.py:129
  154.6 9.0 %collective-permute-start.9 = (s32[1,512]{1,0:T(1,128)S(1)}, s32[1,512]{1,0:T(1,128)S(1)}, u32[]{:S(2)}, u32[]{:S(2)}) collective-permute-start(s32[1,512]{1,0:T(1,128)S(1)} %all_to_all.18), channel_id=1, source_target_pairs={{0,256},{256,0},{1,257},{257,1},{2,258},{258,2},{3,259},{259,3},{4... | collective-permute-start | bytes 6152 | tf_op jit(solution)/shard_map/ppermute | solution.py:28
  164.5 5.5 %all-to-all-done = f32[32,1,768]{2,1,0:T(1,128)S(1)} async-done(((f32[32,1,768]{2,1,0:T(1,128)}), f32[32,1,768]{2,1,0:T(1,128)S(1)}, u32[]{:S(2)}, u32[]{:S(2)}) %all-to-all-start) | async-done | bytes 98336 | tf_op jit(solution)/shard_map/all_to_all | solution.py:129
  171.5 10.2 %collective-permute-start.8 = (f32[48,512]{0,1:T(8,128)S(1)}, f32[48,512]{0,1:T(8,128)S(1)}, u32[]{:S(2)}, u32[]{:S(2)}) collective-permute-start(f32[48,512]{0,1:T(8,128)S(1)} %bitcast.213), channel_id=1, source_target_pairs={{0,256},{256,0},{1,257},{257,1},{2,258},{258,2},{3,259},{259,3},{4... | collective-permute-start | bytes 294920 | tf_op jit(solution)/shard_map/ppermute | solution.py:28
  182.9 1.1 convolution_bitcast_fusion
  (102 shorter events, 23.5 us)
Async XLA Ops:
  2.3 9.4 %copy-start.11 = (s32[1,1,1,512]{3,2,1,0:T(1,128)S(1)}, s32[1,1,1,512]{3,2,1,0:T(1,128)}, u32[]{:S(2)}) copy-start(s32[1,1,1,512]{3,2,1,0:T(1,128)} %param.13) | copy-start | bytes 6148
  2.3 30.8 %copy-start.1 = (f32[1,3,8,32,128]{4,3,2,1,0:T(8,128)S(1)}, f32[1,3,8,32,128]{4,3,2,1,0:T(8,128)}, u32[]{:S(2)}) copy-start(f32[1,3,8,32,128]{4,3,2,1,0:T(8,128)} %param.8) | copy-start | bytes 1179652
  2.3 30.8 %copy-start.2 = (f32[1,3,8,32,128]{4,3,2,1,0:T(8,128)S(1)}, f32[1,3,8,32,128]{4,3,2,1,0:T(8,128)}, u32[]{:S(2)}) copy-start(f32[1,3,8,32,128]{4,3,2,1,0:T(8,128)} %param.9) | copy-start | bytes 1179652
  3.3 58.5 %collective-permute-start = (f32[6,8,32,1]{2,1,3,0:T(8,128)}, f32[6,8,32,1]{2,1,3,0:T(8,128)}, u32[]{:S(2)}, u32[]{:S(2)}) collective-permute-start(f32[6,8,32,1]{2,1,3,0:T(8,128)} %copy.194), channel_id=1, source_target_pairs={{32,0},{64,32},{96,64},{128,96},{160,128},{192,160},{224,192},{33,... | collective-permute-start | bytes 18440 | tf_op jit(solution)/shard_map/ppermute | solution.py:39
  5.5 57.4 %collective-permute-start.1 = (f32[6,8,32,1]{2,1,3,0:T(8,128)}, f32[6,8,32,1]{2,1,3,0:T(8,128)}, u32[]{:S(2)}, u32[]{:S(2)}) collective-permute-start(f32[6,8,32,1]{2,1,3,0:T(8,128)} %copy.195), channel_id=1, source_target_pairs={{0,32},{32,64},{64,96},{96,128},{128,160},{160,192},{192,224},{1,3... | collective-permute-start | bytes 18440 | tf_op jit(solution)/shard_map/ppermute | solution.py:36
  13.0 110.2 %all-to-all-start.1 = ((s32[1,32,16]{2,0,1:T(1,128)}), s32[1,32,16]{2,0,1:T(1,128)S(1)}, u32[]{:S(2)}, u32[]{:S(2)}) async-start(s32[1,32,16]{2,0,1:T(1,128)} %bitcast.50), calls=%async_computation.1 | async-start | bytes 32768 | tf_op jit(solution)/shard_map/all_to_all | solution.py:130
  33.3 0.7 copy-start.4
  33.3 2.1 %copy-start.10 = (s32[1,1,1,512]{3,2,1,0:T(1,128)S(1)}, s32[1,1,1,512]{3,2,1,0:T(1,128)}, u32[]{:S(2)}) copy-start(s32[1,1,1,512]{3,2,1,0:T(1,128)} %param.11) | copy-start | bytes 6148
  33.3 2.8 %copy-start.13 = (s32[4,128]{1,0:T(4,128)S(1)}, s32[4,128]{1,0:T(4,128)}, u32[]{:S(2)}) copy-start(s32[4,128]{1,0:T(4,128)} %constant.165.clone.1) | copy-start | bytes 6148
  33.4 23.8 %copy-start.12 = (f32[1,1,1,512]{3,2,1,0:T(1,128)S(1)}, f32[1,1,1,512]{3,2,1,0:T(1,128)}, u32[]{:S(2)}) copy-start(f32[1,1,1,512]{3,2,1,0:T(1,128)} %param.12) | copy-start | bytes 6148
  33.9 26.1 %copy-start.9 = (s32[32,16]{1,0:T(8,128)S(1)}, s32[32,16]{1,0:T(8,128)}, u32[]{:S(2)}) copy-start(s32[32,16]{1,0:T(8,128)} %constant.162.clone.1) | copy-start | bytes 6148
  64.1 15.3 %copy-start.7 = (f32[8,128]{1,0:T(8,128)S(1)}, f32[8,128]{1,0:T(8,128)}, u32[]{:S(2)}) copy-start(f32[8,128]{1,0:T(8,128)} %multiply_divide_fusion) | copy-start | bytes 12292
  64.2 14.0 %collective-permute-start.2 = (f32[6,8,1,130]{3,1,2,0:T(8,128)S(1)}, f32[6,8,1,130]{3,1,2,0:T(8,128)S(1)}, u32[]{:S(2)}, u32[]{:S(2)}) collective-permute-start(f32[6,8,1,130]{3,1,2,0:T(8,128)S(1)} %get-tuple-element.57), channel_id=1, source_target_pairs={{1,0},{2,1},{3,2},{4,3},{5,4},{6,5},{7,6},{8,7},{9,8},{10,9},{11,1... | collective-permute-start | bytes 74888 | tf_op jit(solution)/shard_map/ppermute | solution.py:39
  65.5 13.9 %collective-permute-start.3 = (f32[6,8,1,130]{3,1,2,0:T(8,128)S(1)}, f32[6,8,1,130]{3,1,2,0:T(8,128)S(1)}, u32[]{:S(2)}, u32[]{:S(2)}) collective-permute-start(f32[6,8,1,130]{3,1,2,0:T(8,128)S(1)} %get-tuple-element.58), channel_id=1, source_target_pairs={{0,1},{1,2},{2,3},{3,4},{4,5},{5,6},{6,7},{7,8},{8,9},{9,10},{10,1... | collective-permute-start | bytes 74888 | tf_op jit(solution)/shard_map/ppermute | solution.py:36
  78.2 2.2 %copy-start.14 = (f32[8]{0:T(128)}, f32[8]{0:T(128)S(1)}, u32[]{:S(2)}) copy-start(f32[8]{0:T(128)S(1)} %multiply_divide_fusion.1) | copy-start | bytes 100
  83.0 0.9 copy-start.6
  83.3 0.9 copy-start.5
  87.8 7.4 %collective-permute-start.4 = (f32[9,8,32,1]{2,1,3,0:T(8,128)S(1)}, f32[9,8,32,1]{2,1,3,0:T(8,128)S(1)}, u32[]{:S(2)}, u32[]{:S(2)}) collective-permute-start(f32[9,8,32,1]{2,1,3,0:T(8,128)S(1)} %copy.171), channel_id=1, source_target_pairs={{32,0},{64,32},{96,64},{128,96},{160,128},{192,160},{224,192},{33,... | collective-permute-start | bytes 27656 | tf_op jit(solution)/shard_map/ppermute | solution.py:39
  90.2 5.5 %collective-permute-start.5 = (f32[9,8,32,1]{2,1,3,0:T(8,128)}, f32[9,8,32,1]{2,1,3,0:T(8,128)}, u32[]{:S(2)}, u32[]{:S(2)}) collective-permute-start(f32[9,8,32,1]{2,1,3,0:T(8,128)} %copy.173), channel_id=1, source_target_pairs={{0,32},{32,64},{64,96},{96,128},{128,160},{160,192},{192,224},{1,3... | collective-permute-start | bytes 27656 | tf_op jit(solution)/shard_map/ppermute | solution.py:36
  98.9 15.4 %collective-permute-start.6 = (f32[9,8,1,130]{3,1,2,0:T(8,128)S(1)}, f32[9,8,1,130]{3,1,2,0:T(8,128)S(1)}, u32[]{:S(2)}, u32[]{:S(2)}) collective-permute-start(f32[9,8,1,130]{3,1,2,0:T(8,128)S(1)} %get-tuple-element.53), channel_id=1, source_target_pairs={{1,0},{2,1},{3,2},{4,3},{5,4},{6,5},{7,6},{8,7},{9,8},{10,9},{11,1... | collective-permute-start | bytes 112328 | tf_op jit(solution)/shard_map/ppermute | solution.py:39
  100.2 15.5 %copy-start = (f32[9,8,32,1]{3,1,2,0:T(8,128)S(1)}, f32[9,8,32,1]{3,1,2,0:T(8,128)}, u32[]{:S(2)}) copy-start(f32[9,8,32,1]{3,1,2,0:T(8,128)} %copy.174) | copy-start | bytes 27652
  100.2 15.5 %copy-start.8 = (f32[8,128]{1,0:T(8,128)S(1)}, f32[8,128]{1,0:T(8,128)}, u32[]{:S(2)}) copy-start(f32[8,128]{1,0:T(8,128)} %multiply_divide_fusion) | copy-start | bytes 12292
  100.2 15.5 %copy-start.15 = (f32[8]{0:T(128)S(1)}, f32[8]{0:T(128)}, u32[]{:S(2)}) copy-start(f32[8]{0:T(128)} %copy-done.14) | copy-start | bytes 100
  100.3 15.4 %collective-permute-start.7 = (f32[9,8,1,130]{3,1,2,0:T(8,128)S(1)}, f32[9,8,1,130]{3,1,2,0:T(8,128)S(1)}, u32[]{:S(2)}, u32[]{:S(2)}) collective-permute-start(f32[9,8,1,130]{3,1,2,0:T(8,128)S(1)} %get-tuple-element.54), channel_id=1, source_target_pairs={{0,1},{1,2},{2,3},{3,4},{4,5},{5,6},{6,7},{7,8},{8,9},{9,10},{10,1... | collective-permute-start | bytes 112328 | tf_op jit(solution)/shard_map/ppermute | solution.py:36
  120.1 43.6 %copy-start.3 = (f32[1,8,32,128]{3,2,1,0:T(8,128)S(1)}, f32[1,8,32,128]{3,2,1,0:T(8,128)}, u32[]{:S(2)}) copy-start(f32[1,8,32,128]{3,2,1,0:T(8,128)} %get-tuple-element.82) | copy-start | bytes 393220
  123.2 46.8 %all-to-all-start = ((f32[32,1,768]{2,1,0:T(1,128)}), f32[32,1,768]{2,1,0:T(1,128)S(1)}, u32[]{:S(2)}, u32[]{:S(2)}) async-start(f32[32,1,768]{2,1,0:T(1,128)} %reshape.983), calls=%async_computation | async-start | bytes 196608 | tf_op jit(solution)/shard_map/all_to_all | solution.py:129
  154.6 27.9 %collective-permute-start.9 = (s32[1,512]{1,0:T(1,128)S(1)}, s32[1,512]{1,0:T(1,128)S(1)}, u32[]{:S(2)}, u32[]{:S(2)}) collective-permute-start(s32[1,512]{1,0:T(1,128)S(1)} %all_to_all.18), channel_id=1, source_target_pairs={{0,256},{256,0},{1,257},{257,1},{2,258},{258,2},{3,259},{259,3},{4... | collective-permute-start | bytes 6152 | tf_op jit(solution)/shard_map/ppermute | solution.py:28
  171.5 11.4 %collective-permute-start.8 = (f32[48,512]{0,1:T(8,128)S(1)}, f32[48,512]{0,1:T(8,128)S(1)}, u32[]{:S(2)}, u32[]{:S(2)}) collective-permute-start(f32[48,512]{0,1:T(8,128)S(1)} %bitcast.213), channel_id=1, source_target_pairs={{0,256},{256,0},{1,257},{257,1},{2,258},{258,2},{3,259},{259,3},{4... | collective-permute-start | bytes 294920 | tf_op jit(solution)/shard_map/ppermute | solution.py:28
where the time goes:
time: 185 us; the launch traced here: 184 us
  starting transfers between devices  112 us (61%)
  other arithmetic  40.5 us (22%)
  local copies, waits for them, and re-layouts  20.9 us (11%)
  waiting for transfers between devices  8.35 us (5%)
    ppermute x4, starting transfers between devices, with_halo(): lax.ppermute(lax.slice_in_dim(block, block.shape[dim] - width, None, axis...  36.8 us
    all_to_all x1, starting transfers between devices, route_lon(): lax.all_to_all(payload[0], 'lon', split_axis=1, concat_axis=1, tiled=True)  30.7 us
    gather x3, other arithmetic, local(): jnp.repeat(pair_rows[0, 0, 0], CAP, total_repeat_length=slots_total)  20.3 us
    all_to_all x1, starting transfers between devices, route_lon(): lax.all_to_all(payload[1], 'lon', split_axis=1, concat_axis=1, tiled=True)  20.1 us
    ppermute x2, starting transfers between devices, from_partner(): return lax.ppermute(block, axis, route)  19.3 us
    unnamed x12, other arithmetic  6.41 us
    all_to_all x1, waiting for transfers between devices, route_lon(): lax.all_to_all(payload[0], 'lon', split_axis=1, concat_axis=1, tiled=True)  5.51 us
    unnamed x44, local copies, waits for them, and re-layouts  5.37 us
  transfers between devices with their start and end apart: 12, of which 4 were waited for; matrix products, arithmetic and copies ran while one was open for 31% of the time, Pallas kernels for 0%

commit v1 on v0

v1 whole, which is shorter than its diff:
```python
import math

import jax
import jax.numpy as jnp
from jax import lax
from jax.experimental import pallas as pl
from jax.experimental.pallas import tpu as pltpu
from jax.sharding import PartitionSpec as P

CAP = 16
CYCLE = 128
LEVELS = 8
CELLS_P = 32
CELLS_T = 128

inner_radius = 0.6
smag_const = 0.2
aniso_weight = 0.8
turb_prandtl = 0.7
courant = 0.2

ALONG_R = (0, 1, 2, 7, 8)
ALONG_T = (1, 3, 4, 6, 8)
ALONG_P = (2, 4, 5, 6, 7)
F32 = jnp.float32


def lanes_of(shape):
    return lax.broadcasted_iota(jnp.int32, shape, len(shape) - 1)


def rows_of(shape):
    return lax.broadcasted_iota(jnp.int32, shape, len(shape) - 2)


def pick(vel_ref, mag_ref, comp):
    return (vel_ref, comp) if comp < 3 else (mag_ref, comp - 3)


def edges_kernel(vel_ref, mag_ref, low_ref, high_ref, first_ref, last_ref):
    pair = lanes_of((CELLS_P, CELLS_T)) // 2
    low = jnp.zeros((CELLS_P, CELLS_T), F32)
    high = jnp.zeros((CELLS_P, CELLS_T), F32)
    for comp in range(6):
        ref, index = pick(vel_ref, mag_ref, comp)
        for level in range(LEVELS):
            place = 16 * comp + 2 * level
            block = ref[0, index, level]
            if place:
                block = pltpu.roll(block, place, 1)
            low = jnp.where(pair == place // 2, block, low)
            high = jnp.where(pair == (place // 2 - 1) % (CELLS_T // 2), block, high)
        first_ref[comp] = ref[0, index, :, 0, :]
        last_ref[comp] = ref[0, index, :, CELLS_P - 1, :]
        if comp < 5:
            first_ref[6 + comp] = ref[0, index, :, 1, :]
            last_ref[6 + comp] = ref[0, index, :, CELLS_P - 2, :]
    low_ref[...] = low
    high_ref[...] = pltpu.roll(high, 2, 1)
    first_ref[11] = jnp.zeros((LEVELS, CELLS_T), F32)
    last_ref[11] = jnp.zeros((LEVELS, CELLS_T), F32)


def strips_kernel(place_ref, below_ref, above_ref, first_ref, last_ref, far_ref, near_ref):
    odd = place_ref[1] % 2

    def corner(row):
        shape = (LEVELS, CELLS_T)
        below = jnp.broadcast_to(below_ref[row : row + 1, :], shape)
        above = jnp.broadcast_to(above_ref[row : row + 1, :], shape)
        return jnp.where(rows_of(shape) == 0, below, above)

    @pl.when(odd == 0)
    def _():
        far_ref[...] = first_ref[...]
        far_ref[11] = corner(0)
        near_ref[0:12] = last_ref[...]
        near_ref[11] = corner(CELLS_P - 1)

    @pl.when(odd == 1)
    def _():
        far_ref[...] = last_ref[...]
        far_ref[11] = corner(CELLS_P - 1)
        near_ref[0:12] = first_ref[...]
        near_ref[11] = corner(0)

    near_ref[12:24] = jnp.zeros((12, LEVELS, CELLS_T), F32)


def flux_of(center, grad_r, grad_t, grad_p, spacing, wanted):
    u0, u1, u2, b0, b1, b2 = center
    s00, s11, s22 = grad_r[0], grad_t[1], grad_p[2]
    d01 = grad_t[0] + grad_r[1]
    d02 = grad_p[0] + grad_r[2]
    d12 = grad_p[1] + grad_t[2]
    squares = 2.0 * (s00 * s00 + s11 * s11 + s22 * s22) + (d01 * d01 + d02 * d02 + d12 * d12)
    viscous = jnp.sqrt(squares) * ((smag_const * spacing) ** 2)
    q00, q11, q22 = b0 * b0, b1 * b1, b2 * b2
    field_sq = q00 + q11 + q22
    inverse = 1.0 / (field_sq + 1.0)
    q01, q02, q12 = b0 * b1, b0 * b2, b1 * b2
    aligned = q00 * s00 + q11 * s11 + q22 * s22 + (q01 * d01 + q02 * d02 + q12 * d12)
    weight = (2.0 * aniso_weight) * viscous * aligned * inverse * inverse - 1.0
    half = 0.5 * field_sq
    twice = viscous + viscous
    ratio = viscous * (1.0 / turb_prandtl)
    result = {}
    for chan in wanted:
        if chan == 0:
            result[0] = u0 * u0 + q00 * weight - twice * s00 + half
        elif chan == 1:
            result[1] = u0 * u1 + q01 * weight - viscous * d01
        elif chan == 2:
            result[2] = u0 * u2 + q02 * weight - viscous * d02
        elif chan == 3:
            result[3] = u1 * u1 + q11 * weight - twice * s11 + half
        elif chan == 4:
            result[4] = u1 * u2 + q12 * weight - viscous * d12
        elif chan == 5:
            result[5] = u2 * u2 + q22 * weight - twice * s22 + half
        elif chan == 6:
            result[6] = u1 * b2 - u2 * b1 - ratio * (grad_t[5] - grad_p[4])
        elif chan == 7:
            result[7] = u2 * b0 - u0 * b2 - ratio * (grad_p[3] - grad_r[5])
        else:
            result[8] = u0 * b1 - u1 * b0 - ratio * (grad_r[4] - grad_t[3])
    return result


def section_kernel(
    spacing,
    theta_step,
    phi_step,
    lat_blocks,
    lon_blocks,
    place_ref,
    vel_ref,
    mag_ref,
    low_ref,
    high_ref,
    below_ref,
    above_ref,
    first_ref,
    last_ref,
    side_ref,
    rows_ref,
    cell_ref,
    weight_ref,
    slot_ref,
    new_vel_ref,
    new_mag_ref,
    send_ref,
    flux_ref,
    edge_t_ref,
    edge_p_ref,
    taken_ref,
):
    lat = place_ref[0]
    lon = place_ref[1]
    odd_block = lon % 2
    time_step = courant * spacing
    wide = (CELLS_P, CELLS_T)
    flat = (LEVELS, CELLS_T)
    lane = lanes_of(wide)
    row = rows_of(wide)
    lane_flat = lanes_of(flat)
    row_flat = rows_of(flat)
    first_lane, last_lane = lane == 0, lane == CELLS_T - 1
    first_row, last_row = row == 0, row == CELLS_P - 1

    def radius(level):
        return inner_radius + (level.astype(F32) + 0.5) * spacing

    def inverse_sine(index):
        return 1.0 / jnp.sin(0.25 * math.pi + (index.astype(F32) + 0.5) * theta_step)

    first_t = lat * CELLS_T
    own_sine = inverse_sine(first_t + lanes_of((8, CELLS_T)))

    base = (12 * (1 - odd_block), 12 * odd_block)

    is_below = lane % 2 == 1
    level_of = (lane % 16) // 2
    below, above = below_ref[...], above_ref[...]
    beside = jnp.where(is_below, below, above)

    def swapped(block):
        return jnp.where(is_below, pltpu.roll(block, 1, 1), pltpu.roll(block, CELLS_T - 1, 1))

    def corner(side):
        tile = side_ref[base[side] + 11]
        return jnp.where(lane_flat[0:1] % 2 == 1, tile[0:1], tile[1:2])

    corners = (corner(0), corner(1))
    inverse_r = 1.0 / radius(level_of)
    own_step = jnp.where((level_of == 0) | (level_of == LEVELS - 1), 1.0 / spacing, 0.5 / spacing)
    up = jnp.where(level_of == LEVELS - 1, beside, pltpu.roll(beside, CELLS_T - 2, 1))
    down = jnp.where(level_of == 0, beside, pltpu.roll(beside, 2, 1))
    pack_r = (up - down) * own_step
    inner = jnp.where(is_below, high_ref[...], low_ref[...])
    outer = jnp.where(is_below, above, below)
    pack_t = swapped(inner - outer) * (
        jnp.where(is_below, 0.5 / theta_step, -0.5 / theta_step) * inverse_r
    )
    t_index = first_t + jnp.where(is_below, -1, CELLS_T)
    up = jnp.where(last_row, corners[1], pltpu.roll(beside, CELLS_P - 1, 0))
    down = jnp.where(first_row, corners[0], pltpu.roll(beside, 1, 0))
    pack_p = (up - down) * (inverse_sine(t_index) * inverse_r * (0.5 / phi_step))

    def spread(block):
        return [block if comp == 0 else pltpu.roll(block, CELLS_T - 16 * comp, 1) for comp in range(6)]

    edge = flux_of(
        spread(beside), spread(pack_r), spread(pack_t), spread(pack_p), spacing, ALONG_T
    )
    outside = (is_below & (lat == 0)) | ((lane % 2 == 0) & (lat == lat_blocks - 1))
    for slot, chan in enumerate(ALONG_T):
        edge_t_ref[slot] = jnp.where(outside, 0.0, edge[chan])

    level_step = jnp.where(
        (row_flat == 0) | (row_flat == LEVELS - 1), 1.0 / spacing, 0.5 / spacing
    )
    inverse_flat = 1.0 / radius(row_flat)
    for side in range(2):
        inner_ref = first_ref if side == 0 else last_ref
        sign = 1.0 if side == 0 else -1.0
        center = [side_ref[base[side] + comp] for comp in range(6)]
        corner_row = jnp.broadcast_to(corners[side], flat)
        grad_r, grad_t, grad_p = [], [], []
        for comp in range(6):
            block = center[comp]
            up = jnp.where(row_flat == LEVELS - 1, block, pltpu.roll(block, LEVELS - 1, 0))
            down = jnp.where(row_flat == 0, block, pltpu.roll(block, 1, 0))
            grad_r.append((up - down) * level_step)
            spot = 16 * comp + 2 * row_flat
            before = jnp.sum(
                jnp.where(lane_flat == spot + 1, corner_row, 0.0), axis=1, keepdims=True
            )
            after = jnp.sum(jnp.where(lane_flat == spot, corner_row, 0.0), axis=1, keepdims=True)
            up = jnp.where(lane_flat == CELLS_T - 1, after, pltpu.roll(block, CELLS_T - 1, 1))
            down = jnp.where(lane_flat == 0, before, pltpu.roll(block, 1, 1))
            grad_t.append((up - down) * (inverse_flat * (0.5 / theta_step)))
            if comp < 5:
                gap = inner_ref[comp] - side_ref[base[side] + 6 + comp]
                grad_p.append(gap * (own_sine * inverse_flat * (sign * 0.5 / phi_step)))
            else:
                grad_p.append(None)
        edge = flux_of(center, grad_r, grad_t, grad_p, spacing, ALONG_P)
        outside = lon == (0 if side == 0 else lon_blocks - 1)
        for slot, chan in enumerate(ALONG_P):
            edge_p_ref[side, slot] = jnp.where(outside, 0.0, edge[chan])

    def shifts(level, scale):
        low_level = jnp.maximum(level - 1, 0)
        high_level = jnp.minimum(level + 1, LEVELS - 1)
        ends = (level == 0) | (level == LEVELS - 1)
        step_r = jnp.where(ends, scale / spacing, 0.5 * scale / spacing)
        inverse = 1.0 / radius(jnp.full((8, CELLS_T), level, jnp.int32))
        step_t = (inverse * (0.5 * scale / theta_step))[0:1]
        step_p = (own_sine * inverse * (0.5 * scale / phi_step))[0:1]
        return low_level, high_level, step_r, step_t, step_p

    def along_t(block, ends, step):
        up = jnp.where(last_lane, ends, pltpu.roll(block, CELLS_T - 1, 1))
        down = jnp.where(first_lane, ends, pltpu.roll(block, 1, 1))
        return (up - down) * step

    def along_p(block, before, after, step):
        up = jnp.where(last_row, after, pltpu.roll(block, CELLS_P - 1, 0))
        down = jnp.where(first_row, before, pltpu.roll(block, 1, 0))
        return (up - down) * step

    def make_flux(level, carry):
        low_level, high_level, step_r, step_t, step_p = shifts(level, 1.0)
        center, grad_r, grad_t, grad_p = [], [], [], []
        for comp in range(6):
            ref, index = pick(vel_ref, mag_ref, comp)
            block = ref[0, index, level]
            center.append(block)
            grad_r.append((ref[0, index, high_level] - ref[0, index, low_level]) * step_r)
            ends = pltpu.roll(beside, 2 * CELLS_T - 1 - 16 * comp - 2 * level, 1)
            grad_t.append(along_t(block, ends, step_t))
            before = side_ref[base[0] + comp, pl.ds(level, 1), :]
            after = side_ref[base[1] + comp, pl.ds(level, 1), :]
            grad_p.append(along_p(block, before, after, step_p))
        flux = flux_of(center, grad_r, grad_t, grad_p, spacing, range(9))
        for chan in range(9):
            flux_ref[chan, level] = flux[chan]
        return carry

    lax.fori_loop(0, LEVELS, make_flux, 0)

    def advance(level, carry):
        low_level, high_level, step_r, step_t, step_p = shifts(level, time_step)

        def d_r(chan):
            return (flux_ref[chan, high_level] - flux_ref[chan, low_level]) * step_r

        def d_t(chan):
            slot = ALONG_T.index(chan)
            ends = pltpu.roll(edge_t_ref[slot], CELLS_T - 1 - 2 * level, 1)
            return along_t(flux_ref[chan, level], ends, step_t)

        def d_p(chan):
            slot = ALONG_P.index(chan)
            before = edge_p_ref[0, slot, pl.ds(level, 1), :]
            after = edge_p_ref[1, slot, pl.ds(level, 1), :]
            return along_p(flux_ref[chan, level], before, after, step_p)

        new_vel_ref[0, 0, level] = vel_ref[0, 0, level] - (d_r(0) + d_t(1) + d_p(2))
        new_vel_ref[0, 1, level] = vel_ref[0, 1, level] - (d_r(1) + d_t(3) + d_p(4))
        new_vel_ref[0, 2, level] = vel_ref[0, 2, level] - (d_r(2) + d_t(4) + d_p(5))
        new_mag_ref[0, 0, level] = mag_ref[0, 0, level] + (d_t(8) - d_p(7))
        new_mag_ref[0, 1, level] = mag_ref[0, 1, level] + (d_p(6) - d_r(8))
        new_mag_ref[0, 2, level] = mag_ref[0, 2, level] + (d_r(7) - d_t(6))
        return carry

    lax.fori_loop(0, LEVELS, advance, 0)

    slots_total = cell_ref.shape[-1]
    chunks = slots_total // CELLS_T
    rows_wide = jnp.broadcast_to(rows_ref[0, 0].astype(F32), (8, lon_blocks))
    owner = lanes_of((lon_blocks, slots_total)) // CAP == rows_of((lon_blocks, slots_total))
    counts = jnp.dot(rows_wide, owner.astype(F32), preferred_element_type=F32)
    bucket = lanes_of((8, slots_total)) % CAP
    live = bucket < (counts + 0.5).astype(jnp.int32)
    scale = jnp.where(live, jnp.broadcast_to(weight_ref[0, 0], (8, slots_total)), 0.0)
    cells = jnp.broadcast_to(cell_ref[0, 0], (8, slots_total))
    cell_t = cells % CELLS_T
    cell_p = cells // CELLS_T
    scale = jnp.where(cell_p % 8 == rows_of(cells.shape), scale, 0.0)
    group = cell_p // 8
    taken_ref[6:8] = jnp.zeros((2, LEVELS, slots_total), F32)
    taken_ref[6, 0:1] = slot_ref[0, 0].astype(F32)
    for start, ref in ((0, new_vel_ref), (3, new_mag_ref)):

        def take(comp, carry, start=start, ref=ref):
            for level in range(LEVELS):
                block = ref[0, comp, level]
                for chunk in range(chunks):
                    part = slice(chunk * CELLS_T, (chunk + 1) * CELLS_T)
                    where_t = cell_t[:, part]
                    total = jnp.zeros((8, CELLS_T), F32)
                    for step in range(CELLS_P // 8):
                        got = jnp.take_along_axis(
                            block[8 * step : 8 * step + 8],
                            where_t,
                            axis=1,
                            mode="promise_in_bounds",
                        )
                        total = jnp.where(group[:, part] == step, got, total)
                    total = jnp.sum(total * scale[:, part], axis=0, keepdims=True)
                    taken_ref[start + comp, level : level + 1, part] = total
            return carry

        lax.fori_loop(0, 3, take, 0)

    for chunk in range(chunks):
        part = taken_ref[:, :, chunk * CELLS_T : (chunk + 1) * CELLS_T].reshape(64, CELLS_T)
        both = jnp.concatenate([part, pltpu.roll(part, CELLS_T - 8, 1)], axis=0)
        turned = jnp.transpose(both)
        for block in range(8):
            send_ref[chunk * 8 + block] = turned[16 * block : 16 * block + 8]


def collect_kernel(got_ref, out_ref):
    rows = got_ref.shape[0] * got_ref.shape[1]
    got = got_ref[...].reshape(rows, CELLS_T)
    total = jnp.zeros((48, CYCLE), F32)
    for start in (0, 64):
        slot = got[:, start + 48 : start + 49].astype(jnp.int32)
        onehot = (slot == lanes_of((rows, CYCLE))).astype(F32)
        part = lax.dot_general(
            got,
            onehot,
            (((0,), (0,)), ((), ())),
            precision=lax.Precision.HIGHEST,
            preferred_element_type=F32,
        )
        total = total + part[start : start + 48]
    out_ref[0, 0, 0] = total


VMEM = pl.BlockSpec(memory_space=pltpu.VMEM)
SMEM = pl.BlockSpec(memory_space=pltpu.SMEM)
LIMIT = pltpu.CompilerParams(vmem_limit_bytes=32 * 1024 * 1024)


def tiles(*shape):
    return jax.ShapeDtypeStruct(shape, F32)


def edges(velocity, magnetic):
    pack = tiles(CELLS_P, CELLS_T)
    strip = tiles(12, LEVELS, CELLS_T)
    return pl.pallas_call(
        edges_kernel,
        in_specs=[VMEM] * 2,
        out_specs=[VMEM] * 4,
        out_shape=[pack, pack, strip, strip],
        compiler_params=LIMIT,
        name="edges",
    )(velocity, magnetic)


def local(velocity, magnetic, pair_rows, send_cell, send_weight, cycle_slot):
    lat_blocks, lon_blocks = lax.axis_size("lat"), lax.axis_size("lon")
    theta_step = 0.5 * math.pi / (lat_blocks * CELLS_T)
    phi_step = 1.5 * math.pi / (lon_blocks * CELLS_P)
    spacing = inner_radius * theta_step
    place = jnp.stack([lax.axis_index("lat"), lax.axis_index("lon")]).astype(jnp.int32)
    low, high, first, last = edges(velocity, magnetic)
    below = lax.ppermute(high, "lat", [(i, i + 1) for i in range(lat_blocks - 1)])
    above = lax.ppermute(low, "lat", [(i + 1, i) for i in range(lat_blocks - 1)])
    far, near = pl.pallas_call(
        strips_kernel,
        in_specs=[SMEM] + [VMEM] * 4,
        out_specs=[VMEM] * 2,
        out_shape=[tiles(12, LEVELS, CELLS_T), tiles(24, LEVELS, CELLS_T)],
        name="strips",
    )(place, below, above, first, last)
    hop = [(i, i - 2 if i % 2 == 0 else i + 2) for i in range(lon_blocks)]
    hop = [(i, j) for i, j in hop if 0 <= j < lon_blocks]
    relayed = lax.ppermute(far, "lon", hop)
    sides = lax.dynamic_update_slice(near, relayed, (12, 0, 0))
    sides = lax.ppermute(sides, "lon", [(i, i ^ 1) for i in range(lon_blocks)])
    slots_total = send_cell.shape[-1]

    def section(*refs):
        section_kernel(spacing, theta_step, phi_step, lat_blocks, lon_blocks, *refs)

    new_velocity, new_magnetic, payload = pl.pallas_call(
        section,
        in_specs=[SMEM] + [VMEM] * 13,
        out_specs=[VMEM] * 3,
        out_shape=[
            tiles(*velocity.shape),
            tiles(*magnetic.shape),
            tiles(lon_blocks, 8, CELLS_T),
        ],
        scratch_shapes=[
            pltpu.VMEM((9, LEVELS, CELLS_P, CELLS_T), F32),
            pltpu.VMEM((5, CELLS_P, CELLS_T), F32),
            pltpu.VMEM((2, 5, LEVELS, CELLS_T), F32),
            pltpu.VMEM((8, LEVELS, slots_total), F32),
        ],
        compiler_params=LIMIT,
        name="section",
    )(
        place,
        velocity,
        magnetic,
        low,
        high,
        below,
        above,
        first,
        last,
        sides,
        pair_rows,
        send_cell,
        send_weight,
        cycle_slot,
    )
    payload = lax.all_to_all(payload, "lon", split_axis=0, concat_axis=0, tiled=True)
    payload = lax.ppermute(payload, "grid", [(0, 1), (1, 0)])
    cycle = pl.pallas_call(
        collect_kernel,
        in_specs=[VMEM],
        out_specs=VMEM,
        out_shape=tiles(1, 1, 1, 48, CYCLE),
        name="collect",
    )(payload)
    return (new_velocity, new_magnetic, cycle)


def solution(mesh):
    state = P("grid", None, None, "lon", "lat")
    rows = P("grid", "lat", "lon", None)
    return jax.shard_map(
        local,
        mesh=mesh,
        in_specs=(state, state, rows, rows, rows, rows),
        out_specs=(state, state, P("grid", "lat", "lon", None, None)),
        check_vma=False,
    )
```

time: 185 us -> 92.7 us (0.50)
  starting transfers between devices: 112 us -> 31.6 us
  other arithmetic: 40.5 us -> 0.58 us
  blocking collectives: 0 us -> 35.5 us
  local copies, waits for them, and re-layouts: 20.9 us -> 6.55 us
  Pallas kernels: 0 us -> 9.79 us
    all_to_all x2 -> x0, starting transfers between devices: 50.8 us -> none  [the longest x1 30.7 us: route_lon(): lax.all_to_all(payload[0], 'lon', split_axis=1, concat_axis=1, tiled=True)]
    all_to_all x0 -> x1, blocking collectives: none -> 35.5 us  [local(): lax.all_to_all(payload, 'lon', split_axis=0, concat_axis=0, tiled=True)]
    ppermute x10 -> x5, starting transfers between devices: 61.2 us -> 31.6 us  [the longest x1 14.9 us: local(): sides = lax.ppermute(sides, 'lon', [(i, i ^ 1) for i in range(lon_blocks)])]
    gather x4 -> x0, other arithmetic: 20.9 us -> none  [the longest x3 20.3 us: local(): jnp.repeat(pair_rows[0, 0, 0], CAP, total_repeat_length=slots_total)]
    pallas_call x0 -> x4, Pallas kernels: none -> 9.79 us  [the longest x1 5.89 us: local(): pl.pallas_call(section, in_specs=[SMEM] + [VMEM] * 13, out_specs=[VMEM] *...]
    unnamed x12 -> x0, other arithmetic: 6.41 us -> none
    all_to_all x2 -> x0, waiting for transfers between devices: 5.51 us -> none  [the longest x1 5.51 us: route_lon(): lax.all_to_all(payload[0], 'lon', split_axis=1, concat_axis=1, tiled=True)]
    ppermute x4 -> x0, local copies, waits for them, and re-layouts: 5.01 us -> none  [the longest x2 3.38 us: with_halo(): lax.ppermute(lax.slice_in_dim(block, block.shape[dim] - width, None, axis...]
  transfers between devices with their start and end apart: 12 -> 5, of which waited for: 4 -> 4; matrix products, arithmetic and copies ran while one was open for 31% -> 1% of each run, Pallas kernels for 0% -> 0%
where the time goes in v1:
time: 92.7 us; the launch traced here: 92.2 us
  blocking collectives  35.5 us (38%)
  starting transfers between devices  31.6 us (34%)
  Pallas kernels  9.79 us (11%)
  waiting for transfers between devices  7.46 us (8%)
  local copies, waits for them, and re-layouts  6.55 us (7%)
    all_to_all x1, blocking collectives, local(): lax.all_to_all(payload, 'lon', split_axis=0, concat_axis=0, tiled=True)  35.5 us
    ppermute x1, starting transfers between devices, local(): sides = lax.ppermute(sides, 'lon', [(i, i ^ 1) for i in range(lon_blocks)])  14.9 us
    ppermute x1, starting transfers between devices, local(): payload = lax.ppermute(payload, 'grid', [(0, 1), (1, 0)])  9.01 us
    unnamed x36, local copies, waits for them, and re-layouts  5.93 us
    pallas_call x1, Pallas kernels, local(): pl.pallas_call(section, in_specs=[SMEM] + [VMEM] * 13, out_specs=[VMEM] *...  5.89 us
    ppermute x1, starting transfers between devices, local(): lax.ppermute(high, 'lat', [(i, i + 1) for i in range(lat_blocks - 1)])  5 us
    ppermute x1, waiting for transfers between devices, local(): relayed = lax.ppermute(far, 'lon', hop)  3.74 us
    ppermute x1, waiting for transfers between devices, local(): sides = lax.ppermute(sides, 'lon', [(i, i ^ 1) for i in range(lon_blocks)])  2.48 us
  transfers between devices with their start and end apart: 5, of which 4 were waited for; matrix products, arithmetic and copies ran while one was open for 1% of the time, Pallas kernels for 0%

profile of v1, /device:TPU:1, one launch (start us, length us, event | category | flops | bytes accessed | tf_op | source)
XLA Modules:
  0.0 92.2 jit_solution(2624349528010571130)
XLA Ops:
  0.6 0.0 copy-start
  0.6 1.0 %copy-done = f32[1,3,8,32,128]{4,3,2,1,0:T(8,128)S(1)} copy-done((f32[1,3,8,32,128]{4,3,2,1,0:T(8,128)S(1)}, f32[1,3,8,32,128]{4,3,2,1,0:T(8,128)}, u32[]{:S(2)}) %copy-start) | copy-done | bytes 393240
  1.6 1.0 %copy-done.2 = f32[1,3,8,32,128]{4,3,2,1,0:T(8,128)S(1)} copy-done((f32[1,3,8,32,128]{4,3,2,1,0:T(8,128)S(1)}, f32[1,3,8,32,128]{4,3,2,1,0:T(8,128)}, u32[]{:S(2)}) %copy-start.2) | copy-done | bytes 393240
  2.6 0.3 edges.1
  3.0 0.6 copy-done.4
  3.6 0.6 copy-done.6
  4.2 1.3 %collective-permute-start.1 = (f32[32,128]{1,0:T(8,128)S(1)}, f32[32,128]{1,0:T(8,128)S(1)}, u32[]{:S(2)}, u32[]{:S(2)}) collective-permute-start(f32[32,128]{1,0:T(8,128)S(1)} %get-tuple-element.12.refs_3_), channel_id=1, source_target_pairs={{32,0},{64,32},{96,64},{128,96},{160,128},{192,160},{224,192},{33,... | collective-permute-start | bytes 49160 | tf_op jit(solution)/shard_map/ppermute | solution.py:414
  5.5 5.0 %collective-permute-start = (f32[32,128]{1,0:T(8,128)S(1)}, f32[32,128]{1,0:T(8,128)S(1)}, u32[]{:S(2)}, u32[]{:S(2)}) collective-permute-start(f32[32,128]{1,0:T(8,128)S(1)} %get-tuple-element.13.refs_4_), channel_id=1, source_target_pairs={{0,32},{32,64},{64,96},{96,128},{128,160},{160,192},{192,224},{1,3... | collective-permute-start | bytes 49160 | tf_op jit(solution)/shard_map/ppermute | solution.py:413
  10.5 0.6 pad_add_fusion.place_ref.refs_0_
  11.1 0.0 collective-permute-done.1.above_ref.refs_6_
  11.1 0.3 collective-permute-done.below_ref.refs_5_
  11.3 0.3 copy-done.8
  11.7 0.3 copy-done.10
  12.0 1.6 %strips.1 = (f32[12,8,128]{2,1,0:T(8,128)}, f32[24,8,128]{2,1,0:T(8,128)}) custom-call(s32[2]{0:T(128)} %pad_add_fusion.place_ref.refs_0_, f32[32,128]{1,0:T(8,128)} %copy-done.10, f32[32,128]{1,0:T(8,128)} %copy-done.8, f32[12,8,128]{2,1,0:T(8,128)} %copy-done.4, f32[12,8,128]{2,1,0:T(8,128)} %copy-done.6), custom_call_target="tpu_custom_call" | custom-call | tf_op jit(solution)/shard_map/strips/pallas_call | solution.py:415
  13.6 1.4 %collective-permute-start.2 = (f32[12,8,128]{2,1,0:T(8,128)}, f32[12,8,128]{2,1,0:T(8,128)S(1)}, u32[]{:S(2)}, u32[]{:S(2)}) collective-permute-start(f32[12,8,128]{2,1,0:T(8,128)} %get-tuple-element.17), channel_id=1, source_target_pairs={{1,3},{2,0},{3,5},{4,2},{5,7},{6,4},{7,9},{8,6},{9,11},{10,8},{11,... | collective-permute-start | bytes 147464 | tf_op jit(solution)/shard_map/ppermute | solution.py:424
  15.0 3.7 %collective-permute-done.2 = f32[12,8,128]{2,1,0:T(8,128)S(1)} collective-permute-done((f32[12,8,128]{2,1,0:T(8,128)}, f32[12,8,128]{2,1,0:T(8,128)S(1)}, u32[]{:S(2)}, u32[]{:S(2)}) %collective-permute-start.2) | collective-permute-done | bytes 49184 | tf_op jit(solution)/shard_map/ppermute | solution.py:424
  18.7 0.6 constant_dynamic-update-slice_fusion
  19.4 14.9 %collective-permute-start.3 = (f32[24,8,128]{2,1,0:T(8,128)}, f32[24,8,128]{2,1,0:T(8,128)S(1)}, u32[]{:S(2)}, u32[]{:S(2)}) collective-permute-start(f32[24,8,128]{2,1,0:T(8,128)} %constant_dynamic-update-slice_fusion), channel_id=1, source_target_pairs={{0,1},{1,0},{2,3},{3,2},{4,5},{5,4},{6,7},{7,6},{8,9},{9,8},{10,11... | collective-permute-start | bytes 294920 | tf_op jit(solution)/shard_map/ppermute | solution.py:426
  34.2 2.5 %collective-permute-done.3.refs_9_ = f32[24,8,128]{2,1,0:T(8,128)S(1)} collective-permute-done((f32[24,8,128]{2,1,0:T(8,128)}, f32[24,8,128]{2,1,0:T(8,128)S(1)}, u32[]{:S(2)}, u32[]{:S(2)}) %collective-permute-start.3) | collective-permute-done | bytes 98336 | tf_op jit(solution)/shard_map/ppermute | solution.py:426
  36.7 0.0 copy-done.1
  36.7 0.0 copy-done.3
  36.7 0.0 copy-done.13
  36.7 0.0 copy-done.14
  36.7 0.0 copy-done.15
  36.8 0.7 copy-done.9
  37.5 0.7 copy-done.11
  38.2 5.9 %section.1 = (f32[1,3,8,32,128]{4,3,2,1,0:T(8,128)}, f32[1,3,8,32,128]{4,3,2,1,0:T(8,128)}, f32[32,8,128]{2,1,0:T(8,128)S(1)}) custom-call(s32[2]{0:T(128)S(1)} %copy-done.12, f32[1,3,8,32,128]{4,3,2,1,0:T(8,128)S(1)} %copy-done.1, f32[1,3,8,32,128]{4,3,2,1,0:T(8,128)S(1)} %copy-done.3, f32[32,128]{1,0:T(8,128)S(1)} %get-tuple-element.12.refs_3_, ...), custom_call_target="tpu_custom_call" | custom-call | tf_op jit(solution)/shard_map/section/pallas_call | solution.py:432
  44.1 35.5 %all_to_all.5 = f32[32,8,128]{2,1,0:T(8,128)S(1)} all-to-all(f32[32,8,128]{2,1,0:T(8,128)S(1)} %get-tuple-element.20), channel_id=1, replica_groups=mesh['grid'=2,'lat'=8,'lon'=32] {'lon'}, dimensions={0} | all-to-all | bytes 262144 | tf_op jit(solution)/shard_map/all_to_all | solution.py:465
  79.6 9.0 %collective-permute-start.4 = (f32[32,8,128]{2,1,0:T(8,128)S(1)}, f32[32,8,128]{2,1,0:T(8,128)S(1)}, u32[]{:S(2)}, u32[]{:S(2)}) collective-permute-start(f32[32,8,128]{2,1,0:T(8,128)S(1)} %all_to_all.5), channel_id=1, source_target_pairs={{0,256},{256,0},{1,257},{257,1},{2,258},{258,2},{3,259},{259,3},{4... | collective-permute-start | bytes 393224 | tf_op jit(solution)/shard_map/ppermute | solution.py:466
  88.6 1.0 %collective-permute-done.4.got_ref = f32[32,8,128]{2,1,0:T(8,128)S(1)} collective-permute-done((f32[32,8,128]{2,1,0:T(8,128)S(1)}, f32[32,8,128]{2,1,0:T(8,128)S(1)}, u32[]{:S(2)}, u32[]{:S(2)}) %collective-permute-start.4) | collective-permute-done | bytes 131104 | tf_op jit(solution)/shard_map/ppermute | solution.py:466
  89.6 0.6 copy-done.17
  90.2 2.0 %collect.1 = f32[1,1,1,48,128]{4,3,2,1,0:T(8,128)} custom-call(f32[32,8,128]{2,1,0:T(8,128)} %copy-done.17), custom_call_target="tpu_custom_call" | custom-call | tf_op jit(solution)/shard_map/collect/pallas_call | solution.py:467
  (21 shorter events, 0.0 us)
Async XLA Ops:
  0.6 1.0 %copy-start = (f32[1,3,8,32,128]{4,3,2,1,0:T(8,128)S(1)}, f32[1,3,8,32,128]{4,3,2,1,0:T(8,128)}, u32[]{:S(2)}) copy-start(f32[1,3,8,32,128]{4,3,2,1,0:T(8,128)} %refs_1_.1) | copy-start | bytes 1179652
  1.6 1.0 %copy-start.2 = (f32[1,3,8,32,128]{4,3,2,1,0:T(8,128)S(1)}, f32[1,3,8,32,128]{4,3,2,1,0:T(8,128)}, u32[]{:S(2)}) copy-start(f32[1,3,8,32,128]{4,3,2,1,0:T(8,128)} %refs_2_.1) | copy-start | bytes 1179652
  2.6 34.1 %copy-start.1 = (f32[1,3,8,32,128]{4,3,2,1,0:T(8,128)S(1)}, f32[1,3,8,32,128]{4,3,2,1,0:T(8,128)}, u32[]{:S(2)}) copy-start(f32[1,3,8,32,128]{4,3,2,1,0:T(8,128)} %refs_1_.1) | copy-start | bytes 1179652
  2.6 34.1 %copy-start.3 = (f32[1,3,8,32,128]{4,3,2,1,0:T(8,128)S(1)}, f32[1,3,8,32,128]{4,3,2,1,0:T(8,128)}, u32[]{:S(2)}) copy-start(f32[1,3,8,32,128]{4,3,2,1,0:T(8,128)} %refs_2_.1) | copy-start | bytes 1179652
  3.0 0.6 copy-start.4
  3.6 0.6 copy-start.6
  4.2 6.9 %collective-permute-start.1 = (f32[32,128]{1,0:T(8,128)S(1)}, f32[32,128]{1,0:T(8,128)S(1)}, u32[]{:S(2)}, u32[]{:S(2)}) collective-permute-start(f32[32,128]{1,0:T(8,128)S(1)} %get-tuple-element.12.refs_3_), channel_id=1, source_target_pairs={{32,0},{64,32},{96,64},{128,96},{160,128},{192,160},{224,192},{33,... | collective-permute-start | bytes 49160 | tf_op jit(solution)/shard_map/ppermute | solution.py:414
  5.5 5.9 %collective-permute-start = (f32[32,128]{1,0:T(8,128)S(1)}, f32[32,128]{1,0:T(8,128)S(1)}, u32[]{:S(2)}, u32[]{:S(2)}) collective-permute-start(f32[32,128]{1,0:T(8,128)S(1)} %get-tuple-element.13.refs_4_), channel_id=1, source_target_pairs={{0,32},{32,64},{64,96},{96,128},{128,160},{160,192},{192,224},{1,3... | collective-permute-start | bytes 49160 | tf_op jit(solution)/shard_map/ppermute | solution.py:413
  11.1 0.6 copy-start.8
  11.3 0.6 copy-start.10
  12.0 24.8 %copy-start.13 = (s32[1,1,1,512]{3,2,1,0:T(1,128)S(1)}, s32[1,1,1,512]{3,2,1,0:T(1,128)}, u32[]{:S(2)}) copy-start(s32[1,1,1,512]{3,2,1,0:T(1,128)} %refs_11_.1) | copy-start | bytes 6148
  12.0 24.8 %copy-start.14 = (f32[1,1,1,512]{3,2,1,0:T(1,128)S(1)}, f32[1,1,1,512]{3,2,1,0:T(1,128)}, u32[]{:S(2)}) copy-start(f32[1,1,1,512]{3,2,1,0:T(1,128)} %refs_12_.1) | copy-start | bytes 6148
  12.0 24.8 %copy-start.15 = (s32[1,1,1,512]{3,2,1,0:T(1,128)S(1)}, s32[1,1,1,512]{3,2,1,0:T(1,128)}, u32[]{:S(2)}) copy-start(s32[1,1,1,512]{3,2,1,0:T(1,128)} %refs_13_.1) | copy-start | bytes 6148
  12.0 24.8 %copy-start.16 = (s32[1,1,1,32]{3,2,1,0:T(1,128)S(1)}, s32[1,1,1,32]{3,2,1,0:T(1,128)}, u32[]{:S(2)}) copy-start(s32[1,1,1,32]{3,2,1,0:T(1,128)} %refs_10_.1) | copy-start | bytes 388
  13.6 23.2 %copy-start.12 = (s32[2]{0:T(128)S(1)}, s32[2]{0:T(128)}, u32[]{:S(2)}) copy-start(s32[2]{0:T(128)} %pad_add_fusion.place_ref.refs_0_) | copy-start | bytes 28
  13.6 5.2 %collective-permute-start.2 = (f32[12,8,128]{2,1,0:T(8,128)}, f32[12,8,128]{2,1,0:T(8,128)S(1)}, u32[]{:S(2)}, u32[]{:S(2)}) collective-permute-start(f32[12,8,128]{2,1,0:T(8,128)} %get-tuple-element.17), channel_id=1, source_target_pairs={{1,3},{2,0},{3,5},{4,2},{5,7},{6,4},{7,9},{8,6},{9,11},{10,8},{11,... | collective-permute-start | bytes 147464 | tf_op jit(solution)/shard_map/ppermute | solution.py:424
  18.7 18.1 %copy-start.5 = (f32[12,8,128]{2,1,0:T(8,128)S(1)}, f32[12,8,128]{2,1,0:T(8,128)}, u32[]{:S(2)}) copy-start(f32[12,8,128]{2,1,0:T(8,128)} %copy-done.4) | copy-start | bytes 147460
  18.7 18.1 %copy-start.7 = (f32[12,8,128]{2,1,0:T(8,128)S(1)}, f32[12,8,128]{2,1,0:T(8,128)}, u32[]{:S(2)}) copy-start(f32[12,8,128]{2,1,0:T(8,128)} %copy-done.6) | copy-start | bytes 147460
  19.4 17.4 %collective-permute-start.3 = (f32[24,8,128]{2,1,0:T(8,128)}, f32[24,8,128]{2,1,0:T(8,128)S(1)}, u32[]{:S(2)}, u32[]{:S(2)}) collective-permute-start(f32[24,8,128]{2,1,0:T(8,128)} %constant_dynamic-update-slice_fusion), channel_id=1, source_target_pairs={{0,1},{1,0},{2,3},{3,2},{4,5},{5,4},{6,7},{7,6},{8,9},{9,8},{10,11... | collective-permute-start | bytes 294920 | tf_op jit(solution)/shard_map/ppermute | solution.py:426
  36.8 0.7 copy-start.9
  37.5 0.7 copy-start.11
  79.6 10.0 %collective-permute-start.4 = (f32[32,8,128]{2,1,0:T(8,128)S(1)}, f32[32,8,128]{2,1,0:T(8,128)S(1)}, u32[]{:S(2)}, u32[]{:S(2)}) collective-permute-start(f32[32,8,128]{2,1,0:T(8,128)S(1)} %all_to_all.5), channel_id=1, source_target_pairs={{0,256},{256,0},{1,257},{257,1},{2,258},{258,2},{3,259},{259,3},{4... | collective-permute-start | bytes 393224 | tf_op jit(solution)/shard_map/ppermute | solution.py:466
  89.6 0.6 copy-start.17

commit v2 on v1

--- a/solution.py
+++ b/solution.py
@@ -61,30 +61,38 @@
     last_ref[11] = jnp.zeros((LEVELS, CELLS_T), F32)
 
 
-def strips_kernel(place_ref, below_ref, above_ref, first_ref, last_ref, far_ref, near_ref):
-    odd = place_ref[1] % 2
-
-    def corner(row):
-        shape = (LEVELS, CELLS_T)
+def corners_kernel(
+    below_ref, above_ref, first_ref, last_ref, before_ref, after_ref, first_out_ref, last_out_ref
+):
+    shape = (LEVELS, CELLS_T)
+    for row, source, target in ((0, first_ref, first_out_ref), (CELLS_P - 1, last_ref, last_out_ref)):
         below = jnp.broadcast_to(below_ref[row : row + 1, :], shape)
         above = jnp.broadcast_to(above_ref[row : row + 1, :], shape)
-        return jnp.where(rows_of(shape) == 0, below, above)
-
-    @pl.when(odd == 0)
+        target[0:11] = source[0:11]
+        target[11] = jnp.where(rows_of(shape) == 0, below, above)
+
+
+def second_kernel(place_ref, before_ref, after_ref, low_ref, high_ref, low_out_ref, high_out_ref):
+    @pl.when(place_ref[1] % 2 == 1)
     def _():
-        far_ref[...] = first_ref[...]
-        far_ref[11] = corner(0)
-        near_ref[0:12] = last_ref[...]
-        near_ref[11] = corner(CELLS_P - 1)
-
-    @pl.when(odd == 1)
+        low_out_ref[...] = low_ref[...]
+        high_out_ref[...] = high_ref[...]
+
+    @pl.when(place_ref[1] % 2 == 0)
     def _():
-        far_ref[...] = last_ref[...]
-        far_ref[11] = corner(CELLS_P - 1)
-        near_ref[0:12] = first_ref[...]
-        near_ref[11] = corner(0)
-
-    near_ref[12:24] = jnp.zeros((12, LEVELS, CELLS_T), F32)
+        lane = lanes_of((LEVELS, CELLS_T))
+        low = jnp.zeros((LEVELS, CELLS_T), F32)
+        high = jnp.zeros((LEVELS, CELLS_T), F32)
+        for side, ref in ((0, before_ref), (1, after_ref)):
+            for comp in range(6):
+                spot = 6 * side + comp
+                block = ref[comp]
+                low = jnp.where(lane == spot, pltpu.roll(block, spot, 1) if spot else block, low)
+                high = jnp.where(lane == spot, pltpu.roll(block, spot + 1, 1), high)
+        low_out_ref[0:LEVELS] = low
+        high_out_ref[0:LEVELS] = high
+        low_out_ref[LEVELS:] = jnp.zeros((CELLS_P - LEVELS, CELLS_T), F32)
+        high_out_ref[LEVELS:] = jnp.zeros((CELLS_P - LEVELS, CELLS_T), F32)
 
 
 def flux_of(center, grad_r, grad_t, grad_p, spacing, wanted):
@@ -127,10 +135,65 @@
     return result
 
 
+def radius(level, spacing):
+    return inner_radius + (level.astype(F32) + 0.5) * spacing
+
+
+def inverse_sine(index, theta_step):
+    return 1.0 / jnp.sin(0.25 * math.pi + (index.astype(F32) + 0.5) * theta_step)
+
+
+def level_steps(level, sine, steps, scale):
+    spacing, theta_step, phi_step = steps
+    low_level = jnp.maximum(level - 1, 0)
+    high_level = jnp.minimum(level + 1, LEVELS - 1)
+    ends = (level == 0) | (level == LEVELS - 1)
+    step_r = jnp.where(ends, scale / spacing, 0.5 * scale / spacing)
+    inverse = 1.0 / radius(jnp.full((8, CELLS_T), level, jnp.int32), spacing)
+    step_t = (inverse * (0.5 * scale / theta_step))[0:1]
+    step_p = (sine * inverse * (0.5 * scale / phi_step))[0:1]
+    return low_level, high_level, step_r, step_t, step_p
+
+
+def along_t(block, ends, step):
+    lane = lanes_of(block.shape)
+    up = jnp.where(lane == CELLS_T - 1, ends, pltpu.roll(block, CELLS_T - 1, 1))
+    down = jnp.where(lane == 0, ends, pltpu.roll(block, 1, 1))
+    return (up - down) * step
+
+
+def flux_kernel(steps, parity, place_ref, vel_ref, mag_ref, below_ref, above_ref, *rest):
+    flux_ref = rest[-1]
+    wide = (CELLS_P, CELLS_T)
+
+    @pl.when(place_ref[1] % 2 == parity)
+    def _():
+        is_below = lanes_of(wide) % 2 == 1
+        beside = jnp.where(is_below, below_ref[...], above_ref[...])
+        own_sine = inverse_sine(place_ref[0] * CELLS_T + lanes_of((8, CELLS_T)), steps[1])
+
+        def make_flux(level, carry):
+            low_level, high_level, step_r, step_t, step_p = level_steps(level, own_sine, steps, 1.0)
+            center, grad_r, grad_t, grad_p = [], [], [], []
+            for comp in range(6):
+                ref, index = pick(vel_ref, mag_ref, comp)
+                block = ref[0, index, level]
+                center.append(block)
+                grad_r.append((ref[0, index, high_level] - ref[0, index, low_level]) * step_r)
+                ends = pltpu.roll(beside, 2 * CELLS_T - 1 - 16 * comp - 2 * level, 1)
+                grad_t.append(along_t(block, ends, step_t))
+                gap = pltpu.roll(block, CELLS_P - 1, 0) - pltpu.roll(block, 1, 0)
+                grad_p.append(gap * step_p)
+            flux = flux_of(center, grad_r, grad_t, grad_p, steps[0], range(9))
+            for chan in range(9):
+                flux_ref[chan, level] = flux[chan]
+            return carry
+
+        lax.fori_loop(0, LEVELS, make_flux, 0)
+
+
 def section_kernel(
-    spacing,
-    theta_step,
-    phi_step,
+    steps,
     lat_blocks,
     lon_blocks,
     place_ref,
@@ -138,26 +201,37 @@
     mag_ref,
     low_ref,
     high_ref,
-    below_ref,
-    above_ref,
+    below_even_ref,
+    above_even_ref,
+    below_odd_ref,
+    above_odd_ref,
     first_ref,
     last_ref,
-    side_ref,
+    before_even_ref,
+    after_even_ref,
+    before_odd_ref,
+    after_odd_ref,
     rows_ref,
     cell_ref,
     weight_ref,
     slot_ref,
-    new_vel_ref,
-    new_mag_ref,
+    flux_in_ref,
+    out_vel_ref,
+    out_mag_ref,
     send_ref,
     flux_ref,
     edge_t_ref,
     edge_p_ref,
     taken_ref,
+    side_ref,
+    new_vel_ref,
+    new_mag_ref,
+    sem_ref,
 ):
+    spacing, theta_step, phi_step = steps
     lat = place_ref[0]
     lon = place_ref[1]
-    odd_block = lon % 2
+    odd_block = lon % 2 == 1
     time_step = courant * spacing
     wide = (CELLS_P, CELLS_T)
     flat = (LEVELS, CELLS_T)
@@ -165,34 +239,43 @@
     row = rows_of(wide)
     lane_flat = lanes_of(flat)
     row_flat = rows_of(flat)
-    first_lane, last_lane = lane == 0, lane == CELLS_T - 1
     first_row, last_row = row == 0, row == CELLS_P - 1
-
-    def radius(level):
-        return inner_radius + (level.astype(F32) + 0.5) * spacing
-
-    def inverse_sine(index):
-        return 1.0 / jnp.sin(0.25 * math.pi + (index.astype(F32) + 0.5) * theta_step)
-
     first_t = lat * CELLS_T
-    own_sine = inverse_sine(first_t + lanes_of((8, CELLS_T)))
-
-    base = (12 * (1 - odd_block), 12 * odd_block)
+    own_sine = inverse_sine(first_t + lanes_of((8, CELLS_T)), theta_step)
+
+    @pl.when(odd_block)
+    def _():
+        side_ref[0] = before_odd_ref[...]
+        side_ref[1] = after_odd_ref[...]
+
+    @pl.when(jnp.logical_not(odd_block))
+    def _():
+        side_ref[0] = before_even_ref[...]
+        side_ref[1] = after_even_ref[...]
 
     is_below = lane % 2 == 1
     level_of = (lane % 16) // 2
-    below, above = below_ref[...], above_ref[...]
+    below = jnp.where(odd_block, below_odd_ref[...], below_even_ref[...])
+    above = jnp.where(odd_block, above_odd_ref[...], above_even_ref[...])
     beside = jnp.where(is_below, below, above)
 
     def swapped(block):
         return jnp.where(is_below, pltpu.roll(block, 1, 1), pltpu.roll(block, CELLS_T - 1, 1))
 
     def corner(side):
-        tile = side_ref[base[side] + 11]
-        return jnp.where(lane_flat[0:1] % 2 == 1, tile[0:1], tile[1:2])
+        tile = side_ref[side, 11]
+        held = jnp.where(lane_flat[0:1] % 2 == 1, tile[0:1], tile[1:2])
+        spot = 2 * row_flat
+        total = jnp.zeros(flat, F32)
+        for comp in range(6):
+            start = 6 * side + comp
+            for ref, shift in ((below_odd_ref, 1), (above_odd_ref, 0)):
+                column = ref[0:LEVELS, start : start + 1]
+                total = jnp.where(lane_flat == spot + (16 * comp + shift), column, total)
+        return jnp.where(odd_block, held, jnp.sum(total, axis=0, keepdims=True))
 
     corners = (corner(0), corner(1))
-    inverse_r = 1.0 / radius(level_of)
+    inverse_r = 1.0 / radius(level_of, spacing)
     own_step = jnp.where((level_of == 0) | (level_of == LEVELS - 1), 1.0 / spacing, 0.5 / spacing)
     up = jnp.where(level_of == LEVELS - 1, beside, pltpu.roll(beside, CELLS_T - 2, 1))
     down = jnp.where(level_of == 0, beside, pltpu.roll(beside, 2, 1))
@@ -202,10 +285,11 @@
     pack_t = swapped(inner - outer) * (
         jnp.where(is_below, 0.5 / theta_step, -0.5 / theta_step) * inverse_r
     )
-    t_index = first_t + jnp.where(is_below, -1, CELLS_T)
+    t_index = first_t + jnp.where(is_below[0:8], -1, CELLS_T)
+    edge_sine = inverse_sine(t_index, theta_step)[0:1]
     up = jnp.where(last_row, corners[1], pltpu.roll(beside, CELLS_P - 1, 0))
     down = jnp.where(first_row, corners[0], pltpu.roll(beside, 1, 0))
-    pack_p = (up - down) * (inverse_sine(t_index) * inverse_r * (0.5 / phi_step))
+    pack_p = (up - down) * (edge_sine * inverse_r * (0.5 / phi_step))
 
     def spread(block):
         return [block if comp == 0 else pltpu.roll(block, CELLS_T - 16 * comp, 1) for comp in range(6)]
@@ -220,12 +304,24 @@
     level_step = jnp.where(
         (row_flat == 0) | (row_flat == LEVELS - 1), 1.0 / spacing, 0.5 / spacing
     )
-    inverse_flat = 1.0 / radius(row_flat)
-    for side in range(2):
-        inner_ref = first_ref if side == 0 else last_ref
-        sign = 1.0 if side == 0 else -1.0
-        center = [side_ref[base[side] + comp] for comp in range(6)]
-        corner_row = jnp.broadcast_to(corners[side], flat)
+    inverse_flat = 1.0 / radius(row_flat, spacing)
+    step_t = inverse_flat * (0.5 / theta_step)
+    step_p = own_sine * inverse_flat * (0.5 / phi_step)
+    for kind in range(4):
+        side, own = kind % 2, kind // 2 == 1
+        edge_row_ref = first_ref if side == 0 else last_ref
+        if own:
+            center = [edge_row_ref[comp] for comp in range(6)]
+            near = [side_ref[side, comp] for comp in range(5)]
+            away = [edge_row_ref[6 + comp] for comp in range(5)]
+            start = 0 if side == 0 else CELLS_P - 1
+            ends = beside[start : start + 1]
+        else:
+            center = [side_ref[side, comp] for comp in range(6)]
+            near = [side_ref[side, 6 + comp] for comp in range(5)]
+            away = [edge_row_ref[comp] for comp in range(5)]
+            ends = corners[side]
+        ends = jnp.broadcast_to(ends, flat)
         grad_r, grad_t, grad_p = [], [], []
         for comp in range(6):
             block = center[comp]
@@ -233,65 +329,35 @@
             down = jnp.where(row_flat == 0, block, pltpu.roll(block, 1, 0))
             grad_r.append((up - down) * level_step)
             spot = 16 * comp + 2 * row_flat
-            before = jnp.sum(
-                jnp.where(lane_flat == spot + 1, corner_row, 0.0), axis=1, keepdims=True
-            )
-            after = jnp.sum(jnp.where(lane_flat == spot, corner_row, 0.0), axis=1, keepdims=True)
+            before = jnp.sum(jnp.where(lane_flat == spot + 1, ends, 0.0), axis=1, keepdims=True)
+            after = jnp.sum(jnp.where(lane_flat == spot, ends, 0.0), axis=1, keepdims=True)
             up = jnp.where(lane_flat == CELLS_T - 1, after, pltpu.roll(block, CELLS_T - 1, 1))
             down = jnp.where(lane_flat == 0, before, pltpu.roll(block, 1, 1))
-            grad_t.append((up - down) * (inverse_flat * (0.5 / theta_step)))
+            grad_t.append((up - down) * step_t)
             if comp < 5:
-                gap = inner_ref[comp] - side_ref[base[side] + 6 + comp]
-                grad_p.append(gap * (own_sine * inverse_flat * (sign * 0.5 / phi_step)))
+                gap = away[comp] - near[comp] if side == 0 else near[comp] - away[comp]
+                grad_p.append(gap * step_p)
             else:
                 grad_p.append(None)
-        edge = flux_of(center, grad_r, grad_t, grad_p, spacing, ALONG_P)
-        outside = lon == (0 if side == 0 else lon_blocks - 1)
-        for slot, chan in enumerate(ALONG_P):
-            edge_p_ref[side, slot] = jnp.where(outside, 0.0, edge[chan])
-
-    def shifts(level, scale):
-        low_level = jnp.maximum(level - 1, 0)
-        high_level = jnp.minimum(level + 1, LEVELS - 1)
-        ends = (level == 0) | (level == LEVELS - 1)
-        step_r = jnp.where(ends, scale / spacing, 0.5 * scale / spacing)
-        inverse = 1.0 / radius(jnp.full((8, CELLS_T), level, jnp.int32))
-        step_t = (inverse * (0.5 * scale / theta_step))[0:1]
-        step_p = (own_sine * inverse * (0.5 * scale / phi_step))[0:1]
-        return low_level, high_level, step_r, step_t, step_p
-
-    def along_t(block, ends, step):
-        up = jnp.where(last_lane, ends, pltpu.roll(block, CELLS_T - 1, 1))
-        down = jnp.where(first_lane, ends, pltpu.roll(block, 1, 1))
-        return (up - down) * step
+        if own:
+            edge = flux_of(center, grad_r, grad_t, grad_p, spacing, range(9))
+            for chan in range(9):
+                flux_ref[chan, :, 0 if side == 0 else CELLS_P - 1, :] = edge[chan]
+        else:
+            edge = flux_of(center, grad_r, grad_t, grad_p, spacing, ALONG_P)
+            outside = lon == (0 if side == 0 else lon_blocks - 1)
+            for slot, chan in enumerate(ALONG_P):
+                edge_p_ref[side, slot] = jnp.where(outside, 0.0, edge[chan])
 
     def along_p(block, before, after, step):
         up = jnp.where(last_row, after, pltpu.roll(block, CELLS_P - 1, 0))
         down = jnp.where(first_row, before, pltpu.roll(block, 1, 0))
         return (up - down) * step
 
-    def make_flux(level, carry):
-        low_level, high_level, step_r, step_t, step_p = shifts(level, 1.0)
-        center, grad_r, grad_t, grad_p = [], [], [], []
-        for comp in range(6):
-            ref, index = pick(vel_ref, mag_ref, comp)
-            block = ref[0, index, level]
-            center.append(block)
-            grad_r.append((ref[0, index, high_level] - ref[0, index, low_level]) * step_r)
-            ends = pltpu.roll(beside, 2 * CELLS_T - 1 - 16 * comp - 2 * level, 1)
-            grad_t.append(along_t(block, ends, step_t))
-            before = side_ref[base[0] + comp, pl.ds(level, 1), :]
-            after = side_ref[base[1] + comp, pl.ds(level, 1), :]
-            grad_p.append(along_p(block, before, after, step_p))
-        flux = flux_of(center, grad_r, grad_t, grad_p, spacing, range(9))
-        for chan in range(9):
-            flux_ref[chan, level] = flux[chan]
-        return carry
-
-    lax.fori_loop(0, LEVELS, make_flux, 0)
-
     def advance(level, carry):
-        low_level, high_level, step_r, step_t, step_p = shifts(level, time_step)
+        low_level, high_level, step_r, step_t, step_p = level_steps(
+            level, own_sine, steps, time_step
+        )
 
         def d_r(chan):
             return (flux_ref[chan, high_level] - flux_ref[chan, low_level]) * step_r
@@ -313,7 +379,15 @@
         new_mag_ref[0, 0, level] = mag_ref[0, 0, level] + (d_t(8) - d_p(7))
         new_mag_ref[0, 1, level] = mag_ref[0, 1, level] + (d_p(6) - d_r(8))
         new_mag_ref[0, 2, level] = mag_ref[0, 2, level] + (d_r(7) - d_t(6))
+        for copy in out_copies(level):
+            copy.start()
         return carry
+
+    def out_copies(level):
+        return [
+            pltpu.make_async_copy(new.at[0, :, level], out.at[0, :, level], sem_ref.at[which, level])
+            for which, new, out in ((0, new_vel_ref, out_vel_ref), (1, new_mag_ref, out_mag_ref))
+        ]
 
     lax.fori_loop(0, LEVELS, advance, 0)
 
@@ -362,6 +436,13 @@
         for block in range(8):
             send_ref[chunk * 8 + block] = turned[16 * block : 16 * block + 8]
 
+    def finish(level, carry):
+        for copy in out_copies(level):
+            copy.wait()
+        return carry
+
+    lax.fori_loop(0, LEVELS, finish, 0)
+
 
 def collect_kernel(got_ref, out_ref):
     rows = got_ref.shape[0] * got_ref.shape[1]
@@ -383,24 +464,15 @@
 
 VMEM = pl.BlockSpec(memory_space=pltpu.VMEM)
 SMEM = pl.BlockSpec(memory_space=pltpu.SMEM)
-LIMIT = pltpu.CompilerParams(vmem_limit_bytes=32 * 1024 * 1024)
+HBM = pl.BlockSpec(memory_space=pltpu.HBM)
+
+
+def limit(mebibytes):
+    return pltpu.CompilerParams(vmem_limit_bytes=mebibytes * 1024 * 1024)
 
 
 def tiles(*shape):
     return jax.ShapeDtypeStruct(shape, F32)
-
-
-def edges(velocity, magnetic):
-    pack = tiles(CELLS_P, CELLS_T)
-    strip = tiles(12, LEVELS, CELLS_T)
-    return pl.pallas_call(
-        edges_kernel,
-        in_specs=[VMEM] * 2,
-        out_specs=[VMEM] * 4,
-        out_shape=[pack, pack, strip, strip],
-        compiler_params=LIMIT,
-        name="edges",
-    )(velocity, magnetic)
 
 
 def local(velocity, magnetic, pair_rows, send_cell, send_weight, cycle_slot):
@@ -409,42 +481,99 @@
     phi_step = 1.5 * math.pi / (lon_blocks * CELLS_P)
     spacing = inner_radius * theta_step
     place = jnp.stack([lax.axis_index("lat"), lax.axis_index("lon")]).astype(jnp.int32)
-    low, high, first, last = edges(velocity, magnetic)
-    below = lax.ppermute(high, "lat", [(i, i + 1) for i in range(lat_blocks - 1)])
-    above = lax.ppermute(low, "lat", [(i + 1, i) for i in range(lat_blocks - 1)])
-    far, near = pl.pallas_call(
-        strips_kernel,
+    pack = tiles(CELLS_P, CELLS_T)
+    strip = tiles(12, LEVELS, CELLS_T)
+    evens, odds = range(0, lon_blocks, 2), range(1, lon_blocks, 2)
+
+    def along_lat(block, step, lons):
+        pairs = [
+            (lat * lon_blocks + lon, (lat + step) * lon_blocks + lon)
+            for lat in range(lat_blocks)
+            for lon in lons
+            if 0 <= lat + step < lat_blocks
+        ]
+        return lax.ppermute(block, ("lat", "lon"), pairs)
+
+    def along_lon(block, step, lons):
+        pairs = [(lon, lon + step) for lon in lons if 0 <= lon + step < lon_blocks]
+        return lax.ppermute(block, "lon", pairs)
+
+    low, high, first, last = pl.pallas_call(
+        edges_kernel,
+        in_specs=[VMEM] * 2,
+        out_specs=[VMEM] * 4,
+        out_shape=[pack, pack, strip, strip],
+        compiler_params=limit(4),
+        name="edges",
+    )(velocity, magnetic)
+    below_even = along_lat(high, 1, evens)
+    above_even = along_lat(low, -1, evens)
+    before_even = along_lon(last, 1, odds)
+    after_even = along_lon(first, -1, odds)
+    first_full, last_full = pl.pallas_call(
+        corners_kernel,
+        in_specs=[VMEM] * 6,
+        out_specs=[VMEM] * 2,
+        out_shape=[strip, strip],
+        compiler_params=limit(4),
+        name="corners",
+    )(below_even, above_even, first, last, before_even, after_even)
+    before_odd = along_lon(last_full, 1, evens)
+    after_odd = along_lon(first_full, -1, evens)
+    second_low, second_high = pl.pallas_call(
+        second_kernel,
         in_specs=[SMEM] + [VMEM] * 4,
         out_specs=[VMEM] * 2,
-        out_shape=[tiles(12, LEVELS, CELLS_T), tiles(24, LEVELS, CELLS_T)],
-        name="strips",
-    )(place, below, above, first, last)
-    hop = [(i, i - 2 if i % 2 == 0 else i + 2) for i in range(lon_blocks)]
-    hop = [(i, j) for i, j in hop if 0 <= j < lon_blocks]
-    relayed = lax.ppermute(far, "lon", hop)
-    sides = lax.dynamic_update_slice(near, relayed, (12, 0, 0))
-    sides = lax.ppermute(sides, "lon", [(i, i ^ 1) for i in range(lon_blocks)])
+        out_shape=[pack, pack],
+        compiler_params=limit(4),
+        name="second",
+    )(place, before_even, after_even, low, high)
+    every = range(lon_blocks)
+    below_odd = along_lat(second_high, 1, every)
+    above_odd = along_lat(second_low, -1, every)
     slots_total = send_cell.shape[-1]
+    steps = (spacing, theta_step, phi_step)
 
     def section(*refs):
-        section_kernel(spacing, theta_step, phi_step, lat_blocks, lon_blocks, *refs)
-
-    new_velocity, new_magnetic, payload = pl.pallas_call(
+        section_kernel(steps, lat_blocks, lon_blocks, *refs)
+
+    def flux_of_cells(parity, below, above, *given):
+        def kernel(*refs):
+            flux_kernel(steps, parity, *refs)
+
+        return pl.pallas_call(
+            kernel,
+            in_specs=[SMEM] + [VMEM] * (4 + len(given)),
+            out_specs=VMEM,
+            out_shape=tiles(9, LEVELS, CELLS_P, CELLS_T),
+            input_output_aliases={5: 0} if given else {},
+            compiler_params=limit(8),
+            name="flux",
+        )(place, velocity, magnetic, below, above, *given)
+
+    flux = flux_of_cells(0, below_even, above_even)
+    flux = flux_of_cells(1, below_odd, above_odd, flux)
+    new_velocity, new_magnetic, payload, _ = pl.pallas_call(
         section,
-        in_specs=[SMEM] + [VMEM] * 13,
-        out_specs=[VMEM] * 3,
+        in_specs=[SMEM] + [VMEM] * 19,
+        out_specs=[HBM] * 2 + [VMEM, VMEM],
         out_shape=[
             tiles(*velocity.shape),
             tiles(*magnetic.shape),
             tiles(lon_blocks, 8, CELLS_T),
+            tiles(9, LEVELS, CELLS_P, CELLS_T),
         ],
+        input_output_aliases={19: 3},
         scratch_shapes=[
-            pltpu.VMEM((9, LEVELS, CELLS_P, CELLS_T), F32),
             pltpu.VMEM((5, CELLS_P, CELLS_T), F32),
             pltpu.VMEM((2, 5, LEVELS, CELLS_T), F32),
             pltpu.VMEM((8, LEVELS, slots_total), F32),
+            pltpu.VMEM((2, 12, LEVELS, CELLS_T), F32),
+            pltpu.VMEM(velocity.shape, F32),
+            pltpu.VMEM(magnetic.shape, F32),
+            pltpu.SemaphoreType.DMA((2, LEVELS)),
         ],
-        compiler_params=LIMIT,
+        compiler_params=limit(16),
         name="section",
     )(
         place,
@@ -452,25 +581,32 @@
         magnetic,
         low,
         high,
-        below,
-        above,
+        below_even,
+        above_even,
+        below_odd,
+        above_odd,
         first,
         last,
-        sides,
+        before_even,
+        after_even,
+        before_odd,
+        after_odd,
         pair_rows,
         send_cell,
         send_weight,
         cycle_slot,
+        flux,
     )
     payload = lax.all_to_all(payload, "lon", split_axis=0, concat_axis=0, tiled=True)
-    payload = lax.ppermute(payload, "grid", [(0, 1), (1, 0)])
     cycle = pl.pallas_call(
         collect_kernel,
         in_specs=[VMEM],
         out_specs=VMEM,
         out_shape=tiles(1, 1, 1, 48, CYCLE),
+        compiler_params=limit(4),
         name="collect",
     )(payload)
+    cycle = lax.ppermute(cycle, "grid", [(0, 1), (1, 0)])
     return (new_velocity, new_magnetic, cycle)
 
 

time: 92.7 us -> 76.7 us (0.83)
  the two profiles are of different devices: /device:TPU:1 before, /device:TPU:193 now
where the time goes in v2:
time: 76.7 us; the launch traced here: 76.3 us
  blocking collectives  31 us (40%)
  starting transfers between devices  18.4 us (24%)
  waiting for transfers between devices  14.7 us (19%)
  Pallas kernels  8.71 us (11%)
  local copies, waits for them, and re-layouts  2.68 us (3%)
  between operations  0.85 us (1%)
    all_to_all x1, blocking collectives, local(): lax.all_to_all(payload, 'lon', split_axis=0, concat_axis=0, tiled=True)  31 us
    ppermute x4, waiting for transfers between devices, along_lon(): return lax.ppermute(block, 'lon', pairs)  12.8 us
    ppermute x4, starting transfers between devices, along_lat(): return lax.ppermute(block, ('lat', 'lon'), pairs)  10.6 us
    pallas_call x1, Pallas kernels, local(): pl.pallas_call(section, in_specs=[SMEM] + [VMEM] * 19, out_specs=[HBM] *...  4.84 us
    ppermute x4, starting transfers between devices, along_lon(): return lax.ppermute(block, 'lon', pairs)  3.9 us
    ppermute x1, starting transfers between devices, local(): cycle = lax.ppermute(cycle, 'grid', [(0, 1), (1, 0)])  3.89 us
    unnamed x17, local copies, waits for them, and re-layouts  2.68 us
    pallas_call x2, Pallas kernels, flux_of_cells(): pl.pallas_call(kernel, in_specs=[SMEM] + [VMEM] * (4 + len(given)), out_s...  2.42 us
  transfers between devices with their start and end apart: 9, of which 3 were waited for; matrix products, arithmetic and copies ran while one was open for 0% of the time, Pallas kernels for 4%

profile of v2, /device:TPU:193, one launch (start us, length us, event | category | flops | bytes accessed | tf_op | source)
XLA Modules:
  0.0 76.3 jit_solution(3712664981099859898)
XLA Ops:
  0.6 1.0 %copy-done = f32[1,3,8,32,128]{4,3,2,1,0:T(8,128)S(1)} copy-done((f32[1,3,8,32,128]{4,3,2,1,0:T(8,128)S(1)}, f32[1,3,8,32,128]{4,3,2,1,0:T(8,128)}, u32[]{:S(2)}) %copy-start) | copy-done | bytes 393240
  1.6 1.0 %copy-done.2 = f32[1,3,8,32,128]{4,3,2,1,0:T(8,128)S(1)} copy-done((f32[1,3,8,32,128]{4,3,2,1,0:T(8,128)S(1)}, f32[1,3,8,32,128]{4,3,2,1,0:T(8,128)}, u32[]{:S(2)}) %copy-start.2) | copy-done | bytes 393240
  2.6 0.3 edges.1
  3.0 0.7 collective-permute-start.2
  3.6 1.3 %collective-permute-start.3 = (f32[12,8,128]{2,1,0:T(8,128)S(1)}, f32[12,8,128]{2,1,0:T(8,128)S(1)}, u32[]{:S(2)}, u32[]{:S(2)}) collective-permute-start(f32[12,8,128]{2,1,0:T(8,128)S(1)} %get-tuple-element.17.first_ref.refs_9_), channel_id=1, source_target_pairs={{1,0},{3,2},{5,4},{7,6},{9,8},{11,10},{13,12},{15,14},{17,16},{19,... | collective-permute-start | bytes 147464 | tf_op jit(solution)/shard_map/ppermute | solution.py:499
  4.9 1.9 %collective-permute-start.1 = (f32[32,128]{1,0:T(8,128)S(1)}, f32[32,128]{1,0:T(8,128)S(1)}, u32[]{:S(2)}, u32[]{:S(2)}) collective-permute-start(f32[32,128]{1,0:T(8,128)S(1)} %get-tuple-element.14.low_ref.refs_3_), channel_id=1, source_target_pairs={{32,0},{34,2},{36,4},{38,6},{40,8},{42,10},{44,12},{46,14},{48,16}... | collective-permute-start | bytes 49160 | tf_op jit(solution)/shard_map/ppermute | solution.py:495
  6.8 3.4 %collective-permute-start = (f32[32,128]{1,0:T(8,128)S(1)}, f32[32,128]{1,0:T(8,128)S(1)}, u32[]{:S(2)}, u32[]{:S(2)}) collective-permute-start(f32[32,128]{1,0:T(8,128)S(1)} %get-tuple-element.15.high_ref.refs_4_), channel_id=1, source_target_pairs={{0,32},{2,34},{4,36},{6,38},{8,40},{10,42},{12,44},{14,46},{16,48}... | collective-permute-start | bytes 49160 | tf_op jit(solution)/shard_map/ppermute | solution.py:495
  10.2 0.0 collective-permute-done.1.above_ref.refs_4_.refs_6_
  10.2 1.1 %collective-permute-done.below_ref.refs_3_.refs_5_ = f32[32,128]{1,0:T(8,128)S(1)} collective-permute-done((f32[32,128]{1,0:T(8,128)S(1)}, f32[32,128]{1,0:T(8,128)S(1)}, u32[]{:S(2)}, u32[]{:S(2)}) %collective-permute-start) | collective-permute-done | bytes 16416 | tf_op jit(solution)/shard_map/ppermute | solution.py:495
  11.3 0.0 collective-permute-done.2.before_ref.refs_11_
  11.3 12.7 %collective-permute-done.3.after_ref.refs_12_ = f32[12,8,128]{2,1,0:T(8,128)S(1)} collective-permute-done((f32[12,8,128]{2,1,0:T(8,128)S(1)}, f32[12,8,128]{2,1,0:T(8,128)S(1)}, u32[]{:S(2)}, u32[]{:S(2)}) %collective-permute-start.3) | collective-permute-done | bytes 49184 | tf_op jit(solution)/shard_map/ppermute | solution.py:499
  24.1 1.3 %collective-permute-start.6 = (f32[12,8,128]{2,1,0:T(8,128)S(1)}, f32[12,8,128]{2,1,0:T(8,128)S(1)}, u32[]{:S(2)}, u32[]{:S(2)}) collective-permute-start(f32[12,8,128]{2,1,0:T(8,128)S(1)} %get-tuple-element.20), channel_id=1, source_target_pairs={{0,1},{2,3},{4,5},{6,7},{8,9},{10,11},{12,13},{14,15},{16,17},{18,... | collective-permute-start | bytes 147464 | tf_op jit(solution)/shard_map/ppermute | solution.py:499
  25.4 0.7 collective-permute-start.7
  26.1 0.1 pad_add_fusion.place_ref.refs_0_
  26.1 0.6 second.1
  26.8 1.9 %collective-permute-start.4 = (f32[32,128]{1,0:T(8,128)S(1)}, f32[32,128]{1,0:T(8,128)S(1)}, u32[]{:S(2)}, u32[]{:S(2)}) collective-permute-start(f32[32,128]{1,0:T(8,128)S(1)} %get-tuple-element.18), channel_id=1, source_target_pairs={{0,32},{1,33},{2,34},{3,35},{4,36},{5,37},{6,38},{7,39},{8,40},{9,... | collective-permute-start | bytes 49160 | tf_op jit(solution)/shard_map/ppermute | solution.py:495
  28.7 3.4 %collective-permute-start.5 = (f32[32,128]{1,0:T(8,128)S(1)}, f32[32,128]{1,0:T(8,128)S(1)}, u32[]{:S(2)}, u32[]{:S(2)}) collective-permute-start(f32[32,128]{1,0:T(8,128)S(1)} %get-tuple-element.19), channel_id=1, source_target_pairs={{32,0},{33,1},{34,2},{35,3},{36,4},{37,5},{38,6},{39,7},{40,8},{41... | collective-permute-start | bytes 49160 | tf_op jit(solution)/shard_map/ppermute | solution.py:495
  32.1 1.9 %flux.2.refs_5_ = f32[9,8,32,128]{3,2,1,0:T(8,128)S(1)} custom-call(s32[2]{0:T(128)S(1)} %pad_add_fusion.place_ref.refs_0_, f32[1,3,8,32,128]{4,3,2,1,0:T(8,128)S(1)} %copy-done.1, f32[1,3,8,32,128]{4,3,2,1,0:T(8,128)S(1)} %copy-done.3, f32[32,128]{1,0:T(8,128)S(1)} %collective-permute-done.below_ref.refs_3_.refs_5_, ...), custom_call_target="tpu_custom_call" | custom-call | tf_op jit(solution)/shard_map/flux/pallas_call | solution.py:544
  34.0 0.0 copy-start.4
  34.0 0.0 copy-start.5
  34.0 0.0 copy-start.6
  34.0 0.0 copy-start.7
  34.1 0.6 flux.3.refs_19_
  34.6 0.0 copy-done.4
  34.7 0.0 copy-done.5
  34.7 0.0 copy-done.6
  34.7 4.8 %section.1 = (f32[1,3,8,32,128]{4,3,2,1,0:T(8,128)}, f32[1,3,8,32,128]{4,3,2,1,0:T(8,128)}, f32[32,8,128]{2,1,0:T(8,128)S(1)}, f32[9,8,32,128]{3,2,1,0:T(8,128)S(1)}) custom-call(s32[2]{0:T(128)S(1)} %pad_add_fusion.place_ref.refs_0_, f32[1,3,8,32,128]{4,3,2,1,0:T(8,128)S(1)} %copy-done.1, ...), custom_call_target="tpu_custom_call", output_to_operand_aliasing={{3}: (19, {})} | custom-call | tf_op jit(solution)/shard_map/section/pallas_call | solution.py:556
  39.6 31.0 %all_to_all.5.got_ref = f32[32,8,128]{2,1,0:T(8,128)S(1)} all-to-all(f32[32,8,128]{2,1,0:T(8,128)S(1)} %get-tuple-element.24), channel_id=1, replica_groups=mesh['grid'=2,'lat'=8,'lon'=32] {'lon'}, dimensions={0} | all-to-all | bytes 262144 | tf_op jit(solution)/shard_map/all_to_all | solution.py:600
  70.5 0.5 collect.1
  71.0 3.9 %collective-permute-start.8 = (f32[1,1,1,48,128]{4,3,2,1,0:T(8,128)S(1)}, f32[1,1,1,48,128]{4,3,2,1,0:T(8,128)S(1)}, u32[]{:S(2)}, u32[]{:S(2)}) collective-permute-start(f32[1,1,1,48,128]{4,3,2,1,0:T(8,128)S(1)} %collect.1), channel_id=1, source_target_pairs={{0,256},{256,0},{1,257},{257,1},{2,258},{258,2},{3,259},{259,3},{4... | collective-permute-start | bytes 73736 | tf_op jit(solution)/shard_map/ppermute | solution.py:609
  74.9 0.8 %collective-permute-done.8 = f32[1,1,1,48,128]{4,3,2,1,0:T(8,128)S(1)} collective-permute-done((f32[1,1,1,48,128]{4,3,2,1,0:T(8,128)S(1)}, f32[1,1,1,48,128]{4,3,2,1,0:T(8,128)S(1)}, u32[]{:S(2)}, u32[]{:S(2)}) %collective-permute-start.8) | collective-permute-done | bytes 24608 | tf_op jit(solution)/shard_map/ppermute | solution.py:609
  75.7 0.6 copy.14
  (12 shorter events, 0.0 us)
Async XLA Ops:
  0.6 1.0 %copy-start = (f32[1,3,8,32,128]{4,3,2,1,0:T(8,128)S(1)}, f32[1,3,8,32,128]{4,3,2,1,0:T(8,128)}, u32[]{:S(2)}) copy-start(f32[1,3,8,32,128]{4,3,2,1,0:T(8,128)} %refs_1_.5) | copy-start | bytes 1179652
  1.6 1.0 %copy-start.2 = (f32[1,3,8,32,128]{4,3,2,1,0:T(8,128)S(1)}, f32[1,3,8,32,128]{4,3,2,1,0:T(8,128)}, u32[]{:S(2)}) copy-start(f32[1,3,8,32,128]{4,3,2,1,0:T(8,128)} %refs_2_.5) | copy-start | bytes 1179652
  2.6 29.5 %copy-start.1 = (f32[1,3,8,32,128]{4,3,2,1,0:T(8,128)S(1)}, f32[1,3,8,32,128]{4,3,2,1,0:T(8,128)}, u32[]{:S(2)}) copy-start(f32[1,3,8,32,128]{4,3,2,1,0:T(8,128)} %refs_1_.5) | copy-start | bytes 1179652
  2.6 29.5 %copy-start.3 = (f32[1,3,8,32,128]{4,3,2,1,0:T(8,128)S(1)}, f32[1,3,8,32,128]{4,3,2,1,0:T(8,128)}, u32[]{:S(2)}) copy-start(f32[1,3,8,32,128]{4,3,2,1,0:T(8,128)} %refs_2_.5) | copy-start | bytes 1179652
  3.0 8.4 %collective-permute-start.2 = (f32[12,8,128]{2,1,0:T(8,128)S(1)}, f32[12,8,128]{2,1,0:T(8,128)S(1)}, u32[]{:S(2)}, u32[]{:S(2)}) collective-permute-start(f32[12,8,128]{2,1,0:T(8,128)S(1)} %get-tuple-element.16.last_ref.refs_10_), channel_id=1, source_target_pairs={{1,2},{3,4},{5,6},{7,8},{9,10},{11,12},{13,14},{15,16},{17,18},{19... | collective-permute-start | bytes 147464 | tf_op jit(solution)/shard_map/ppermute | solution.py:499
  3.6 20.5 %collective-permute-start.3 = (f32[12,8,128]{2,1,0:T(8,128)S(1)}, f32[12,8,128]{2,1,0:T(8,128)S(1)}, u32[]{:S(2)}, u32[]{:S(2)}) collective-permute-start(f32[12,8,128]{2,1,0:T(8,128)S(1)} %get-tuple-element.17.first_ref.refs_9_), channel_id=1, source_target_pairs={{1,0},{3,2},{5,4},{7,6},{9,8},{11,10},{13,12},{15,14},{17,16},{19,... | collective-permute-start | bytes 147464 | tf_op jit(solution)/shard_map/ppermute | solution.py:499
  4.9 5.3 %collective-permute-start.1 = (f32[32,128]{1,0:T(8,128)S(1)}, f32[32,128]{1,0:T(8,128)S(1)}, u32[]{:S(2)}, u32[]{:S(2)}) collective-permute-start(f32[32,128]{1,0:T(8,128)S(1)} %get-tuple-element.14.low_ref.refs_3_), channel_id=1, source_target_pairs={{32,0},{34,2},{36,4},{38,6},{40,8},{42,10},{44,12},{46,14},{48,16}... | collective-permute-start | bytes 49160 | tf_op jit(solution)/shard_map/ppermute | solution.py:495
  6.8 4.5 %collective-permute-start = (f32[32,128]{1,0:T(8,128)S(1)}, f32[32,128]{1,0:T(8,128)S(1)}, u32[]{:S(2)}, u32[]{:S(2)}) collective-permute-start(f32[32,128]{1,0:T(8,128)S(1)} %get-tuple-element.15.high_ref.refs_4_), channel_id=1, source_target_pairs={{0,32},{2,34},{4,36},{6,38},{8,40},{10,42},{12,44},{14,46},{16,48}... | collective-permute-start | bytes 49160 | tf_op jit(solution)/shard_map/ppermute | solution.py:495
  24.1 10.5 %collective-permute-start.6 = (f32[12,8,128]{2,1,0:T(8,128)S(1)}, f32[12,8,128]{2,1,0:T(8,128)S(1)}, u32[]{:S(2)}, u32[]{:S(2)}) collective-permute-start(f32[12,8,128]{2,1,0:T(8,128)S(1)} %get-tuple-element.20), channel_id=1, source_target_pairs={{0,1},{2,3},{4,5},{6,7},{8,9},{10,11},{12,13},{14,15},{16,17},{18,... | collective-permute-start | bytes 147464 | tf_op jit(solution)/shard_map/ppermute | solution.py:499
  25.4 9.2 %collective-permute-start.7 = (f32[12,8,128]{2,1,0:T(8,128)S(1)}, f32[12,8,128]{2,1,0:T(8,128)S(1)}, u32[]{:S(2)}, u32[]{:S(2)}) collective-permute-start(f32[12,8,128]{2,1,0:T(8,128)S(1)} %get-tuple-element.21), channel_id=1, source_target_pairs={{2,1},{4,3},{6,5},{8,7},{10,9},{12,11},{14,13},{16,15},{18,17},{20... | collective-permute-start | bytes 147464 | tf_op jit(solution)/shard_map/ppermute | solution.py:499
  26.8 7.2 %collective-permute-start.4 = (f32[32,128]{1,0:T(8,128)S(1)}, f32[32,128]{1,0:T(8,128)S(1)}, u32[]{:S(2)}, u32[]{:S(2)}) collective-permute-start(f32[32,128]{1,0:T(8,128)S(1)} %get-tuple-element.18), channel_id=1, source_target_pairs={{0,32},{1,33},{2,34},{3,35},{4,36},{5,37},{6,38},{7,39},{8,40},{9,... | collective-permute-start | bytes 49160 | tf_op jit(solution)/shard_map/ppermute | solution.py:495
  28.7 5.3 %collective-permute-start.5 = (f32[32,128]{1,0:T(8,128)S(1)}, f32[32,128]{1,0:T(8,128)S(1)}, u32[]{:S(2)}, u32[]{:S(2)}) collective-permute-start(f32[32,128]{1,0:T(8,128)S(1)} %get-tuple-element.19), channel_id=1, source_target_pairs={{32,0},{33,1},{34,2},{35,3},{36,4},{37,5},{38,6},{39,7},{40,8},{41... | collective-permute-start | bytes 49160 | tf_op jit(solution)/shard_map/ppermute | solution.py:495
  34.0 0.7 copy-start.4
  34.0 0.7 copy-start.5
  34.0 0.7 copy-start.6
  34.0 0.7 copy-start.7
  71.0 4.7 %collective-permute-start.8 = (f32[1,1,1,48,128]{4,3,2,1,0:T(8,128)S(1)}, f32[1,1,1,48,128]{4,3,2,1,0:T(8,128)S(1)}, u32[]{:S(2)}, u32[]{:S(2)}) collective-permute-start(f32[1,1,1,48,128]{4,3,2,1,0:T(8,128)S(1)} %collect.1), channel_id=1, source_target_pairs={{0,256},{256,0},{1,257},{257,1},{2,258},{258,2},{3,259},{259,3},{4... | collective-permute-start | bytes 73736 | tf_op jit(solution)/shard_map/ppermute | solution.py:609

commit v3 on v2

--- a/solution.py
+++ b/solution.py
@@ -189,7 +189,7 @@
                 flux_ref[chan, level] = flux[chan]
             return carry
 
-        lax.fori_loop(0, LEVELS, make_flux, 0)
+        lax.fori_loop(0, LEVELS, make_flux, 0, unroll=8)
 
 
 def section_kernel(
@@ -389,7 +389,7 @@
             for which, new, out in ((0, new_vel_ref, out_vel_ref), (1, new_mag_ref, out_mag_ref))
         ]
 
-    lax.fori_loop(0, LEVELS, advance, 0)
+    lax.fori_loop(0, LEVELS, advance, 0, unroll=8)
 
     slots_total = cell_ref.shape[-1]
     chunks = slots_total // CELLS_T
@@ -406,15 +406,33 @@
     group = cell_p // 8
     taken_ref[6:8] = jnp.zeros((2, LEVELS, slots_total), F32)
     taken_ref[6, 0:1] = slot_ref[0, 0].astype(F32)
-    for start, ref in ((0, new_vel_ref), (3, new_mag_ref)):
-
-        def take(comp, carry, start=start, ref=ref):
-            for level in range(LEVELS):
-                block = ref[0, comp, level]
-                for chunk in range(chunks):
-                    part = slice(chunk * CELLS_T, (chunk + 1) * CELLS_T)
-                    where_t = cell_t[:, part]
-                    total = jnp.zeros((8, CELLS_T), F32)
+    sub = rows_of((8, CELLS_T))
+
+    def fold(blocks):
+        for width in (4, 2, 1):
+            keep = sub % (2 * width) < width
+            half = len(blocks) // 2
+            merged = []
+            for one, two in zip(blocks[:half], blocks[half:]):
+                mine, other = jnp.where(keep, one, two), jnp.where(keep, two, one)
+                moved = pltpu.roll(other, width, 0)
+                if width < 4:
+                    moved = jnp.where(keep, pltpu.roll(other, 8 - width, 0), moved)
+                merged.append(mine + moved)
+            blocks = merged
+        return blocks[0]
+
+    for chunk in range(chunks):
+        part = slice(chunk * CELLS_T, (chunk + 1) * CELLS_T)
+        where_t = cell_t[:, part]
+        weights = [jnp.where(group[:, part] == step, scale[:, part], 0.0) for step in range(4)]
+        for start, ref in ((0, new_vel_ref), (3, new_mag_ref)):
+
+            def take(comp, carry, start=start, ref=ref, part=part, where_t=where_t, weights=weights):
+                sums = []
+                for level in range(LEVELS):
+                    block = ref[0, comp, level]
+                    total = 0.0
                     for step in range(CELLS_P // 8):
                         got = jnp.take_along_axis(
                             block[8 * step : 8 * step + 8],
@@ -422,12 +440,12 @@
                             axis=1,
                             mode="promise_in_bounds",
                         )
-                        total = jnp.where(group[:, part] == step, got, total)
-                    total = jnp.sum(total * scale[:, part], axis=0, keepdims=True)
-                    taken_ref[start + comp, level : level + 1, part] = total
-            return carry
-
-        lax.fori_loop(0, 3, take, 0)
+                        total = total + got * weights[step]
+                    sums.append(total)
+                taken_ref[start + comp, :, part] = fold(sums)
+
+            for comp in range(3):
+                take(comp, 0)
 
     for chunk in range(chunks):
         part = taken_ref[:, :, chunk * CELLS_T : (chunk + 1) * CELLS_T].reshape(64, CELLS_T)

time: 76.7 us -> 75.4 us (0.983)
  Pallas kernels: 8.71 us -> 6.87 us
    pallas_call x1, Pallas kernels: 4.84 us -> 3.53 us  [local(): pl.pallas_call(section, in_specs=[SMEM] + [VMEM] * 19, out_specs=[HBM] *...]
  transfers between devices with their start and end apart: 9 -> 9, of which waited for: 3 -> 3; matrix products, arithmetic and copies ran while one was open for 0% -> 0% of each run, Pallas kernels for 4% -> 3%
where the time goes in v3:
time: 75.4 us; the launch traced here: 75 us
  blocking collectives  31.5 us (42%)
  starting transfers between devices  18.4 us (24%)
  waiting for transfers between devices  14.7 us (19%)
  Pallas kernels  6.87 us (9%)
  local copies, waits for them, and re-layouts  2.68 us (4%)
  between operations  0.85 us (1%)
    all_to_all x1, blocking collectives, local(): lax.all_to_all(payload, 'lon', split_axis=0, concat_axis=0, tiled=True)  31.5 us
    ppermute x4, waiting for transfers between devices, along_lon(): return lax.ppermute(block, 'lon', pairs)  12.8 us
    ppermute x4, starting transfers between devices, along_lat(): return lax.ppermute(block, ('lat', 'lon'), pairs)  10.6 us
    ppermute x4, starting transfers between devices, along_lon(): return lax.ppermute(block, 'lon', pairs)  3.9 us
    ppermute x1, starting transfers between devices, local(): cycle = lax.ppermute(cycle, 'grid', [(0, 1), (1, 0)])  3.89 us
    pallas_call x1, Pallas kernels, local(): pl.pallas_call(section, in_specs=[SMEM] + [VMEM] * 19, out_specs=[HBM] *...  3.53 us
    unnamed x17, local copies, waits for them, and re-layouts  2.68 us
    pallas_call x2, Pallas kernels, flux_of_cells(): pl.pallas_call(kernel, in_specs=[SMEM] + [VMEM] * (4 + len(given)), out_s...  1.9 us
  transfers between devices with their start and end apart: 9, of which 3 were waited for; matrix products, arithmetic and copies ran while one was open for 0% of the time, Pallas kernels for 3%

profile of v3, /device:TPU:193, one launch (start us, length us, event | category | flops | bytes accessed | tf_op | source)
XLA Modules:
  0.0 75.0 jit_solution(7515088154710176776)
XLA Ops:
  0.6 1.0 %copy-done = f32[1,3,8,32,128]{4,3,2,1,0:T(8,128)S(1)} copy-done((f32[1,3,8,32,128]{4,3,2,1,0:T(8,128)S(1)}, f32[1,3,8,32,128]{4,3,2,1,0:T(8,128)}, u32[]{:S(2)}) %copy-start) | copy-done | bytes 393240
  1.6 1.0 %copy-done.2 = f32[1,3,8,32,128]{4,3,2,1,0:T(8,128)S(1)} copy-done((f32[1,3,8,32,128]{4,3,2,1,0:T(8,128)S(1)}, f32[1,3,8,32,128]{4,3,2,1,0:T(8,128)}, u32[]{:S(2)}) %copy-start.2) | copy-done | bytes 393240
  2.6 0.3 edges.1
  3.0 0.7 collective-permute-start.2
  3.6 1.3 %collective-permute-start.3 = (f32[12,8,128]{2,1,0:T(8,128)S(1)}, f32[12,8,128]{2,1,0:T(8,128)S(1)}, u32[]{:S(2)}, u32[]{:S(2)}) collective-permute-start(f32[12,8,128]{2,1,0:T(8,128)S(1)} %get-tuple-element.17.first_ref.refs_9_), channel_id=1, source_target_pairs={{1,0},{3,2},{5,4},{7,6},{9,8},{11,10},{13,12},{15,14},{17,16},{19,... | collective-permute-start | bytes 147464 | tf_op jit(solution)/shard_map/ppermute | solution.py:517
  4.9 1.9 %collective-permute-start.1 = (f32[32,128]{1,0:T(8,128)S(1)}, f32[32,128]{1,0:T(8,128)S(1)}, u32[]{:S(2)}, u32[]{:S(2)}) collective-permute-start(f32[32,128]{1,0:T(8,128)S(1)} %get-tuple-element.14.low_ref.refs_3_), channel_id=1, source_target_pairs={{32,0},{34,2},{36,4},{38,6},{40,8},{42,10},{44,12},{46,14},{48,16}... | collective-permute-start | bytes 49160 | tf_op jit(solution)/shard_map/ppermute | solution.py:513
  6.8 3.4 %collective-permute-start = (f32[32,128]{1,0:T(8,128)S(1)}, f32[32,128]{1,0:T(8,128)S(1)}, u32[]{:S(2)}, u32[]{:S(2)}) collective-permute-start(f32[32,128]{1,0:T(8,128)S(1)} %get-tuple-element.15.high_ref.refs_4_), channel_id=1, source_target_pairs={{0,32},{2,34},{4,36},{6,38},{8,40},{10,42},{12,44},{14,46},{16,48}... | collective-permute-start | bytes 49160 | tf_op jit(solution)/shard_map/ppermute | solution.py:513
  10.2 0.0 collective-permute-done.1.above_ref.refs_4_.refs_6_
  10.2 1.1 %collective-permute-done.below_ref.refs_3_.refs_5_ = f32[32,128]{1,0:T(8,128)S(1)} collective-permute-done((f32[32,128]{1,0:T(8,128)S(1)}, f32[32,128]{1,0:T(8,128)S(1)}, u32[]{:S(2)}, u32[]{:S(2)}) %collective-permute-start) | collective-permute-done | bytes 16416 | tf_op jit(solution)/shard_map/ppermute | solution.py:513
  11.3 0.0 collective-permute-done.2.before_ref.refs_11_
  11.3 12.7 %collective-permute-done.3.after_ref.refs_12_ = f32[12,8,128]{2,1,0:T(8,128)S(1)} collective-permute-done((f32[12,8,128]{2,1,0:T(8,128)S(1)}, f32[12,8,128]{2,1,0:T(8,128)S(1)}, u32[]{:S(2)}, u32[]{:S(2)}) %collective-permute-start.3) | collective-permute-done | bytes 49184 | tf_op jit(solution)/shard_map/ppermute | solution.py:517
  24.1 1.3 %collective-permute-start.6 = (f32[12,8,128]{2,1,0:T(8,128)S(1)}, f32[12,8,128]{2,1,0:T(8,128)S(1)}, u32[]{:S(2)}, u32[]{:S(2)}) collective-permute-start(f32[12,8,128]{2,1,0:T(8,128)S(1)} %get-tuple-element.20), channel_id=1, source_target_pairs={{0,1},{2,3},{4,5},{6,7},{8,9},{10,11},{12,13},{14,15},{16,17},{18,... | collective-permute-start | bytes 147464 | tf_op jit(solution)/shard_map/ppermute | solution.py:517
  25.4 0.7 collective-permute-start.7
  26.1 0.1 pad_add_fusion.place_ref.refs_0_
  26.1 0.6 second.1
  26.8 1.9 %collective-permute-start.4 = (f32[32,128]{1,0:T(8,128)S(1)}, f32[32,128]{1,0:T(8,128)S(1)}, u32[]{:S(2)}, u32[]{:S(2)}) collective-permute-start(f32[32,128]{1,0:T(8,128)S(1)} %get-tuple-element.18), channel_id=1, source_target_pairs={{0,32},{1,33},{2,34},{3,35},{4,36},{5,37},{6,38},{7,39},{8,40},{9,... | collective-permute-start | bytes 49160 | tf_op jit(solution)/shard_map/ppermute | solution.py:513
  28.7 3.4 %collective-permute-start.5 = (f32[32,128]{1,0:T(8,128)S(1)}, f32[32,128]{1,0:T(8,128)S(1)}, u32[]{:S(2)}, u32[]{:S(2)}) collective-permute-start(f32[32,128]{1,0:T(8,128)S(1)} %get-tuple-element.19), channel_id=1, source_target_pairs={{32,0},{33,1},{34,2},{35,3},{36,4},{37,5},{38,6},{39,7},{40,8},{41... | collective-permute-start | bytes 49160 | tf_op jit(solution)/shard_map/ppermute | solution.py:513
  32.1 1.3 %flux.2.refs_5_ = f32[9,8,32,128]{3,2,1,0:T(8,128)S(1)} custom-call(s32[2]{0:T(128)S(1)} %pad_add_fusion.place_ref.refs_0_, f32[1,3,8,32,128]{4,3,2,1,0:T(8,128)S(1)} %copy-done.1, f32[1,3,8,32,128]{4,3,2,1,0:T(8,128)S(1)} %copy-done.3, f32[32,128]{1,0:T(8,128)S(1)} %collective-permute-done.below_ref.refs_3_.refs_5_, ...), custom_call_target="tpu_custom_call" | custom-call | tf_op jit(solution)/shard_map/flux/pallas_call | solution.py:562
  33.5 0.0 copy-start.4
  33.5 0.0 copy-start.5
  33.5 0.0 copy-start.6
  33.5 0.0 copy-start.7
  33.5 0.6 flux.3.refs_19_
  34.1 0.0 copy-done.4
  34.1 0.0 copy-done.5
  34.2 0.0 copy-done.6
  34.2 3.5 %section.1 = (f32[1,3,8,32,128]{4,3,2,1,0:T(8,128)}, f32[1,3,8,32,128]{4,3,2,1,0:T(8,128)}, f32[32,8,128]{2,1,0:T(8,128)S(1)}, f32[9,8,32,128]{3,2,1,0:T(8,128)S(1)}) custom-call(s32[2]{0:T(128)S(1)} %pad_add_fusion.place_ref.refs_0_, f32[1,3,8,32,128]{4,3,2,1,0:T(8,128)S(1)} %copy-done.1, ...), custom_call_target="tpu_custom_call", output_to_operand_aliasing={{3}: (19, {})} | custom-call | tf_op jit(solution)/shard_map/section/pallas_call | solution.py:574
  37.7 31.5 %all_to_all.5.got_ref = f32[32,8,128]{2,1,0:T(8,128)S(1)} all-to-all(f32[32,8,128]{2,1,0:T(8,128)S(1)} %get-tuple-element.24), channel_id=1, replica_groups=mesh['grid'=2,'lat'=8,'lon'=32] {'lon'}, dimensions={0} | all-to-all | bytes 262144 | tf_op jit(solution)/shard_map/all_to_all | solution.py:618
  69.2 0.5 collect.1
  69.7 3.9 %collective-permute-start.8 = (f32[1,1,1,48,128]{4,3,2,1,0:T(8,128)S(1)}, f32[1,1,1,48,128]{4,3,2,1,0:T(8,128)S(1)}, u32[]{:S(2)}, u32[]{:S(2)}) collective-permute-start(f32[1,1,1,48,128]{4,3,2,1,0:T(8,128)S(1)} %collect.1), channel_id=1, source_target_pairs={{0,256},{256,0},{1,257},{257,1},{2,258},{258,2},{3,259},{259,3},{4... | collective-permute-start | bytes 73736 | tf_op jit(solution)/shard_map/ppermute | solution.py:627
  73.6 0.8 %collective-permute-done.8 = f32[1,1,1,48,128]{4,3,2,1,0:T(8,128)S(1)} collective-permute-done((f32[1,1,1,48,128]{4,3,2,1,0:T(8,128)S(1)}, f32[1,1,1,48,128]{4,3,2,1,0:T(8,128)S(1)}, u32[]{:S(2)}, u32[]{:S(2)}) %collective-permute-start.8) | collective-permute-done | bytes 24608 | tf_op jit(solution)/shard_map/ppermute | solution.py:627
  74.4 0.6 copy.14
  (12 shorter events, 0.0 us)
Async XLA Ops:
  0.6 1.0 %copy-start = (f32[1,3,8,32,128]{4,3,2,1,0:T(8,128)S(1)}, f32[1,3,8,32,128]{4,3,2,1,0:T(8,128)}, u32[]{:S(2)}) copy-start(f32[1,3,8,32,128]{4,3,2,1,0:T(8,128)} %refs_1_.5) | copy-start | bytes 1179652
  1.6 1.0 %copy-start.2 = (f32[1,3,8,32,128]{4,3,2,1,0:T(8,128)S(1)}, f32[1,3,8,32,128]{4,3,2,1,0:T(8,128)}, u32[]{:S(2)}) copy-start(f32[1,3,8,32,128]{4,3,2,1,0:T(8,128)} %refs_2_.5) | copy-start | bytes 1179652
  2.6 29.5 %copy-start.1 = (f32[1,3,8,32,128]{4,3,2,1,0:T(8,128)S(1)}, f32[1,3,8,32,128]{4,3,2,1,0:T(8,128)}, u32[]{:S(2)}) copy-start(f32[1,3,8,32,128]{4,3,2,1,0:T(8,128)} %refs_1_.5) | copy-start | bytes 1179652
  2.6 29.5 %copy-start.3 = (f32[1,3,8,32,128]{4,3,2,1,0:T(8,128)S(1)}, f32[1,3,8,32,128]{4,3,2,1,0:T(8,128)}, u32[]{:S(2)}) copy-start(f32[1,3,8,32,128]{4,3,2,1,0:T(8,128)} %refs_2_.5) | copy-start | bytes 1179652
  3.0 8.4 %collective-permute-start.2 = (f32[12,8,128]{2,1,0:T(8,128)S(1)}, f32[12,8,128]{2,1,0:T(8,128)S(1)}, u32[]{:S(2)}, u32[]{:S(2)}) collective-permute-start(f32[12,8,128]{2,1,0:T(8,128)S(1)} %get-tuple-element.16.last_ref.refs_10_), channel_id=1, source_target_pairs={{1,2},{3,4},{5,6},{7,8},{9,10},{11,12},{13,14},{15,16},{17,18},{19... | collective-permute-start | bytes 147464 | tf_op jit(solution)/shard_map/ppermute | solution.py:517
  3.6 20.5 %collective-permute-start.3 = (f32[12,8,128]{2,1,0:T(8,128)S(1)}, f32[12,8,128]{2,1,0:T(8,128)S(1)}, u32[]{:S(2)}, u32[]{:S(2)}) collective-permute-start(f32[12,8,128]{2,1,0:T(8,128)S(1)} %get-tuple-element.17.first_ref.refs_9_), channel_id=1, source_target_pairs={{1,0},{3,2},{5,4},{7,6},{9,8},{11,10},{13,12},{15,14},{17,16},{19,... | collective-permute-start | bytes 147464 | tf_op jit(solution)/shard_map/ppermute | solution.py:517
  4.9 5.3 %collective-permute-start.1 = (f32[32,128]{1,0:T(8,128)S(1)}, f32[32,128]{1,0:T(8,128)S(1)}, u32[]{:S(2)}, u32[]{:S(2)}) collective-permute-start(f32[32,128]{1,0:T(8,128)S(1)} %get-tuple-element.14.low_ref.refs_3_), channel_id=1, source_target_pairs={{32,0},{34,2},{36,4},{38,6},{40,8},{42,10},{44,12},{46,14},{48,16}... | collective-permute-start | bytes 49160 | tf_op jit(solution)/shard_map/ppermute | solution.py:513
  6.8 4.5 %collective-permute-start = (f32[32,128]{1,0:T(8,128)S(1)}, f32[32,128]{1,0:T(8,128)S(1)}, u32[]{:S(2)}, u32[]{:S(2)}) collective-permute-start(f32[32,128]{1,0:T(8,128)S(1)} %get-tuple-element.15.high_ref.refs_4_), channel_id=1, source_target_pairs={{0,32},{2,34},{4,36},{6,38},{8,40},{10,42},{12,44},{14,46},{16,48}... | collective-permute-start | bytes 49160 | tf_op jit(solution)/shard_map/ppermute | solution.py:513
  24.1 10.0 %collective-permute-start.6 = (f32[12,8,128]{2,1,0:T(8,128)S(1)}, f32[12,8,128]{2,1,0:T(8,128)S(1)}, u32[]{:S(2)}, u32[]{:S(2)}) collective-permute-start(f32[12,8,128]{2,1,0:T(8,128)S(1)} %get-tuple-element.20), channel_id=1, source_target_pairs={{0,1},{2,3},{4,5},{6,7},{8,9},{10,11},{12,13},{14,15},{16,17},{18,... | collective-permute-start | bytes 147464 | tf_op jit(solution)/shard_map/ppermute | solution.py:517
  25.4 8.7 %collective-permute-start.7 = (f32[12,8,128]{2,1,0:T(8,128)S(1)}, f32[12,8,128]{2,1,0:T(8,128)S(1)}, u32[]{:S(2)}, u32[]{:S(2)}) collective-permute-start(f32[12,8,128]{2,1,0:T(8,128)S(1)} %get-tuple-element.21), channel_id=1, source_target_pairs={{2,1},{4,3},{6,5},{8,7},{10,9},{12,11},{14,13},{16,15},{18,17},{20... | collective-permute-start | bytes 147464 | tf_op jit(solution)/shard_map/ppermute | solution.py:517
  26.8 6.7 %collective-permute-start.4 = (f32[32,128]{1,0:T(8,128)S(1)}, f32[32,128]{1,0:T(8,128)S(1)}, u32[]{:S(2)}, u32[]{:S(2)}) collective-permute-start(f32[32,128]{1,0:T(8,128)S(1)} %get-tuple-element.18), channel_id=1, source_target_pairs={{0,32},{1,33},{2,34},{3,35},{4,36},{5,37},{6,38},{7,39},{8,40},{9,... | collective-permute-start | bytes 49160 | tf_op jit(solution)/shard_map/ppermute | solution.py:513
  28.7 4.8 %collective-permute-start.5 = (f32[32,128]{1,0:T(8,128)S(1)}, f32[32,128]{1,0:T(8,128)S(1)}, u32[]{:S(2)}, u32[]{:S(2)}) collective-permute-start(f32[32,128]{1,0:T(8,128)S(1)} %get-tuple-element.19), channel_id=1, source_target_pairs={{32,0},{33,1},{34,2},{35,3},{36,4},{37,5},{38,6},{39,7},{40,8},{41... | collective-permute-start | bytes 49160 | tf_op jit(solution)/shard_map/ppermute | solution.py:513
  33.5 0.7 copy-start.4
  33.5 0.7 copy-start.5
  33.5 0.7 copy-start.6
  33.5 0.7 copy-start.7
  69.7 4.7 %collective-permute-start.8 = (f32[1,1,1,48,128]{4,3,2,1,0:T(8,128)S(1)}, f32[1,1,1,48,128]{4,3,2,1,0:T(8,128)S(1)}, u32[]{:S(2)}, u32[]{:S(2)}) collective-permute-start(f32[1,1,1,48,128]{4,3,2,1,0:T(8,128)S(1)} %collect.1), channel_id=1, source_target_pairs={{0,256},{256,0},{1,257},{257,1},{2,258},{258,2},{3,259},{259,3},{4... | collective-permute-start | bytes 73736 | tf_op jit(solution)/shard_map/ppermute | solution.py:627

commit v4 on v3

--- a/solution.py
+++ b/solution.py
@@ -57,8 +57,6 @@
             last_ref[6 + comp] = ref[0, index, :, CELLS_P - 2, :]
     low_ref[...] = low
     high_ref[...] = pltpu.roll(high, 2, 1)
-    first_ref[11] = jnp.zeros((LEVELS, CELLS_T), F32)
-    last_ref[11] = jnp.zeros((LEVELS, CELLS_T), F32)
 
 
 def corners_kernel(
@@ -68,17 +66,19 @@
     for row, source, target in ((0, first_ref, first_out_ref), (CELLS_P - 1, last_ref, last_out_ref)):
         below = jnp.broadcast_to(below_ref[row : row + 1, :], shape)
         above = jnp.broadcast_to(above_ref[row : row + 1, :], shape)
-        target[0:11] = source[0:11]
+        target[0:11] = source[...]
         target[11] = jnp.where(rows_of(shape) == 0, below, above)
 
 
-def second_kernel(place_ref, before_ref, after_ref, low_ref, high_ref, low_out_ref, high_out_ref):
-    @pl.when(place_ref[1] % 2 == 1)
+def second_kernel(before_ref, after_ref, low_ref, high_ref, low_out_ref, high_out_ref):
+    odd = lax.axis_index("lon") % 2
+
+    @pl.when(odd == 1)
     def _():
         low_out_ref[...] = low_ref[...]
         high_out_ref[...] = high_ref[...]
 
-    @pl.when(place_ref[1] % 2 == 0)
+    @pl.when(odd == 0)
     def _():
         lane = lanes_of((LEVELS, CELLS_T))
         low = jnp.zeros((LEVELS, CELLS_T), F32)
@@ -162,15 +162,15 @@
     return (up - down) * step
 
 
-def flux_kernel(steps, parity, place_ref, vel_ref, mag_ref, below_ref, above_ref, *rest):
+def flux_kernel(steps, parity, vel_ref, mag_ref, below_ref, above_ref, *rest):
     flux_ref = rest[-1]
     wide = (CELLS_P, CELLS_T)
 
-    @pl.when(place_ref[1] % 2 == parity)
+    @pl.when(lax.axis_index("lon") % 2 == parity)
     def _():
         is_below = lanes_of(wide) % 2 == 1
         beside = jnp.where(is_below, below_ref[...], above_ref[...])
-        own_sine = inverse_sine(place_ref[0] * CELLS_T + lanes_of((8, CELLS_T)), steps[1])
+        own_sine = inverse_sine(lax.axis_index("lat") * CELLS_T + lanes_of((8, CELLS_T)), steps[1])
 
         def make_flux(level, carry):
             low_level, high_level, step_r, step_t, step_p = level_steps(level, own_sine, steps, 1.0)
@@ -196,7 +196,6 @@
     steps,
     lat_blocks,
     lon_blocks,
-    place_ref,
     vel_ref,
     mag_ref,
     low_ref,
@@ -216,21 +215,18 @@
     weight_ref,
     slot_ref,
     flux_in_ref,
-    out_vel_ref,
-    out_mag_ref,
+    new_vel_ref,
+    new_mag_ref,
     send_ref,
     flux_ref,
     edge_t_ref,
     edge_p_ref,
     taken_ref,
     side_ref,
-    new_vel_ref,
-    new_mag_ref,
-    sem_ref,
 ):
     spacing, theta_step, phi_step = steps
-    lat = place_ref[0]
-    lon = place_ref[1]
+    lat = lax.axis_index("lat")
+    lon = lax.axis_index("lon")
     odd_block = lon % 2 == 1
     time_step = courant * spacing
     wide = (CELLS_P, CELLS_T)
@@ -250,8 +246,9 @@
 
     @pl.when(jnp.logical_not(odd_block))
     def _():
-        side_ref[0] = before_even_ref[...]
-        side_ref[1] = after_even_ref[...]
+        side_ref[0, 0:11] = before_even_ref[...]
+        side_ref[1, 0:11] = after_even_ref[...]
+        side_ref[:, 11] = jnp.zeros((2, LEVELS, CELLS_T), F32)
 
     is_below = lane % 2 == 1
     level_of = (lane % 16) // 2
@@ -379,15 +376,7 @@
         new_mag_ref[0, 0, level] = mag_ref[0, 0, level] + (d_t(8) - d_p(7))
         new_mag_ref[0, 1, level] = mag_ref[0, 1, level] + (d_p(6) - d_r(8))
         new_mag_ref[0, 2, level] = mag_ref[0, 2, level] + (d_r(7) - d_t(6))
-        for copy in out_copies(level):
-            copy.start()
         return carry
-
-    def out_copies(level):
-        return [
-            pltpu.make_async_copy(new.at[0, :, level], out.at[0, :, level], sem_ref.at[which, level])
-            for which, new, out in ((0, new_vel_ref, out_vel_ref), (1, new_mag_ref, out_mag_ref))
-        ]
 
     lax.fori_loop(0, LEVELS, advance, 0, unroll=8)
 
@@ -454,34 +443,43 @@
         for block in range(8):
             send_ref[chunk * 8 + block] = turned[16 * block : 16 * block + 8]
 
-    def finish(level, carry):
-        for copy in out_copies(level):
-            copy.wait()
-        return carry
-
-    lax.fori_loop(0, LEVELS, finish, 0)
-
-
-def collect_kernel(got_ref, out_ref):
-    rows = got_ref.shape[0] * got_ref.shape[1]
-    got = got_ref[...].reshape(rows, CELLS_T)
-    total = jnp.zeros((48, CYCLE), F32)
-    for start in (0, 64):
-        slot = got[:, start + 48 : start + 49].astype(jnp.int32)
-        onehot = (slot == lanes_of((rows, CYCLE))).astype(F32)
-        part = lax.dot_general(
-            got,
-            onehot,
-            (((0,), (0,)), ((), ())),
-            precision=lax.Precision.HIGHEST,
-            preferred_element_type=F32,
-        )
-        total = total + part[start : start + 48]
-    out_ref[0, 0, 0] = total
+
+def store_kernel(vel_ref, mag_ref, out_vel_ref, out_mag_ref, sem_ref):
+    copies = [
+        pltpu.make_async_copy(vel_ref, out_vel_ref, sem_ref.at[0]),
+        pltpu.make_async_copy(mag_ref, out_mag_ref, sem_ref.at[1]),
+    ]
+    for copy in copies:
+        copy.start()
+    for copy in copies:
+        copy.wait()
+
+
+def collect_kernel(got_ref, near_ref, far_ref):
+    sources = got_ref.shape[0]
+    rows = sources * 8
+    totals = []
+    for half in range(2):
+        got = got_ref[:, 8 * half : 8 * half + 8].reshape(rows, CELLS_T)
+        total = jnp.zeros((48, CYCLE), F32)
+        for start in (0, 64):
+            slot = got[:, start + 48 : start + 49].astype(jnp.int32)
+            onehot = (slot == lanes_of((rows, CYCLE))).astype(F32)
+            part = lax.dot_general(
+                got,
+                onehot,
+                (((0,), (0,)), ((), ())),
+                precision=lax.Precision.HIGHEST,
+                preferred_element_type=F32,
+            )
+            total = total + part[start : start + 48]
+        totals.append(total)
+    odd = lax.axis_index("lon") % 2 == 1
+    near_ref[0, 0, 0] = jnp.where(odd, totals[1], totals[0])
+    far_ref[0, 0, 0] = jnp.where(odd, totals[0], totals[1])
 
 
 VMEM = pl.BlockSpec(memory_space=pltpu.VMEM)
-SMEM = pl.BlockSpec(memory_space=pltpu.SMEM)
 HBM = pl.BlockSpec(memory_space=pltpu.HBM)
 
 
@@ -498,9 +496,9 @@
     theta_step = 0.5 * math.pi / (lat_blocks * CELLS_T)
     phi_step = 1.5 * math.pi / (lon_blocks * CELLS_P)
     spacing = inner_radius * theta_step
-    place = jnp.stack([lax.axis_index("lat"), lax.axis_index("lon")]).astype(jnp.int32)
     pack = tiles(CELLS_P, CELLS_T)
-    strip = tiles(12, LEVELS, CELLS_T)
+    strip = tiles(11, LEVELS, CELLS_T)
+    strip_full = tiles(12, LEVELS, CELLS_T)
     evens, odds = range(0, lon_blocks, 2), range(1, lon_blocks, 2)
 
     def along_lat(block, step, lons):
@@ -532,7 +530,7 @@
         corners_kernel,
         in_specs=[VMEM] * 6,
         out_specs=[VMEM] * 2,
-        out_shape=[strip, strip],
+        out_shape=[strip_full, strip_full],
         compiler_params=limit(4),
         name="corners",
     )(below_even, above_even, first, last, before_even, after_even)
@@ -540,12 +538,12 @@
     after_odd = along_lon(first_full, -1, evens)
     second_low, second_high = pl.pallas_call(
         second_kernel,
-        in_specs=[SMEM] + [VMEM] * 4,
+        in_specs=[VMEM] * 4,
         out_specs=[VMEM] * 2,
         out_shape=[pack, pack],
         compiler_params=limit(4),
         name="second",
-    )(place, before_even, after_even, low, high)
+    )(before_even, after_even, low, high)
     every = range(lon_blocks)
     below_odd = along_lat(second_high, 1, every)
     above_odd = along_lat(second_low, -1, every)
@@ -561,40 +559,36 @@
 
         return pl.pallas_call(
             kernel,
-            in_specs=[SMEM] + [VMEM] * (4 + len(given)),
+            in_specs=[VMEM] * (4 + len(given)),
             out_specs=VMEM,
             out_shape=tiles(9, LEVELS, CELLS_P, CELLS_T),
-            input_output_aliases={5: 0} if given else {},
+            input_output_aliases={4: 0} if given else {},
             compiler_params=limit(8),
             name="flux",
-        )(place, velocity, magnetic, below, above, *given)
+        )(velocity, magnetic, below, above, *given)
 
     flux = flux_of_cells(0, below_even, above_even)
     flux = flux_of_cells(1, below_odd, above_odd, flux)
     new_velocity, new_magnetic, payload, _ = pl.pallas_call(
         section,
-        in_specs=[SMEM] + [VMEM] * 19,
-        out_specs=[HBM] * 2 + [VMEM, VMEM],
+        in_specs=[VMEM] * 19,
+        out_specs=[VMEM] * 4,
         out_shape=[
             tiles(*velocity.shape),
             tiles(*magnetic.shape),
             tiles(lon_blocks, 8, CELLS_T),
             tiles(9, LEVELS, CELLS_P, CELLS_T),
         ],
-        input_output_aliases={19: 3},
+        input_output_aliases={18: 3},
         scratch_shapes=[
             pltpu.VMEM((5, CELLS_P, CELLS_T), F32),
             pltpu.VMEM((2, 5, LEVELS, CELLS_T), F32),
             pltpu.VMEM((8, LEVELS, slots_total), F32),
             pltpu.VMEM((2, 12, LEVELS, CELLS_T), F32),
-            pltpu.VMEM(velocity.shape, F32),
-            pltpu.VMEM(magnetic.shape, F32),
-            pltpu.SemaphoreType.DMA((2, LEVELS)),
         ],
         compiler_params=limit(16),
         name="section",
     )(
-        place,
         velocity,
         magnetic,
         low,
@@ -615,16 +609,41 @@
         cycle_slot,
         flux,
     )
-    payload = lax.all_to_all(payload, "lon", split_axis=0, concat_axis=0, tiled=True)
-    cycle = pl.pallas_call(
+    new_velocity, new_magnetic = pl.pallas_call(
+        store_kernel,
+        in_specs=[VMEM] * 2,
+        out_specs=[HBM] * 2,
+        out_shape=[tiles(*velocity.shape), tiles(*magnetic.shape)],
+        scratch_shapes=[pltpu.SemaphoreType.DMA((2,))],
+        compiler_params=limit(4),
+        name="store",
+    )(new_velocity, new_magnetic)
+    pairs = lon_blocks // 2
+    groups = [[2 * pair + parity for pair in range(pairs)] for parity in range(2)]
+    payload = lax.all_to_all(
+        payload.reshape(pairs, 16, CELLS_T),
+        "lon",
+        split_axis=0,
+        concat_axis=0,
+        axis_index_groups=groups,
+        tiled=True,
+    )
+    near, far = pl.pallas_call(
         collect_kernel,
         in_specs=[VMEM],
-        out_specs=VMEM,
-        out_shape=tiles(1, 1, 1, 48, CYCLE),
+        out_specs=[VMEM] * 2,
+        out_shape=[tiles(1, 1, 1, 48, CYCLE)] * 2,
         compiler_params=limit(4),
         name="collect",
     )(payload)
-    cycle = lax.ppermute(cycle, "grid", [(0, 1), (1, 0)])
+    across = [
+        (grid * lon_blocks + lon, (1 - grid) * lon_blocks + (lon ^ 1))
+        for grid in range(2)
+        for lon in range(lon_blocks)
+    ]
+    far = lax.ppermute(far, ("grid", "lon"), across)
+    near = lax.ppermute(near, "grid", [(0, 1), (1, 0)])
+    cycle = far + near
     return (new_velocity, new_magnetic, cycle)
 
 

time: 75.4 us -> 69.5 us (0.922)
  the two profiles are of different devices: /device:TPU:193 before, /device:TPU:96 now
where the time goes in v4:
time: 69.5 us; the launch traced here: 69 us
  starting transfers between devices  25.5 us (37%)
  waiting for transfers between devices  20.1 us (29%)
  blocking collectives  15.1 us (22%)
  Pallas kernels  4.94 us (7%)
  local copies, waits for them, and re-layouts  2.02 us (3%)
  between operations  0.85 us (1%)
    ppermute x4, starting transfers between devices, along_lat(): return lax.ppermute(block, ('lat', 'lon'), pairs)  16.2 us
    all_to_all x1, blocking collectives, local(): lax.all_to_all(payload.reshape(pairs, 16, CELLS_T), 'lon', split_axis=0,...  15.1 us
    ppermute x1, waiting for transfers between devices, local(): far = lax.ppermute(far, ('grid', 'lon'), across)  8.1 us
    ppermute x4, waiting for transfers between devices, along_lon(): return lax.ppermute(block, 'lon', pairs)  6.51 us
    ppermute x4, waiting for transfers between devices, along_lat(): return lax.ppermute(block, ('lat', 'lon'), pairs)  5.44 us
    ppermute x4, starting transfers between devices, along_lon(): return lax.ppermute(block, 'lon', pairs)  4.21 us
    ppermute x1, starting transfers between devices, local(): near = lax.ppermute(near, 'grid', [(0, 1), (1, 0)])  3.08 us
    pallas_call x1, Pallas kernels, local(): pl.pallas_call(section, in_specs=[VMEM] * 19, out_specs=[VMEM] * 4, out_s...  2.34 us
  transfers between devices with their start and end apart: 10, of which 4 were waited for; matrix products, arithmetic and copies ran while one was open for 0% of the time, Pallas kernels for 3%

profile of v4, /device:TPU:96, one launch (start us, length us, event | category | flops | bytes accessed | tf_op | source)
XLA Modules:
  0.0 69.0 jit_solution(11425972037717840212)
XLA Ops:
  0.6 1.0 %copy-done = f32[1,3,8,32,128]{4,3,2,1,0:T(8,128)S(1)} copy-done((f32[1,3,8,32,128]{4,3,2,1,0:T(8,128)S(1)}, f32[1,3,8,32,128]{4,3,2,1,0:T(8,128)}, u32[]{:S(2)}) %copy-start) | copy-done | bytes 393240
  1.6 1.0 %copy-done.2 = f32[1,3,8,32,128]{4,3,2,1,0:T(8,128)S(1)} copy-done((f32[1,3,8,32,128]{4,3,2,1,0:T(8,128)S(1)}, f32[1,3,8,32,128]{4,3,2,1,0:T(8,128)}, u32[]{:S(2)}) %copy-start.2) | copy-done | bytes 393240
  2.6 0.3 edges.1
  3.0 0.7 collective-permute-start.2
  3.6 1.3 %collective-permute-start.3 = (f32[11,8,128]{2,1,0:T(8,128)S(1)}, f32[11,8,128]{2,1,0:T(8,128)S(1)}, u32[]{:S(2)}, u32[]{:S(2)}) collective-permute-start(f32[11,8,128]{2,1,0:T(8,128)S(1)} %get-tuple-element.21.first_ref.refs_8_), channel_id=1, source_target_pairs={{1,0},{3,2},{5,4},{7,6},{9,8},{11,10},{13,12},{15,14},{17,16},{19,... | collective-permute-start | bytes 135176 | tf_op jit(solution)/shard_map/ppermute | solution.py:515
  4.9 2.0 %collective-permute-start.1 = (f32[32,128]{1,0:T(8,128)S(1)}, f32[32,128]{1,0:T(8,128)S(1)}, u32[]{:S(2)}, u32[]{:S(2)}) collective-permute-start(f32[32,128]{1,0:T(8,128)S(1)} %get-tuple-element.18.low_ref.refs_2_), channel_id=1, source_target_pairs={{32,0},{34,2},{36,4},{38,6},{40,8},{42,10},{44,12},{46,14},{48,16}... | collective-permute-start | bytes 49160 | tf_op jit(solution)/shard_map/ppermute | solution.py:511
  6.9 5.0 %collective-permute-start = (f32[32,128]{1,0:T(8,128)S(1)}, f32[32,128]{1,0:T(8,128)S(1)}, u32[]{:S(2)}, u32[]{:S(2)}) collective-permute-start(f32[32,128]{1,0:T(8,128)S(1)} %get-tuple-element.19.high_ref.refs_3_), channel_id=1, source_target_pairs={{0,32},{2,34},{4,36},{6,38},{8,40},{10,42},{12,44},{14,46},{16,48}... | collective-permute-start | bytes 49160 | tf_op jit(solution)/shard_map/ppermute | solution.py:511
  12.0 0.0 collective-permute-done.1.above_ref.refs_3_.refs_5_
  12.0 1.4 %collective-permute-done.below_ref.refs_2_.refs_4_ = f32[32,128]{1,0:T(8,128)S(1)} collective-permute-done((f32[32,128]{1,0:T(8,128)S(1)}, f32[32,128]{1,0:T(8,128)S(1)}, u32[]{:S(2)}, u32[]{:S(2)}) %collective-permute-start) | collective-permute-done | bytes 16416 | tf_op jit(solution)/shard_map/ppermute | solution.py:511
  13.4 0.0 collective-permute-done.2.before_ref.refs_10_
  13.4 6.5 %collective-permute-done.3.after_ref.refs_11_ = f32[11,8,128]{2,1,0:T(8,128)S(1)} collective-permute-done((f32[11,8,128]{2,1,0:T(8,128)S(1)}, f32[11,8,128]{2,1,0:T(8,128)S(1)}, u32[]{:S(2)}, u32[]{:S(2)}) %collective-permute-start.3) | collective-permute-done | bytes 45088 | tf_op jit(solution)/shard_map/ppermute | solution.py:515
  19.9 1.6 %collective-permute-start.6 = (f32[12,8,128]{2,1,0:T(8,128)S(1)}, f32[12,8,128]{2,1,0:T(8,128)S(1)}, u32[]{:S(2)}, u32[]{:S(2)}) collective-permute-start(f32[12,8,128]{2,1,0:T(8,128)S(1)} %get-tuple-element.24), channel_id=1, source_target_pairs={{0,1},{2,3},{4,5},{6,7},{8,9},{10,11},{12,13},{14,15},{16,17},{18,... | collective-permute-start | bytes 147464 | tf_op jit(solution)/shard_map/ppermute | solution.py:515
  21.5 0.7 collective-permute-start.7
  22.2 0.1 second.1
  22.3 7.3 %collective-permute-start.4 = (f32[32,128]{1,0:T(8,128)S(1)}, f32[32,128]{1,0:T(8,128)S(1)}, u32[]{:S(2)}, u32[]{:S(2)}) collective-permute-start(f32[32,128]{1,0:T(8,128)S(1)} %get-tuple-element.22), channel_id=1, source_target_pairs={{0,32},{1,33},{2,34},{3,35},{4,36},{5,37},{6,38},{7,39},{8,40},{9,... | collective-permute-start | bytes 49160 | tf_op jit(solution)/shard_map/ppermute | solution.py:511
  29.6 1.9 %collective-permute-start.5 = (f32[32,128]{1,0:T(8,128)S(1)}, f32[32,128]{1,0:T(8,128)S(1)}, u32[]{:S(2)}, u32[]{:S(2)}) collective-permute-start(f32[32,128]{1,0:T(8,128)S(1)} %get-tuple-element.23), channel_id=1, source_target_pairs={{32,0},{33,1},{34,2},{35,3},{36,4},{37,5},{38,6},{39,7},{40,8},{41... | collective-permute-start | bytes 49160 | tf_op jit(solution)/shard_map/ppermute | solution.py:511
  31.5 0.8 %flux.2.refs_4_ = f32[9,8,32,128]{3,2,1,0:T(8,128)S(1)} custom-call(f32[1,3,8,32,128]{4,3,2,1,0:T(8,128)S(1)} %copy-done.1, f32[1,3,8,32,128]{4,3,2,1,0:T(8,128)S(1)} %copy-done.3, f32[32,128]{1,0:T(8,128)S(1)} %collective-permute-done.below_ref.refs_2_.refs_4_, f32[32,128]{1,0:T(8,128)S(1)} %collective-permute-done.1.above_ref.refs_3_.refs_5_), custom_call_target="tpu_custom_call" | custom-call | tf_op jit(solution)/shard_map/flux/pallas_call | solution.py:560
  32.3 0.0 copy-start.4
  32.4 0.0 copy-start.5
  32.4 0.0 copy-start.6
  32.4 0.0 copy-start.7
  32.4 0.0 collective-permute-done.4.refs_2_.refs_6_
  32.4 4.0 %collective-permute-done.5.refs_3_.refs_7_ = f32[32,128]{1,0:T(8,128)S(1)} collective-permute-done((f32[32,128]{1,0:T(8,128)S(1)}, f32[32,128]{1,0:T(8,128)S(1)}, u32[]{:S(2)}, u32[]{:S(2)}) %collective-permute-start.5) | collective-permute-done | bytes 16416 | tf_op jit(solution)/shard_map/ppermute | solution.py:511
  36.4 0.0 collective-permute-done.6.refs_12_
  36.5 2.3 %section.1 = (f32[1,3,8,32,128]{4,3,2,1,0:T(8,128)S(1)}, f32[1,3,8,32,128]{4,3,2,1,0:T(8,128)S(1)}, f32[32,8,128]{2,1,0:T(8,128)S(1)}, f32[9,8,32,128]{3,2,1,0:T(8,128)S(1)}) custom-call(f32[1,3,8,32,128]{4,3,2,1,0:T(8,128)S(1)} %copy-done.1, f32[1,3,8,32,128]{4,3,2,1,0:T(8,128)S(1)} %copy-done.3, ...), custom_call_target="tpu_custom_call", output_to_operand_aliasing={{3}: (18, {})} | custom-call | tf_op jit(solution)/shard_map/section/pallas_call | solution.py:572
  38.8 15.1 %all_to_all.5.got_ref = f32[16,16,128]{2,1,0:T(8,128)S(1)} all-to-all(f32[16,16,128]{2,1,0:T(8,128)S(1)} %bitcast.1), channel_id=1, replica_groups={{0,2,4,6,8,10,12,14,16,18,20,22,24,26,28,30},{1,3,5,7,9,11,13,15,17,19,..., dimensions={0} | all-to-all | bytes 262144 | tf_op jit(solution)/shard_map/all_to_all | solution.py:623
  53.9 0.5 collect.1
  54.4 1.9 %collective-permute-start.8 = (f32[1,1,1,48,128]{4,3,2,1,0:T(8,128)S(1)}, f32[1,1,1,48,128]{4,3,2,1,0:T(8,128)S(1)}, u32[]{:S(2)}, u32[]{:S(2)}) collective-permute-start(f32[1,1,1,48,128]{4,3,2,1,0:T(8,128)S(1)} %get-tuple-element.31), channel_id=1, source_target_pairs={{0,257},{1,256},{2,259},{3,258},{4,261},{5,260},{6,263},{7,262},{8... | collective-permute-start | bytes 73736 | tf_op jit(solution)/shard_map/ppermute | solution.py:644
  56.3 3.1 %collective-permute-start.9 = (f32[1,1,1,48,128]{4,3,2,1,0:T(8,128)S(1)}, f32[1,1,1,48,128]{4,3,2,1,0:T(8,128)S(1)}, u32[]{:S(2)}, u32[]{:S(2)}) collective-permute-start(f32[1,1,1,48,128]{4,3,2,1,0:T(8,128)S(1)} %get-tuple-element.32), channel_id=1, source_target_pairs={{0,256},{256,0},{1,257},{257,1},{2,258},{258,2},{3,259},{259,3},{4... | collective-permute-start | bytes 73736 | tf_op jit(solution)/shard_map/ppermute | solution.py:645
  59.4 0.9 %store.1 = (f32[1,3,8,32,128]{4,3,2,1,0:T(8,128)}, f32[1,3,8,32,128]{4,3,2,1,0:T(8,128)}) custom-call(f32[1,3,8,32,128]{4,3,2,1,0:T(8,128)S(1)} %get-tuple-element.26.vel_ref, f32[1,3,8,32,128]{4,3,2,1,0:T(8,128)S(1)} %get-tuple-element.27.mag_ref), custom_call_target="tpu_custom_call" | custom-call | tf_op jit(solution)/shard_map/store/pallas_call | solution.py:612
  60.3 8.1 %collective-permute-done.8 = f32[1,1,1,48,128]{4,3,2,1,0:T(8,128)S(1)} collective-permute-done((f32[1,1,1,48,128]{4,3,2,1,0:T(8,128)S(1)}, f32[1,1,1,48,128]{4,3,2,1,0:T(8,128)S(1)}, u32[]{:S(2)}, u32[]{:S(2)}) %collective-permute-start.8) | collective-permute-done | bytes 24608 | tf_op jit(solution)/shard_map/ppermute | solution.py:644
  68.4 0.6 add.3
  (14 shorter events, 0.0 us)
Async XLA Ops:
  0.6 1.0 %copy-start = (f32[1,3,8,32,128]{4,3,2,1,0:T(8,128)S(1)}, f32[1,3,8,32,128]{4,3,2,1,0:T(8,128)}, u32[]{:S(2)}) copy-start(f32[1,3,8,32,128]{4,3,2,1,0:T(8,128)} %refs_0_.5) | copy-start | bytes 1179652
  1.6 1.0 %copy-start.2 = (f32[1,3,8,32,128]{4,3,2,1,0:T(8,128)S(1)}, f32[1,3,8,32,128]{4,3,2,1,0:T(8,128)}, u32[]{:S(2)}) copy-start(f32[1,3,8,32,128]{4,3,2,1,0:T(8,128)} %refs_1_.5) | copy-start | bytes 1179652
  2.6 28.9 %copy-start.1 = (f32[1,3,8,32,128]{4,3,2,1,0:T(8,128)S(1)}, f32[1,3,8,32,128]{4,3,2,1,0:T(8,128)}, u32[]{:S(2)}) copy-start(f32[1,3,8,32,128]{4,3,2,1,0:T(8,128)} %refs_0_.5) | copy-start | bytes 1179652
  2.6 28.9 %copy-start.3 = (f32[1,3,8,32,128]{4,3,2,1,0:T(8,128)S(1)}, f32[1,3,8,32,128]{4,3,2,1,0:T(8,128)}, u32[]{:S(2)}) copy-start(f32[1,3,8,32,128]{4,3,2,1,0:T(8,128)} %refs_1_.5) | copy-start | bytes 1179652
  3.0 10.5 %collective-permute-start.2 = (f32[11,8,128]{2,1,0:T(8,128)S(1)}, f32[11,8,128]{2,1,0:T(8,128)S(1)}, u32[]{:S(2)}, u32[]{:S(2)}) collective-permute-start(f32[11,8,128]{2,1,0:T(8,128)S(1)} %get-tuple-element.20.last_ref.refs_9_), channel_id=1, source_target_pairs={{1,2},{3,4},{5,6},{7,8},{9,10},{11,12},{13,14},{15,16},{17,18},{19... | collective-permute-start | bytes 135176 | tf_op jit(solution)/shard_map/ppermute | solution.py:515
  3.6 16.3 %collective-permute-start.3 = (f32[11,8,128]{2,1,0:T(8,128)S(1)}, f32[11,8,128]{2,1,0:T(8,128)S(1)}, u32[]{:S(2)}, u32[]{:S(2)}) collective-permute-start(f32[11,8,128]{2,1,0:T(8,128)S(1)} %get-tuple-element.21.first_ref.refs_8_), channel_id=1, source_target_pairs={{1,0},{3,2},{5,4},{7,6},{9,8},{11,10},{13,12},{15,14},{17,16},{19,... | collective-permute-start | bytes 135176 | tf_op jit(solution)/shard_map/ppermute | solution.py:515
  4.9 7.1 %collective-permute-start.1 = (f32[32,128]{1,0:T(8,128)S(1)}, f32[32,128]{1,0:T(8,128)S(1)}, u32[]{:S(2)}, u32[]{:S(2)}) collective-permute-start(f32[32,128]{1,0:T(8,128)S(1)} %get-tuple-element.18.low_ref.refs_2_), channel_id=1, source_target_pairs={{32,0},{34,2},{36,4},{38,6},{40,8},{42,10},{44,12},{46,14},{48,16}... | collective-permute-start | bytes 49160 | tf_op jit(solution)/shard_map/ppermute | solution.py:511
  6.9 6.5 %collective-permute-start = (f32[32,128]{1,0:T(8,128)S(1)}, f32[32,128]{1,0:T(8,128)S(1)}, u32[]{:S(2)}, u32[]{:S(2)}) collective-permute-start(f32[32,128]{1,0:T(8,128)S(1)} %get-tuple-element.19.high_ref.refs_3_), channel_id=1, source_target_pairs={{0,32},{2,34},{4,36},{6,38},{8,40},{10,42},{12,44},{14,46},{16,48}... | collective-permute-start | bytes 49160 | tf_op jit(solution)/shard_map/ppermute | solution.py:511
  19.9 16.5 %collective-permute-start.6 = (f32[12,8,128]{2,1,0:T(8,128)S(1)}, f32[12,8,128]{2,1,0:T(8,128)S(1)}, u32[]{:S(2)}, u32[]{:S(2)}) collective-permute-start(f32[12,8,128]{2,1,0:T(8,128)S(1)} %get-tuple-element.24), channel_id=1, source_target_pairs={{0,1},{2,3},{4,5},{6,7},{8,9},{10,11},{12,13},{14,15},{16,17},{18,... | collective-permute-start | bytes 147464 | tf_op jit(solution)/shard_map/ppermute | solution.py:515
  21.5 14.9 %collective-permute-start.7 = (f32[12,8,128]{2,1,0:T(8,128)S(1)}, f32[12,8,128]{2,1,0:T(8,128)S(1)}, u32[]{:S(2)}, u32[]{:S(2)}) collective-permute-start(f32[12,8,128]{2,1,0:T(8,128)S(1)} %get-tuple-element.25), channel_id=1, source_target_pairs={{2,1},{4,3},{6,5},{8,7},{10,9},{12,11},{14,13},{16,15},{18,17},{20... | collective-permute-start | bytes 147464 | tf_op jit(solution)/shard_map/ppermute | solution.py:515
  22.3 10.1 %collective-permute-start.4 = (f32[32,128]{1,0:T(8,128)S(1)}, f32[32,128]{1,0:T(8,128)S(1)}, u32[]{:S(2)}, u32[]{:S(2)}) collective-permute-start(f32[32,128]{1,0:T(8,128)S(1)} %get-tuple-element.22), channel_id=1, source_target_pairs={{0,32},{1,33},{2,34},{3,35},{4,36},{5,37},{6,38},{7,39},{8,40},{9,... | collective-permute-start | bytes 49160 | tf_op jit(solution)/shard_map/ppermute | solution.py:511
  29.6 6.8 %collective-permute-start.5 = (f32[32,128]{1,0:T(8,128)S(1)}, f32[32,128]{1,0:T(8,128)S(1)}, u32[]{:S(2)}, u32[]{:S(2)}) collective-permute-start(f32[32,128]{1,0:T(8,128)S(1)} %get-tuple-element.23), channel_id=1, source_target_pairs={{32,0},{33,1},{34,2},{35,3},{36,4},{37,5},{38,6},{39,7},{40,8},{41... | collective-permute-start | bytes 49160 | tf_op jit(solution)/shard_map/ppermute | solution.py:511
  32.3 4.1 %copy-start.4 = (s32[1,1,1,512]{3,2,1,0:T(1,128)S(1)}, s32[1,1,1,512]{3,2,1,0:T(1,128)}, u32[]{:S(2)}) copy-start(s32[1,1,1,512]{3,2,1,0:T(1,128)} %refs_15_.1) | copy-start | bytes 6148
  32.4 4.1 %copy-start.5 = (f32[1,1,1,512]{3,2,1,0:T(1,128)S(1)}, f32[1,1,1,512]{3,2,1,0:T(1,128)}, u32[]{:S(2)}) copy-start(f32[1,1,1,512]{3,2,1,0:T(1,128)} %refs_16_.1) | copy-start | bytes 6148
  32.4 4.1 %copy-start.6 = (s32[1,1,1,512]{3,2,1,0:T(1,128)S(1)}, s32[1,1,1,512]{3,2,1,0:T(1,128)}, u32[]{:S(2)}) copy-start(s32[1,1,1,512]{3,2,1,0:T(1,128)} %refs_17_.1) | copy-start | bytes 6148
  32.4 4.1 %copy-start.7 = (s32[1,1,1,32]{3,2,1,0:T(1,128)S(1)}, s32[1,1,1,32]{3,2,1,0:T(1,128)}, u32[]{:S(2)}) copy-start(s32[1,1,1,32]{3,2,1,0:T(1,128)} %refs_14_.1) | copy-start | bytes 388
  54.4 14.0 %collective-permute-start.8 = (f32[1,1,1,48,128]{4,3,2,1,0:T(8,128)S(1)}, f32[1,1,1,48,128]{4,3,2,1,0:T(8,128)S(1)}, u32[]{:S(2)}, u32[]{:S(2)}) collective-permute-start(f32[1,1,1,48,128]{4,3,2,1,0:T(8,128)S(1)} %get-tuple-element.31), channel_id=1, source_target_pairs={{0,257},{1,256},{2,259},{3,258},{4,261},{5,260},{6,263},{7,262},{8... | collective-permute-start | bytes 73736 | tf_op jit(solution)/shard_map/ppermute | solution.py:644
  56.3 12.1 %collective-permute-start.9 = (f32[1,1,1,48,128]{4,3,2,1,0:T(8,128)S(1)}, f32[1,1,1,48,128]{4,3,2,1,0:T(8,128)S(1)}, u32[]{:S(2)}, u32[]{:S(2)}) collective-permute-start(f32[1,1,1,48,128]{4,3,2,1,0:T(8,128)S(1)} %get-tuple-element.32), channel_id=1, source_target_pairs={{0,256},{256,0},{1,257},{257,1},{2,258},{258,2},{3,259},{259,3},{4... | collective-permute-start | bytes 73736 | tf_op jit(solution)/shard_map/ppermute | solution.py:645

commit v5 on v4

--- a/solution.py
+++ b/solution.py
@@ -37,7 +37,7 @@
     return (vel_ref, comp) if comp < 3 else (mag_ref, comp - 3)
 
 
-def edges_kernel(vel_ref, mag_ref, low_ref, high_ref, first_ref, last_ref):
+def edges_kernel(vel_ref, mag_ref, low_ref, high_ref, first_ref, last_ref, one_ref, two_ref):
     pair = lanes_of((CELLS_P, CELLS_T)) // 2
     low = jnp.zeros((CELLS_P, CELLS_T), F32)
     high = jnp.zeros((CELLS_P, CELLS_T), F32)
@@ -55,28 +55,40 @@
         if comp < 5:
             first_ref[6 + comp] = ref[0, index, :, 1, :]
             last_ref[6 + comp] = ref[0, index, :, CELLS_P - 2, :]
+    high = pltpu.roll(high, 2, 1)
     low_ref[...] = low
-    high_ref[...] = pltpu.roll(high, 2, 1)
+    high_ref[...] = high
+    upward = lax.axis_index("lat") % 2 == 0
+    one_ref[...] = jnp.where(upward, high, low)
+    two_ref[...] = jnp.where(upward, low, high)
+
+
+def below_above(one, two):
+    upward = lax.axis_index("lat") % 2 == 0
+    return jnp.where(upward, two, one), jnp.where(upward, one, two)
 
 
 def corners_kernel(
-    below_ref, above_ref, first_ref, last_ref, before_ref, after_ref, first_out_ref, last_out_ref
+    one_ref, two_ref, first_ref, last_ref, before_ref, after_ref, first_out_ref, last_out_ref
 ):
     shape = (LEVELS, CELLS_T)
     for row, source, target in ((0, first_ref, first_out_ref), (CELLS_P - 1, last_ref, last_out_ref)):
-        below = jnp.broadcast_to(below_ref[row : row + 1, :], shape)
-        above = jnp.broadcast_to(above_ref[row : row + 1, :], shape)
+        below, above = below_above(one_ref[row : row + 1, :], two_ref[row : row + 1, :])
+        below = jnp.broadcast_to(below, shape)
+        above = jnp.broadcast_to(above, shape)
         target[0:11] = source[...]
         target[11] = jnp.where(rows_of(shape) == 0, below, above)
 
 
-def second_kernel(before_ref, after_ref, low_ref, high_ref, low_out_ref, high_out_ref):
+def second_kernel(before_ref, after_ref, low_ref, high_ref, one_ref, two_ref):
+    upward = lax.axis_index("lat") % 2 == 0
+
     odd = lax.axis_index("lon") % 2
 
     @pl.when(odd == 1)
     def _():
-        low_out_ref[...] = low_ref[...]
-        high_out_ref[...] = high_ref[...]
+        one_ref[...] = jnp.where(upward, high_ref[...], low_ref[...])
+        two_ref[...] = jnp.where(upward, low_ref[...], high_ref[...])
 
     @pl.when(odd == 0)
     def _():
@@ -89,10 +101,10 @@
                 block = ref[comp]
                 low = jnp.where(lane == spot, pltpu.roll(block, spot, 1) if spot else block, low)
                 high = jnp.where(lane == spot, pltpu.roll(block, spot + 1, 1), high)
-        low_out_ref[0:LEVELS] = low
-        high_out_ref[0:LEVELS] = high
-        low_out_ref[LEVELS:] = jnp.zeros((CELLS_P - LEVELS, CELLS_T), F32)
-        high_out_ref[LEVELS:] = jnp.zeros((CELLS_P - LEVELS, CELLS_T), F32)
+        one_ref[0:LEVELS] = jnp.where(upward, high, low)
+        two_ref[0:LEVELS] = jnp.where(upward, low, high)
+        one_ref[LEVELS:] = jnp.zeros((CELLS_P - LEVELS, CELLS_T), F32)
+        two_ref[LEVELS:] = jnp.zeros((CELLS_P - LEVELS, CELLS_T), F32)
 
 
 def flux_of(center, grad_r, grad_t, grad_p, spacing, wanted):
@@ -162,14 +174,15 @@
     return (up - down) * step
 
 
-def flux_kernel(steps, parity, vel_ref, mag_ref, below_ref, above_ref, *rest):
+def flux_kernel(steps, parity, vel_ref, mag_ref, one_ref, two_ref, *rest):
     flux_ref = rest[-1]
     wide = (CELLS_P, CELLS_T)
 
     @pl.when(lax.axis_index("lon") % 2 == parity)
     def _():
         is_below = lanes_of(wide) % 2 == 1
-        beside = jnp.where(is_below, below_ref[...], above_ref[...])
+        below, above = below_above(one_ref[...], two_ref[...])
+        beside = jnp.where(is_below, below, above)
         own_sine = inverse_sine(lax.axis_index("lat") * CELLS_T + lanes_of((8, CELLS_T)), steps[1])
 
         def make_flux(level, carry):
@@ -200,19 +213,18 @@
     mag_ref,
     low_ref,
     high_ref,
-    below_even_ref,
-    above_even_ref,
-    below_odd_ref,
-    above_odd_ref,
+    one_even_ref,
+    two_even_ref,
+    one_odd_ref,
+    two_odd_ref,
     first_ref,
     last_ref,
     before_even_ref,
     after_even_ref,
     before_odd_ref,
     after_odd_ref,
-    rows_ref,
-    cell_ref,
-    weight_ref,
+    spot_ref,
+    factor_ref,
     slot_ref,
     flux_in_ref,
     new_vel_ref,
@@ -252,8 +264,10 @@
 
     is_below = lane % 2 == 1
     level_of = (lane % 16) // 2
-    below = jnp.where(odd_block, below_odd_ref[...], below_even_ref[...])
-    above = jnp.where(odd_block, above_odd_ref[...], above_even_ref[...])
+    first_below, first_above = below_above(one_even_ref[...], two_even_ref[...])
+    second_below, second_above = below_above(one_odd_ref[...], two_odd_ref[...])
+    below = jnp.where(odd_block, second_below, first_below)
+    above = jnp.where(odd_block, second_above, first_above)
     beside = jnp.where(is_below, below, above)
 
     def swapped(block):
@@ -266,8 +280,8 @@
         total = jnp.zeros(flat, F32)
         for comp in range(6):
             start = 6 * side + comp
-            for ref, shift in ((below_odd_ref, 1), (above_odd_ref, 0)):
-                column = ref[0:LEVELS, start : start + 1]
+            for block, shift in ((second_below, 1), (second_above, 0)):
+                column = block[0:LEVELS, start : start + 1]
                 total = jnp.where(lane_flat == spot + (16 * comp + shift), column, total)
         return jnp.where(odd_block, held, jnp.sum(total, axis=0, keepdims=True))
 
@@ -380,19 +394,8 @@
 
     lax.fori_loop(0, LEVELS, advance, 0, unroll=8)
 
-    slots_total = cell_ref.shape[-1]
+    slots_total = spot_ref.shape[-1]
     chunks = slots_total // CELLS_T
-    rows_wide = jnp.broadcast_to(rows_ref[0, 0].astype(F32), (8, lon_blocks))
-    owner = lanes_of((lon_blocks, slots_total)) // CAP == rows_of((lon_blocks, slots_total))
-    counts = jnp.dot(rows_wide, owner.astype(F32), preferred_element_type=F32)
-    bucket = lanes_of((8, slots_total)) % CAP
-    live = bucket < (counts + 0.5).astype(jnp.int32)
-    scale = jnp.where(live, jnp.broadcast_to(weight_ref[0, 0], (8, slots_total)), 0.0)
-    cells = jnp.broadcast_to(cell_ref[0, 0], (8, slots_total))
-    cell_t = cells % CELLS_T
-    cell_p = cells // CELLS_T
-    scale = jnp.where(cell_p % 8 == rows_of(cells.shape), scale, 0.0)
-    group = cell_p // 8
     taken_ref[6:8] = jnp.zeros((2, LEVELS, slots_total), F32)
     taken_ref[6, 0:1] = slot_ref[0, 0].astype(F32)
     sub = rows_of((8, CELLS_T))
@@ -413,8 +416,8 @@
 
     for chunk in range(chunks):
         part = slice(chunk * CELLS_T, (chunk + 1) * CELLS_T)
-        where_t = cell_t[:, part]
-        weights = [jnp.where(group[:, part] == step, scale[:, part], 0.0) for step in range(4)]
+        where_t = spot_ref[:, part]
+        weights = [factor_ref[step, :, part] for step in range(CELLS_P // 8)]
         for start, ref in ((0, new_vel_ref), (3, new_mag_ref)):
 
             def take(comp, carry, start=start, ref=ref, part=part, where_t=where_t, weights=weights):
@@ -453,6 +456,21 @@
         copy.start()
     for copy in copies:
         copy.wait()
+
+
+def donors_kernel(lon_blocks, rows_ref, cell_ref, weight_ref, spot_ref, factor_ref):
+    slots_total = cell_ref.shape[-1]
+    rows_wide = jnp.broadcast_to(rows_ref[0, 0].astype(F32), (8, lon_blocks))
+    owner = lanes_of((lon_blocks, slots_total)) // CAP == rows_of((lon_blocks, slots_total))
+    counts = jnp.dot(rows_wide, owner.astype(F32), preferred_element_type=F32)
+    bucket = lanes_of((8, slots_total)) % CAP
+    live = bucket < (counts + 0.5).astype(jnp.int32)
+    scale = jnp.where(live, jnp.broadcast_to(weight_ref[0, 0], (8, slots_total)), 0.0)
+    cells = jnp.broadcast_to(cell_ref[0, 0], (8, slots_total))
+    spot_ref[...] = cells % CELLS_T
+    cell_p = cells // CELLS_T
+    for step in range(CELLS_P // 8):
+        factor_ref[step] = jnp.where(cell_p == 8 * step + rows_of(cells.shape), scale, 0.0)
 
 
 def collect_kernel(got_ref, near_ref, far_ref):
@@ -501,29 +519,29 @@
     strip_full = tiles(12, LEVELS, CELLS_T)
     evens, odds = range(0, lon_blocks, 2), range(1, lon_blocks, 2)
 
-    def along_lat(block, step, lons):
-        pairs = [
-            (lat * lon_blocks + lon, (lat + step) * lon_blocks + lon)
-            for lat in range(lat_blocks)
-            for lon in lons
-            if 0 <= lat + step < lat_blocks
-        ]
-        return lax.ppermute(block, ("lat", "lon"), pairs)
-
     def along_lon(block, step, lons):
         pairs = [(lon, lon + step) for lon in lons if 0 <= lon + step < lon_blocks]
         return lax.ppermute(block, "lon", pairs)
 
-    low, high, first, last = pl.pallas_call(
+    def between_lat(block, start, lons):
+        pairs = [
+            (lat * lon_blocks + lon, other * lon_blocks + lon)
+            for first_lat in range(start, lat_blocks - 1, 2)
+            for lat, other in ((first_lat, first_lat + 1), (first_lat + 1, first_lat))
+            for lon in lons
+        ]
+        return lax.ppermute(block, ("lat", "lon"), pairs)
+
+    low, high, first, last, one, two = pl.pallas_call(
         edges_kernel,
         in_specs=[VMEM] * 2,
-        out_specs=[VMEM] * 4,
-        out_shape=[pack, pack, strip, strip],
+        out_specs=[VMEM] * 6,
+        out_shape=[pack, pack, strip, strip, pack, pack],
         compiler_params=limit(4),
         name="edges",
     )(velocity, magnetic)
-    below_even = along_lat(high, 1, evens)
-    above_even = along_lat(low, -1, evens)
+    one_even = between_lat(one, 0, evens)
+    two_even = between_lat(two, 1, evens)
     before_even = along_lon(last, 1, odds)
     after_even = along_lon(first, -1, odds)
     first_full, last_full = pl.pallas_call(
@@ -533,10 +551,10 @@
         out_shape=[strip_full, strip_full],
         compiler_params=limit(4),
         name="corners",
-    )(below_even, above_even, first, last, before_even, after_even)
+    )(one_even, two_even, first, last, before_even, after_even)
     before_odd = along_lon(last_full, 1, evens)
     after_odd = along_lon(first_full, -1, evens)
-    second_low, second_high = pl.pallas_call(
+    second_one, second_two = pl.pallas_call(
         second_kernel,
         in_specs=[VMEM] * 4,
         out_specs=[VMEM] * 2,
@@ -544,16 +562,31 @@
         compiler_params=limit(4),
         name="second",
     )(before_even, after_even, low, high)
-    every = range(lon_blocks)
-    below_odd = along_lat(second_high, 1, every)
-    above_odd = along_lat(second_low, -1, every)
+    one_odd = between_lat(second_one, 0, range(lon_blocks))
+    two_odd = between_lat(second_two, 1, range(lon_blocks))
     slots_total = send_cell.shape[-1]
     steps = (spacing, theta_step, phi_step)
 
+    def donors(*refs):
+        donors_kernel(lon_blocks, *refs)
+
+    spots, factors = pl.pallas_call(
+        donors,
+        in_specs=[VMEM] * 3,
+        out_specs=[VMEM] * 2,
+        out_shape=[
+            jax.ShapeDtypeStruct((8, slots_total), jnp.int32),
+            tiles(CELLS_P // 8, 8, slots_total),
+        ],
+        compiler_params=limit(4),
+        cost_estimate=pl.CostEstimate(flops=0, bytes_accessed=1, transcendentals=0),
+        name="donors",
+    )(pair_rows, send_cell, send_weight)
+
     def section(*refs):
         section_kernel(steps, lat_blocks, lon_blocks, *refs)
 
-    def flux_of_cells(parity, below, above, *given):
+    def flux_of_cells(parity, one, two, *given):
         def kernel(*refs):
             flux_kernel(steps, parity, *refs)
 
@@ -565,13 +598,13 @@
             input_output_aliases={4: 0} if given else {},
             compiler_params=limit(8),
             name="flux",
-        )(velocity, magnetic, below, above, *given)
-
-    flux = flux_of_cells(0, below_even, above_even)
-    flux = flux_of_cells(1, below_odd, above_odd, flux)
+        )(velocity, magnetic, one, two, *given)
+
+    flux = flux_of_cells(0, one_even, two_even)
+    flux = flux_of_cells(1, one_odd, two_odd, flux)
     new_velocity, new_magnetic, payload, _ = pl.pallas_call(
         section,
-        in_specs=[VMEM] * 19,
+        in_specs=[VMEM] * 18,
         out_specs=[VMEM] * 4,
         out_shape=[
             tiles(*velocity.shape),
@@ -579,7 +612,7 @@
             tiles(lon_blocks, 8, CELLS_T),
             tiles(9, LEVELS, CELLS_P, CELLS_T),
         ],
-        input_output_aliases={18: 3},
+        input_output_aliases={17: 3},
         scratch_shapes=[
             pltpu.VMEM((5, CELLS_P, CELLS_T), F32),
             pltpu.VMEM((2, 5, LEVELS, CELLS_T), F32),
@@ -593,19 +626,18 @@
         magnetic,
         low,
         high,
-        below_even,
-        above_even,
-        below_odd,
-        above_odd,
+        one_even,
+        two_even,
+        one_odd,
+        two_odd,
         first,
         last,
         before_even,
         after_even,
         before_odd,
         after_odd,
-        pair_rows,
-        send_cell,
-        send_weight,
+        spots,
+        factors,
         cycle_slot,
         flux,
     )

time: 69.5 us -> 68.1 us (0.980)
  waiting for transfers between devices: 20.1 us -> 12.9 us
  starting transfers between devices: 25.5 us -> 28.4 us
  local copies, waits for them, and re-layouts: 2.02 us -> 4.61 us
    ppermute x4, waiting for transfers between devices: 5.44 us -> 1.98 us  [between_lat(): return lax.ppermute(block, ('lat', 'lon'), pairs)]
    unnamed x16, local copies, waits for them, and re-layouts: 2.02 us -> 4.61 us
    ppermute x4, waiting for transfers between devices: 6.51 us -> 4.14 us  [along_lon(): return lax.ppermute(block, 'lon', pairs)]
    ppermute x4, starting transfers between devices: 16.2 us -> 18 us  [between_lat(): return lax.ppermute(block, ('lat', 'lon'), pairs)]
    ppermute x1, waiting for transfers between devices: 8.1 us -> 6.75 us  [local(): far = lax.ppermute(far, ('grid', 'lon'), across)]
    ppermute x1, starting transfers between devices: 3.08 us -> 4.27 us  [local(): near = lax.ppermute(near, 'grid', [(0, 1), (1, 0)])]
    pallas_call x2 -> x3, Pallas kernels: 2.67 us -> 2.81 us  [the longest x1 2.35 us: local(): pl.pallas_call(section, in_specs=[VMEM] * 18, out_specs=[VMEM] * 4, out_s...]
  transfers between devices with their start and end apart: 10 -> 10, of which waited for: 4 -> 3; matrix products, arithmetic and copies ran while one was open for 0% -> 0% of each run, Pallas kernels for 3% -> 3%
where the time goes in v5:
time: 68.1 us; the launch traced here: 67.6 us
  starting transfers between devices  28.4 us (42%)
  blocking collectives  15.1 us (22%)
  waiting for transfers between devices  12.9 us (19%)
  Pallas kernels  5.11 us (8%)
  local copies, waits for them, and re-layouts  4.61 us (7%)
  between operations  0.84 us (1%)
    ppermute x4, starting transfers between devices, between_lat(): return lax.ppermute(block, ('lat', 'lon'), pairs)  18 us
    all_to_all x1, blocking collectives, local(): lax.all_to_all(payload.reshape(pairs, 16, CELLS_T), 'lon', split_axis=0,...  15.1 us
    ppermute x1, waiting for transfers between devices, local(): far = lax.ppermute(far, ('grid', 'lon'), across)  6.75 us
    unnamed x16, local copies, waits for them, and re-layouts  4.61 us
    ppermute x1, starting transfers between devices, local(): near = lax.ppermute(near, 'grid', [(0, 1), (1, 0)])  4.27 us
    ppermute x4, starting transfers between devices, along_lon(): return lax.ppermute(block, 'lon', pairs)  4.2 us
    ppermute x4, waiting for transfers between devices, along_lon(): return lax.ppermute(block, 'lon', pairs)  4.14 us
    pallas_call x1, Pallas kernels, local(): pl.pallas_call(section, in_specs=[VMEM] * 18, out_specs=[VMEM] * 4, out_s...  2.35 us
  transfers between devices with their start and end apart: 10, of which 3 were waited for; matrix products, arithmetic and copies ran while one was open for 0% of the time, Pallas kernels for 3%

profile of v5, /device:TPU:96, one launch (start us, length us, event | category | flops | bytes accessed | tf_op | source)
XLA Modules:
  0.0 67.6 jit_solution(7858868208066226973)
XLA Ops:
  0.6 1.0 %copy-done = f32[1,3,8,32,128]{4,3,2,1,0:T(8,128)S(1)} copy-done((f32[1,3,8,32,128]{4,3,2,1,0:T(8,128)S(1)}, f32[1,3,8,32,128]{4,3,2,1,0:T(8,128)}, u32[]{:S(2)}) %copy-start) | copy-done | bytes 393240
  1.6 1.0 %copy-done.2 = f32[1,3,8,32,128]{4,3,2,1,0:T(8,128)S(1)} copy-done((f32[1,3,8,32,128]{4,3,2,1,0:T(8,128)S(1)}, f32[1,3,8,32,128]{4,3,2,1,0:T(8,128)}, u32[]{:S(2)}) %copy-start.2) | copy-done | bytes 393240
  2.6 0.3 edges.1
  3.0 0.7 collective-permute-start.2
  3.6 1.3 %collective-permute-start.3 = (f32[11,8,128]{2,1,0:T(8,128)S(1)}, f32[11,8,128]{2,1,0:T(8,128)S(1)}, u32[]{:S(2)}, u32[]{:S(2)}) collective-permute-start(f32[11,8,128]{2,1,0:T(8,128)S(1)} %get-tuple-element.27.first_ref.refs_8_), channel_id=1, source_target_pairs={{1,0},{3,2},{5,4},{7,6},{9,8},{11,10},{13,12},{15,14},{17,16},{19,... | collective-permute-start | bytes 135176 | tf_op jit(solution)/shard_map/ppermute | solution.py:524
  4.9 2.0 %collective-permute-start = (f32[32,128]{1,0:T(8,128)S(1)}, f32[32,128]{1,0:T(8,128)S(1)}, u32[]{:S(2)}, u32[]{:S(2)}) collective-permute-start(f32[32,128]{1,0:T(8,128)S(1)} %get-tuple-element.24), channel_id=1, source_target_pairs={{0,32},{2,34},{4,36},{6,38},{8,40},{10,42},{12,44},{14,46},{16,48}... | collective-permute-start | bytes 49160 | tf_op jit(solution)/shard_map/ppermute | solution.py:533
  6.9 6.8 %collective-permute-start.1 = (f32[32,128]{1,0:T(8,128)S(1)}, f32[32,128]{1,0:T(8,128)S(1)}, u32[]{:S(2)}, u32[]{:S(2)}) collective-permute-start(f32[32,128]{1,0:T(8,128)S(1)} %get-tuple-element.25), channel_id=1, source_target_pairs={{32,64},{34,66},{36,68},{38,70},{40,72},{42,74},{44,76},{46,78},{4... | collective-permute-start | bytes 49160 | tf_op jit(solution)/shard_map/ppermute | solution.py:533
  13.8 0.0 collective-permute-done.one_ref.refs_2_.refs_4_
  13.8 2.0 %collective-permute-done.1.two_ref.refs_3_.refs_5_ = f32[32,128]{1,0:T(8,128)S(1)} collective-permute-done((f32[32,128]{1,0:T(8,128)S(1)}, f32[32,128]{1,0:T(8,128)S(1)}, u32[]{:S(2)}, u32[]{:S(2)}) %collective-permute-start.1) | collective-permute-done | bytes 16416 | tf_op jit(solution)/shard_map/ppermute | solution.py:533
  15.8 0.0 collective-permute-done.2.before_ref.refs_10_
  15.8 4.1 %collective-permute-done.3.after_ref.refs_11_ = f32[11,8,128]{2,1,0:T(8,128)S(1)} collective-permute-done((f32[11,8,128]{2,1,0:T(8,128)S(1)}, f32[11,8,128]{2,1,0:T(8,128)S(1)}, u32[]{:S(2)}, u32[]{:S(2)}) %collective-permute-start.3) | collective-permute-done | bytes 45088 | tf_op jit(solution)/shard_map/ppermute | solution.py:524
  19.9 1.6 %collective-permute-start.6 = (f32[12,8,128]{2,1,0:T(8,128)S(1)}, f32[12,8,128]{2,1,0:T(8,128)S(1)}, u32[]{:S(2)}, u32[]{:S(2)}) collective-permute-start(f32[12,8,128]{2,1,0:T(8,128)S(1)} %get-tuple-element.30), channel_id=1, source_target_pairs={{0,1},{2,3},{4,5},{6,7},{8,9},{10,11},{12,13},{14,15},{16,17},{18,... | collective-permute-start | bytes 147464 | tf_op jit(solution)/shard_map/ppermute | solution.py:524
  21.5 0.7 collective-permute-start.7
  22.2 0.1 second.1
  22.3 2.7 %collective-permute-start.4 = (f32[32,128]{1,0:T(8,128)S(1)}, f32[32,128]{1,0:T(8,128)S(1)}, u32[]{:S(2)}, u32[]{:S(2)}) collective-permute-start(f32[32,128]{1,0:T(8,128)S(1)} %get-tuple-element.28), channel_id=1, source_target_pairs={{0,32},{1,33},{2,34},{3,35},{4,36},{5,37},{6,38},{7,39},{8,40},{9,... | collective-permute-start | bytes 49160 | tf_op jit(solution)/shard_map/ppermute | solution.py:533
  25.0 6.5 %collective-permute-start.5 = (f32[32,128]{1,0:T(8,128)S(1)}, f32[32,128]{1,0:T(8,128)S(1)}, u32[]{:S(2)}, u32[]{:S(2)}) collective-permute-start(f32[32,128]{1,0:T(8,128)S(1)} %get-tuple-element.29), channel_id=1, source_target_pairs={{32,64},{33,65},{34,66},{35,67},{36,68},{37,69},{38,70},{39,71},{4... | collective-permute-start | bytes 49160 | tf_op jit(solution)/shard_map/ppermute | solution.py:533
  31.5 0.0 copy-start.4
  31.5 0.7 copy-done.4
  32.2 0.7 %copy-done.5 = f32[1,1,1,512]{3,2,1,0:T(1,128)S(1)} copy-done((f32[1,1,1,512]{3,2,1,0:T(1,128)S(1)}, f32[1,1,1,512]{3,2,1,0:T(1,128)}, u32[]{:S(2)}) %copy-start.5) | copy-done | bytes 2072
  32.9 0.7 copy-done.7
  33.5 0.1 donors.1
  33.7 0.8 %flux.2.refs_4_ = f32[9,8,32,128]{3,2,1,0:T(8,128)S(1)} custom-call(f32[1,3,8,32,128]{4,3,2,1,0:T(8,128)S(1)} %copy-done.1, f32[1,3,8,32,128]{4,3,2,1,0:T(8,128)S(1)} %copy-done.3, f32[32,128]{1,0:T(8,128)S(1)} %collective-permute-done.one_ref.refs_2_.refs_4_, f32[32,128]{1,0:T(8,128)S(1)} %collective-permute-done.1.two_ref.refs_3_.refs_5_), custom_call_target="tpu_custom_call" | custom-call | tf_op jit(solution)/shard_map/flux/pallas_call | solution.py:593
  34.5 0.0 copy-start.6
  34.6 0.6 copy-done.6
  35.2 2.4 %section.1 = (f32[1,3,8,32,128]{4,3,2,1,0:T(8,128)S(1)}, f32[1,3,8,32,128]{4,3,2,1,0:T(8,128)S(1)}, f32[32,8,128]{2,1,0:T(8,128)S(1)}, f32[9,8,32,128]{3,2,1,0:T(8,128)S(1)}) custom-call(f32[1,3,8,32,128]{4,3,2,1,0:T(8,128)S(1)} %copy-done.1, f32[1,3,8,32,128]{4,3,2,1,0:T(8,128)S(1)} %copy-done.3, ...), custom_call_target="tpu_custom_call", output_to_operand_aliasing={{3}: (17, {})} | custom-call | tf_op jit(solution)/shard_map/section/pallas_call | solution.py:605
  37.5 15.1 %all_to_all.5.got_ref = f32[16,16,128]{2,1,0:T(8,128)S(1)} all-to-all(f32[16,16,128]{2,1,0:T(8,128)S(1)} %bitcast.1), channel_id=1, replica_groups={{0,2,4,6,8,10,12,14,16,18,20,22,24,26,28,30},{1,3,5,7,9,11,13,15,17,19,..., dimensions={0} | all-to-all | bytes 262144 | tf_op jit(solution)/shard_map/all_to_all | solution.py:655
  52.7 0.5 collect.1
  53.1 1.9 %collective-permute-start.8 = (f32[1,1,1,48,128]{4,3,2,1,0:T(8,128)S(1)}, f32[1,1,1,48,128]{4,3,2,1,0:T(8,128)S(1)}, u32[]{:S(2)}, u32[]{:S(2)}) collective-permute-start(f32[1,1,1,48,128]{4,3,2,1,0:T(8,128)S(1)} %get-tuple-element.39), channel_id=1, source_target_pairs={{0,257},{1,256},{2,259},{3,258},{4,261},{5,260},{6,263},{7,262},{8... | collective-permute-start | bytes 73736 | tf_op jit(solution)/shard_map/ppermute | solution.py:676
  55.1 4.3 %collective-permute-start.9 = (f32[1,1,1,48,128]{4,3,2,1,0:T(8,128)S(1)}, f32[1,1,1,48,128]{4,3,2,1,0:T(8,128)S(1)}, u32[]{:S(2)}, u32[]{:S(2)}) collective-permute-start(f32[1,1,1,48,128]{4,3,2,1,0:T(8,128)S(1)} %get-tuple-element.40), channel_id=1, source_target_pairs={{0,256},{256,0},{1,257},{257,1},{2,258},{258,2},{3,259},{259,3},{4... | collective-permute-start | bytes 73736 | tf_op jit(solution)/shard_map/ppermute | solution.py:677
  59.3 0.9 %store.1 = (f32[1,3,8,32,128]{4,3,2,1,0:T(8,128)}, f32[1,3,8,32,128]{4,3,2,1,0:T(8,128)}) custom-call(f32[1,3,8,32,128]{4,3,2,1,0:T(8,128)S(1)} %get-tuple-element.34.vel_ref, f32[1,3,8,32,128]{4,3,2,1,0:T(8,128)S(1)} %get-tuple-element.35.mag_ref), custom_call_target="tpu_custom_call" | custom-call | tf_op jit(solution)/shard_map/store/pallas_call | solution.py:644
  60.2 6.7 %collective-permute-done.8 = f32[1,1,1,48,128]{4,3,2,1,0:T(8,128)S(1)} collective-permute-done((f32[1,1,1,48,128]{4,3,2,1,0:T(8,128)S(1)}, f32[1,1,1,48,128]{4,3,2,1,0:T(8,128)S(1)}, u32[]{:S(2)}, u32[]{:S(2)}) %collective-permute-start.8) | collective-permute-done | bytes 24608 | tf_op jit(solution)/shard_map/ppermute | solution.py:676
  67.0 0.6 add.3
  (15 shorter events, 0.1 us)
Async XLA Ops:
  0.6 1.0 %copy-start = (f32[1,3,8,32,128]{4,3,2,1,0:T(8,128)S(1)}, f32[1,3,8,32,128]{4,3,2,1,0:T(8,128)}, u32[]{:S(2)}) copy-start(f32[1,3,8,32,128]{4,3,2,1,0:T(8,128)} %refs_0_.7) | copy-start | bytes 1179652
  1.6 1.0 %copy-start.2 = (f32[1,3,8,32,128]{4,3,2,1,0:T(8,128)S(1)}, f32[1,3,8,32,128]{4,3,2,1,0:T(8,128)}, u32[]{:S(2)}) copy-start(f32[1,3,8,32,128]{4,3,2,1,0:T(8,128)} %refs_1_.7) | copy-start | bytes 1179652
  2.6 31.1 %copy-start.1 = (f32[1,3,8,32,128]{4,3,2,1,0:T(8,128)S(1)}, f32[1,3,8,32,128]{4,3,2,1,0:T(8,128)}, u32[]{:S(2)}) copy-start(f32[1,3,8,32,128]{4,3,2,1,0:T(8,128)} %refs_0_.7) | copy-start | bytes 1179652
  2.6 31.1 %copy-start.3 = (f32[1,3,8,32,128]{4,3,2,1,0:T(8,128)S(1)}, f32[1,3,8,32,128]{4,3,2,1,0:T(8,128)}, u32[]{:S(2)}) copy-start(f32[1,3,8,32,128]{4,3,2,1,0:T(8,128)} %refs_1_.7) | copy-start | bytes 1179652
  3.0 12.8 %collective-permute-start.2 = (f32[11,8,128]{2,1,0:T(8,128)S(1)}, f32[11,8,128]{2,1,0:T(8,128)S(1)}, u32[]{:S(2)}, u32[]{:S(2)}) collective-permute-start(f32[11,8,128]{2,1,0:T(8,128)S(1)} %get-tuple-element.26.last_ref.refs_9_), channel_id=1, source_target_pairs={{1,2},{3,4},{5,6},{7,8},{9,10},{11,12},{13,14},{15,16},{17,18},{19... | collective-permute-start | bytes 135176 | tf_op jit(solution)/shard_map/ppermute | solution.py:524
  3.6 16.3 %collective-permute-start.3 = (f32[11,8,128]{2,1,0:T(8,128)S(1)}, f32[11,8,128]{2,1,0:T(8,128)S(1)}, u32[]{:S(2)}, u32[]{:S(2)}) collective-permute-start(f32[11,8,128]{2,1,0:T(8,128)S(1)} %get-tuple-element.27.first_ref.refs_8_), channel_id=1, source_target_pairs={{1,0},{3,2},{5,4},{7,6},{9,8},{11,10},{13,12},{15,14},{17,16},{19,... | collective-permute-start | bytes 135176 | tf_op jit(solution)/shard_map/ppermute | solution.py:524
  4.9 8.9 %collective-permute-start = (f32[32,128]{1,0:T(8,128)S(1)}, f32[32,128]{1,0:T(8,128)S(1)}, u32[]{:S(2)}, u32[]{:S(2)}) collective-permute-start(f32[32,128]{1,0:T(8,128)S(1)} %get-tuple-element.24), channel_id=1, source_target_pairs={{0,32},{2,34},{4,36},{6,38},{8,40},{10,42},{12,44},{14,46},{16,48}... | collective-permute-start | bytes 49160 | tf_op jit(solution)/shard_map/ppermute | solution.py:533
  6.9 8.8 %collective-permute-start.1 = (f32[32,128]{1,0:T(8,128)S(1)}, f32[32,128]{1,0:T(8,128)S(1)}, u32[]{:S(2)}, u32[]{:S(2)}) collective-permute-start(f32[32,128]{1,0:T(8,128)S(1)} %get-tuple-element.25), channel_id=1, source_target_pairs={{32,64},{34,66},{36,68},{38,70},{40,72},{42,74},{44,76},{46,78},{4... | collective-permute-start | bytes 49160 | tf_op jit(solution)/shard_map/ppermute | solution.py:533
  19.9 14.6 %collective-permute-start.6 = (f32[12,8,128]{2,1,0:T(8,128)S(1)}, f32[12,8,128]{2,1,0:T(8,128)S(1)}, u32[]{:S(2)}, u32[]{:S(2)}) collective-permute-start(f32[12,8,128]{2,1,0:T(8,128)S(1)} %get-tuple-element.30), channel_id=1, source_target_pairs={{0,1},{2,3},{4,5},{6,7},{8,9},{10,11},{12,13},{14,15},{16,17},{18,... | collective-permute-start | bytes 147464 | tf_op jit(solution)/shard_map/ppermute | solution.py:524
  21.5 13.0 %collective-permute-start.7 = (f32[12,8,128]{2,1,0:T(8,128)S(1)}, f32[12,8,128]{2,1,0:T(8,128)S(1)}, u32[]{:S(2)}, u32[]{:S(2)}) collective-permute-start(f32[12,8,128]{2,1,0:T(8,128)S(1)} %get-tuple-element.31), channel_id=1, source_target_pairs={{2,1},{4,3},{6,5},{8,7},{10,9},{12,11},{14,13},{16,15},{18,17},{20... | collective-permute-start | bytes 147464 | tf_op jit(solution)/shard_map/ppermute | solution.py:524
  22.3 12.2 %collective-permute-start.4 = (f32[32,128]{1,0:T(8,128)S(1)}, f32[32,128]{1,0:T(8,128)S(1)}, u32[]{:S(2)}, u32[]{:S(2)}) collective-permute-start(f32[32,128]{1,0:T(8,128)S(1)} %get-tuple-element.28), channel_id=1, source_target_pairs={{0,32},{1,33},{2,34},{3,35},{4,36},{5,37},{6,38},{7,39},{8,40},{9,... | collective-permute-start | bytes 49160 | tf_op jit(solution)/shard_map/ppermute | solution.py:533
  25.0 9.5 %collective-permute-start.5 = (f32[32,128]{1,0:T(8,128)S(1)}, f32[32,128]{1,0:T(8,128)S(1)}, u32[]{:S(2)}, u32[]{:S(2)}) collective-permute-start(f32[32,128]{1,0:T(8,128)S(1)} %get-tuple-element.29), channel_id=1, source_target_pairs={{32,64},{33,65},{34,66},{35,67},{36,68},{37,69},{38,70},{39,71},{4... | collective-permute-start | bytes 49160 | tf_op jit(solution)/shard_map/ppermute | solution.py:533
  31.5 0.7 %copy-start.4 = (s32[1,1,1,512]{3,2,1,0:T(1,128)S(1)}, s32[1,1,1,512]{3,2,1,0:T(1,128)}, u32[]{:S(2)}) copy-start(s32[1,1,1,512]{3,2,1,0:T(1,128)} %refs_1_.4) | copy-start | bytes 6148
  32.2 0.7 %copy-start.5 = (f32[1,1,1,512]{3,2,1,0:T(1,128)S(1)}, f32[1,1,1,512]{3,2,1,0:T(1,128)}, u32[]{:S(2)}) copy-start(f32[1,1,1,512]{3,2,1,0:T(1,128)} %refs_2_.1) | copy-start | bytes 6148
  32.9 0.7 copy-start.7
  34.5 0.7 %copy-start.6 = (s32[1,1,1,512]{3,2,1,0:T(1,128)S(1)}, s32[1,1,1,512]{3,2,1,0:T(1,128)}, u32[]{:S(2)}) copy-start(s32[1,1,1,512]{3,2,1,0:T(1,128)} %refs_16_.1) | copy-start | bytes 6148
  53.1 13.9 %collective-permute-start.8 = (f32[1,1,1,48,128]{4,3,2,1,0:T(8,128)S(1)}, f32[1,1,1,48,128]{4,3,2,1,0:T(8,128)S(1)}, u32[]{:S(2)}, u32[]{:S(2)}) collective-permute-start(f32[1,1,1,48,128]{4,3,2,1,0:T(8,128)S(1)} %get-tuple-element.39), channel_id=1, source_target_pairs={{0,257},{1,256},{2,259},{3,258},{4,261},{5,260},{6,263},{7,262},{8... | collective-permute-start | bytes 73736 | tf_op jit(solution)/shard_map/ppermute | solution.py:676
  55.1 11.9 %collective-permute-start.9 = (f32[1,1,1,48,128]{4,3,2,1,0:T(8,128)S(1)}, f32[1,1,1,48,128]{4,3,2,1,0:T(8,128)S(1)}, u32[]{:S(2)}, u32[]{:S(2)}) collective-permute-start(f32[1,1,1,48,128]{4,3,2,1,0:T(8,128)S(1)} %get-tuple-element.40), channel_id=1, source_target_pairs={{0,256},{256,0},{1,257},{257,1},{2,258},{258,2},{3,259},{259,3},{4... | collective-permute-start | bytes 73736 | tf_op jit(solution)/shard_map/ppermute | solution.py:677

commit v6 on v5

--- a/solution.py
+++ b/solution.py
@@ -37,12 +37,34 @@
     return (vel_ref, comp) if comp < 3 else (mag_ref, comp - 3)
 
 
-def edges_kernel(vel_ref, mag_ref, low_ref, high_ref, first_ref, last_ref, one_ref, two_ref):
+def edges_kernel(
+    vel_ref,
+    mag_ref,
+    low_ref,
+    high_ref,
+    first_ref,
+    last_ref,
+    one_ref,
+    two_ref,
+    held_vel_ref,
+    held_mag_ref,
+    sem_ref,
+):
+    copies = []
+    for comp in range(6):
+        ref, index = pick(vel_ref, mag_ref, comp)
+        held, _ = pick(held_vel_ref, held_mag_ref, comp)
+        copies.append(
+            pltpu.make_async_copy(ref.at[0, index], held.at[0, index], sem_ref.at[comp])
+        )
+    for copy in copies:
+        copy.start()
     pair = lanes_of((CELLS_P, CELLS_T)) // 2
     low = jnp.zeros((CELLS_P, CELLS_T), F32)
     high = jnp.zeros((CELLS_P, CELLS_T), F32)
     for comp in range(6):
-        ref, index = pick(vel_ref, mag_ref, comp)
+        copies[comp].wait()
+        ref, index = pick(held_vel_ref, held_mag_ref, comp)
         for level in range(LEVELS):
             place = 16 * comp + 2 * level
             block = ref[0, index, level]
@@ -69,7 +91,15 @@
 
 
 def corners_kernel(
-    one_ref, two_ref, first_ref, last_ref, before_ref, after_ref, first_out_ref, last_out_ref
+    one_ref,
+    two_ref,
+    first_ref,
+    last_ref,
+    before_ref,
+    after_ref,
+    flux_ref,
+    first_out_ref,
+    last_out_ref,
 ):
     shape = (LEVELS, CELLS_T)
     for row, source, target in ((0, first_ref, first_out_ref), (CELLS_P - 1, last_ref, last_out_ref)):
@@ -532,26 +562,55 @@
         ]
         return lax.ppermute(block, ("lat", "lon"), pairs)
 
-    low, high, first, last, one, two = pl.pallas_call(
+    low, high, first, last, one, two, held_vel, held_mag = pl.pallas_call(
         edges_kernel,
-        in_specs=[VMEM] * 2,
-        out_specs=[VMEM] * 6,
-        out_shape=[pack, pack, strip, strip, pack, pack],
+        in_specs=[HBM] * 2,
+        out_specs=[VMEM] * 8,
+        out_shape=[
+            pack,
+            pack,
+            strip,
+            strip,
+            pack,
+            pack,
+            tiles(*velocity.shape),
+            tiles(*magnetic.shape),
+        ],
+        scratch_shapes=[
+            pltpu.SemaphoreType.DMA((6,)),
+        ],
         compiler_params=limit(4),
         name="edges",
-    )(velocity, magnetic)
+    )(*(pltpu.with_memory_space_constraint(array, pltpu.HBM) for array in (velocity, magnetic)))
     one_even = between_lat(one, 0, evens)
     two_even = between_lat(two, 1, evens)
     before_even = along_lon(last, 1, odds)
     after_even = along_lon(first, -1, odds)
+    steps = (spacing, theta_step, phi_step)
+
+    def flux_of_cells(parity, one, two, *given):
+        def kernel(*refs):
+            flux_kernel(steps, parity, *refs)
+
+        return pl.pallas_call(
+            kernel,
+            in_specs=[VMEM] * (4 + len(given)),
+            out_specs=VMEM,
+            out_shape=tiles(9, LEVELS, CELLS_P, CELLS_T),
+            input_output_aliases={4: 0} if given else {},
+            compiler_params=limit(8),
+            name="flux",
+        )(held_vel, held_mag, one, two, *given)
+
+    flux = flux_of_cells(0, one_even, two_even)
     first_full, last_full = pl.pallas_call(
         corners_kernel,
-        in_specs=[VMEM] * 6,
+        in_specs=[VMEM] * 7,
         out_specs=[VMEM] * 2,
         out_shape=[strip_full, strip_full],
         compiler_params=limit(4),
         name="corners",
-    )(one_even, two_even, first, last, before_even, after_even)
+    )(one_even, two_even, first, last, before_even, after_even, flux)
     before_odd = along_lon(last_full, 1, evens)
     after_odd = along_lon(first_full, -1, evens)
     second_one, second_two = pl.pallas_call(
@@ -565,7 +624,6 @@
     one_odd = between_lat(second_one, 0, range(lon_blocks))
     two_odd = between_lat(second_two, 1, range(lon_blocks))
     slots_total = send_cell.shape[-1]
-    steps = (spacing, theta_step, phi_step)
 
     def donors(*refs):
         donors_kernel(lon_blocks, *refs)
@@ -586,21 +644,6 @@
     def section(*refs):
         section_kernel(steps, lat_blocks, lon_blocks, *refs)
 
-    def flux_of_cells(parity, one, two, *given):
-        def kernel(*refs):
-            flux_kernel(steps, parity, *refs)
-
-        return pl.pallas_call(
-            kernel,
-            in_specs=[VMEM] * (4 + len(given)),
-            out_specs=VMEM,
-            out_shape=tiles(9, LEVELS, CELLS_P, CELLS_T),
-            input_output_aliases={4: 0} if given else {},
-            compiler_params=limit(8),
-            name="flux",
-        )(velocity, magnetic, one, two, *given)
-
-    flux = flux_of_cells(0, one_even, two_even)
     flux = flux_of_cells(1, one_odd, two_odd, flux)
     new_velocity, new_magnetic, payload, _ = pl.pallas_call(
         section,
@@ -622,8 +665,8 @@
         compiler_params=limit(16),
         name="section",
     )(
-        velocity,
-        magnetic,
+        held_vel,
+        held_mag,
         low,
         high,
         one_even,

time: 68.1 us -> 66.7 us (0.979)
  the two profiles are of different devices: /device:TPU:96 before, /device:TPU:448 now
where the time goes in v6:
time: 66.7 us; the launch traced here: 66.3 us
  waiting for transfers between devices  23 us (34%)
  starting transfers between devices  21.5 us (32%)
  blocking collectives  14 us (21%)
  Pallas kernels  6.37 us (10%)
  between operations  0.84 us (1%)
    all_to_all x1, blocking collectives, local(): lax.all_to_all(payload.reshape(pairs, 16, CELLS_T), 'lon', split_axis=0,...  14 us
    ppermute x4, waiting for transfers between devices, along_lon(): return lax.ppermute(block, 'lon', pairs)  12.6 us
    ppermute x4, starting transfers between devices, along_lon(): return lax.ppermute(block, 'lon', pairs)  10.3 us
    ppermute x1, waiting for transfers between devices, local(): far = lax.ppermute(far, ('grid', 'lon'), across)  6.9 us
    ppermute x4, starting transfers between devices, between_lat(): return lax.ppermute(block, ('lat', 'lon'), pairs)  5.17 us
    ppermute x1, starting transfers between devices, local(): near = lax.ppermute(near, 'grid', [(0, 1), (1, 0)])  4.12 us
    ppermute x4, waiting for transfers between devices, between_lat(): return lax.ppermute(block, ('lat', 'lon'), pairs)  3.54 us
    pallas_call x1, Pallas kernels, local(): pl.pallas_call(section, in_specs=[VMEM] * 18, out_specs=[VMEM] * 4, out_s...  2.35 us
  transfers between devices with their start and end apart: 10, of which 7 were waited for; matrix products, arithmetic and copies ran while one was open for 0% of the time, Pallas kernels for 3%

profile of v6, /device:TPU:448, one launch (start us, length us, event | category | flops | bytes accessed | tf_op | source)
XLA Modules:
  0.0 66.3 jit_solution(7056664822614162956)
XLA Ops:
  0.6 1.7 %edges.1 = (f32[32,128]{1,0:T(8,128)S(1)}, f32[32,128]{1,0:T(8,128)S(1)}, f32[11,8,128]{2,1,0:T(8,128)S(1)}, f32[11,8,128]{2,1,0:T(8,128)S(1)}, f32[32,128]{1,0:...) custom-call(f32[1,3,8,32,128]{4,3,2,1,0:T(8,128)} %vel_ref.1, ...), custom_call_target="tpu_custom_call" | custom-call | tf_op jit(solution)/shard_map/edges/pallas_call | solution.py:565
  2.3 6.4 %collective-permute-start.2 = (f32[11,8,128]{2,1,0:T(8,128)S(1)}, f32[11,8,128]{2,1,0:T(8,128)S(1)}, u32[]{:S(2)}, u32[]{:S(2)}) collective-permute-start(f32[11,8,128]{2,1,0:T(8,128)S(1)} %get-tuple-element.30.last_ref.refs_9_), channel_id=1, source_target_pairs={{1,2},{3,4},{5,6},{7,8},{9,10},{11,12},{13,14},{15,16},{17,18},{19... | collective-permute-start | bytes 135176 | tf_op jit(solution)/shard_map/ppermute | solution.py:554
  8.8 1.3 %collective-permute-start.3 = (f32[11,8,128]{2,1,0:T(8,128)S(1)}, f32[11,8,128]{2,1,0:T(8,128)S(1)}, u32[]{:S(2)}, u32[]{:S(2)}) collective-permute-start(f32[11,8,128]{2,1,0:T(8,128)S(1)} %get-tuple-element.31.first_ref.refs_8_), channel_id=1, source_target_pairs={{1,0},{3,2},{5,4},{7,6},{9,8},{11,10},{13,12},{15,14},{17,16},{19,... | collective-permute-start | bytes 135176 | tf_op jit(solution)/shard_map/ppermute | solution.py:554
  10.1 0.7 collective-permute-start
  10.7 0.7 collective-permute-start.1
  11.4 0.0 collective-permute-done.refs_2_.one_ref.refs_4_
  11.4 0.0 collective-permute-done.1.refs_3_.two_ref.refs_5_
  11.4 0.0 copy-start
  11.5 0.0 copy-start.1
  11.5 0.0 copy-start.3
  11.5 2.6 %collective-permute-done.2.before_ref.refs_10_ = f32[11,8,128]{2,1,0:T(8,128)S(1)} collective-permute-done((f32[11,8,128]{2,1,0:T(8,128)S(1)}, f32[11,8,128]{2,1,0:T(8,128)S(1)}, u32[]{:S(2)}, u32[]{:S(2)}) %collective-permute-start.2) | collective-permute-done | bytes 45088 | tf_op jit(solution)/shard_map/ppermute | solution.py:554
  14.0 0.9 %collective-permute-done.3.after_ref.refs_11_ = f32[11,8,128]{2,1,0:T(8,128)S(1)} collective-permute-done((f32[11,8,128]{2,1,0:T(8,128)S(1)}, f32[11,8,128]{2,1,0:T(8,128)S(1)}, u32[]{:S(2)}, u32[]{:S(2)}) %collective-permute-start.3) | collective-permute-done | bytes 45088 | tf_op jit(solution)/shard_map/ppermute | solution.py:554
  14.9 1.3 %collective-permute-start.6 = (f32[12,8,128]{2,1,0:T(8,128)S(1)}, f32[12,8,128]{2,1,0:T(8,128)S(1)}, u32[]{:S(2)}, u32[]{:S(2)}) collective-permute-start(f32[12,8,128]{2,1,0:T(8,128)S(1)} %get-tuple-element.34), channel_id=1, source_target_pairs={{0,1},{2,3},{4,5},{6,7},{8,9},{10,11},{12,13},{14,15},{16,17},{18,... | collective-permute-start | bytes 147464 | tf_op jit(solution)/shard_map/ppermute | solution.py:554
  16.2 1.3 %collective-permute-start.7 = (f32[12,8,128]{2,1,0:T(8,128)S(1)}, f32[12,8,128]{2,1,0:T(8,128)S(1)}, u32[]{:S(2)}, u32[]{:S(2)}) collective-permute-start(f32[12,8,128]{2,1,0:T(8,128)S(1)} %get-tuple-element.35), channel_id=1, source_target_pairs={{2,1},{4,3},{6,5},{8,7},{10,9},{12,11},{14,13},{16,15},{18,17},{20... | collective-permute-start | bytes 147464 | tf_op jit(solution)/shard_map/ppermute | solution.py:554
  17.6 1.9 %collective-permute-start.4 = (f32[32,128]{1,0:T(8,128)S(1)}, f32[32,128]{1,0:T(8,128)S(1)}, u32[]{:S(2)}, u32[]{:S(2)}) collective-permute-start(f32[32,128]{1,0:T(8,128)S(1)} %get-tuple-element.32), channel_id=1, source_target_pairs={{0,32},{1,33},{2,34},{3,35},{4,36},{5,37},{6,38},{7,39},{8,40},{9,... | collective-permute-start | bytes 49160 | tf_op jit(solution)/shard_map/ppermute | solution.py:563
  19.5 1.9 %collective-permute-start.5 = (f32[32,128]{1,0:T(8,128)S(1)}, f32[32,128]{1,0:T(8,128)S(1)}, u32[]{:S(2)}, u32[]{:S(2)}) collective-permute-start(f32[32,128]{1,0:T(8,128)S(1)} %get-tuple-element.33), channel_id=1, source_target_pairs={{32,64},{33,65},{34,66},{35,67},{36,68},{37,69},{38,70},{39,71},{4... | collective-permute-start | bytes 49160 | tf_op jit(solution)/shard_map/ppermute | solution.py:563
  21.4 0.0 copy-done
  21.5 0.1 donors.1
  21.6 2.0 %collective-permute-done.4.refs_2_.refs_6_ = f32[32,128]{1,0:T(8,128)S(1)} collective-permute-done((f32[32,128]{1,0:T(8,128)S(1)}, f32[32,128]{1,0:T(8,128)S(1)}, u32[]{:S(2)}, u32[]{:S(2)}) %collective-permute-start.4) | collective-permute-done | bytes 16416 | tf_op jit(solution)/shard_map/ppermute | solution.py:563
  23.6 1.5 %collective-permute-done.5.refs_3_.refs_7_ = f32[32,128]{1,0:T(8,128)S(1)} collective-permute-done((f32[32,128]{1,0:T(8,128)S(1)}, f32[32,128]{1,0:T(8,128)S(1)}, u32[]{:S(2)}, u32[]{:S(2)}) %collective-permute-start.5) | collective-permute-done | bytes 16416 | tf_op jit(solution)/shard_map/ppermute | solution.py:563
  25.1 0.8 %flux.3.refs_17_ = f32[9,8,32,128]{3,2,1,0:T(8,128)S(1)} custom-call(f32[1,3,8,32,128]{4,3,2,1,0:T(8,128)S(1)} %get-tuple-element.24.refs_0_, f32[1,3,8,32,128]{4,3,2,1,0:T(8,128)S(1)} %get-tuple-element.25.refs_1_, f32[32,128]{1,0:T(8,128)S(1)} %collective-permute-done.4.refs_2_.refs_6_, ...), custom_call_target="tpu_custom_call", output_to_operand_aliasing={{}: (4, {})} | custom-call | tf_op jit(solution)/shard_map/flux/pallas_call | solution.py:595
  26.0 3.7 %collective-permute-done.6.refs_12_ = f32[12,8,128]{2,1,0:T(8,128)S(1)} collective-permute-done((f32[12,8,128]{2,1,0:T(8,128)S(1)}, f32[12,8,128]{2,1,0:T(8,128)S(1)}, u32[]{:S(2)}, u32[]{:S(2)}) %collective-permute-start.6) | collective-permute-done | bytes 49184 | tf_op jit(solution)/shard_map/ppermute | solution.py:554
  29.7 5.4 %collective-permute-done.7.refs_13_ = f32[12,8,128]{2,1,0:T(8,128)S(1)} collective-permute-done((f32[12,8,128]{2,1,0:T(8,128)S(1)}, f32[12,8,128]{2,1,0:T(8,128)S(1)}, u32[]{:S(2)}, u32[]{:S(2)}) %collective-permute-start.7) | collective-permute-done | bytes 49184 | tf_op jit(solution)/shard_map/ppermute | solution.py:554
  35.1 2.4 %section.1 = (f32[1,3,8,32,128]{4,3,2,1,0:T(8,128)S(1)}, f32[1,3,8,32,128]{4,3,2,1,0:T(8,128)S(1)}, f32[32,8,128]{2,1,0:T(8,128)S(1)}, f32[9,8,32,128]{3,2,1,0:T(8,128)S(1)}) custom-call(f32[1,3,8,32,128]{4,3,2,1,0:T(8,128)S(1)} %get-tuple-element.24.refs_0_, f32[1,3,8,32,128]{4,3,2,1,0:T(8,128)S(1)} %get-tuple-element.25.refs_1_, ...), custom_call_target="tpu_custom_call", output_to_operand_aliasing={{3}: (17, {})} | custom-call | tf_op jit(solution)/shard_map/section/pallas_call | solution.py:648
  37.4 14.0 %all_to_all.5.got_ref = f32[16,16,128]{2,1,0:T(8,128)S(1)} all-to-all(f32[16,16,128]{2,1,0:T(8,128)S(1)} %bitcast.1), channel_id=1, replica_groups={{0,2,4,6,8,10,12,14,16,18,20,22,24,26,28,30},{1,3,5,7,9,11,13,15,17,19,..., dimensions={0} | all-to-all | bytes 262144 | tf_op jit(solution)/shard_map/all_to_all | solution.py:698
  51.4 0.5 collect.1
  51.9 1.9 %collective-permute-start.8 = (f32[1,1,1,48,128]{4,3,2,1,0:T(8,128)S(1)}, f32[1,1,1,48,128]{4,3,2,1,0:T(8,128)S(1)}, u32[]{:S(2)}, u32[]{:S(2)}) collective-permute-start(f32[1,1,1,48,128]{4,3,2,1,0:T(8,128)S(1)} %get-tuple-element.43), channel_id=1, source_target_pairs={{0,257},{1,256},{2,259},{3,258},{4,261},{5,260},{6,263},{7,262},{8... | collective-permute-start | bytes 73736 | tf_op jit(solution)/shard_map/ppermute | solution.py:719
  53.8 4.1 %collective-permute-start.9 = (f32[1,1,1,48,128]{4,3,2,1,0:T(8,128)S(1)}, f32[1,1,1,48,128]{4,3,2,1,0:T(8,128)S(1)}, u32[]{:S(2)}, u32[]{:S(2)}) collective-permute-start(f32[1,1,1,48,128]{4,3,2,1,0:T(8,128)S(1)} %get-tuple-element.44), channel_id=1, source_target_pairs={{0,256},{256,0},{1,257},{257,1},{2,258},{258,2},{3,259},{259,3},{4... | collective-permute-start | bytes 73736 | tf_op jit(solution)/shard_map/ppermute | solution.py:720
  57.9 0.9 %store.1 = (f32[1,3,8,32,128]{4,3,2,1,0:T(8,128)}, f32[1,3,8,32,128]{4,3,2,1,0:T(8,128)}) custom-call(f32[1,3,8,32,128]{4,3,2,1,0:T(8,128)S(1)} %get-tuple-element.38.vel_ref, f32[1,3,8,32,128]{4,3,2,1,0:T(8,128)S(1)} %get-tuple-element.39.mag_ref), custom_call_target="tpu_custom_call" | custom-call | tf_op jit(solution)/shard_map/store/pallas_call | solution.py:687
  58.8 6.9 %collective-permute-done.8 = f32[1,1,1,48,128]{4,3,2,1,0:T(8,128)S(1)} collective-permute-done((f32[1,1,1,48,128]{4,3,2,1,0:T(8,128)S(1)}, f32[1,1,1,48,128]{4,3,2,1,0:T(8,128)S(1)}, u32[]{:S(2)}, u32[]{:S(2)}) %collective-permute-start.8) | collective-permute-done | bytes 24608 | tf_op jit(solution)/shard_map/ppermute | solution.py:719
  65.7 0.0 collective-permute-done.9
  65.7 0.6 add.3
  (7 shorter events, 0.1 us)
Async XLA Ops:
  2.3 11.8 %collective-permute-start.2 = (f32[11,8,128]{2,1,0:T(8,128)S(1)}, f32[11,8,128]{2,1,0:T(8,128)S(1)}, u32[]{:S(2)}, u32[]{:S(2)}) collective-permute-start(f32[11,8,128]{2,1,0:T(8,128)S(1)} %get-tuple-element.30.last_ref.refs_9_), channel_id=1, source_target_pairs={{1,2},{3,4},{5,6},{7,8},{9,10},{11,12},{13,14},{15,16},{17,18},{19... | collective-permute-start | bytes 135176 | tf_op jit(solution)/shard_map/ppermute | solution.py:554
  8.8 6.2 %collective-permute-start.3 = (f32[11,8,128]{2,1,0:T(8,128)S(1)}, f32[11,8,128]{2,1,0:T(8,128)S(1)}, u32[]{:S(2)}, u32[]{:S(2)}) collective-permute-start(f32[11,8,128]{2,1,0:T(8,128)S(1)} %get-tuple-element.31.first_ref.refs_8_), channel_id=1, source_target_pairs={{1,0},{3,2},{5,4},{7,6},{9,8},{11,10},{13,12},{15,14},{17,16},{19,... | collective-permute-start | bytes 135176 | tf_op jit(solution)/shard_map/ppermute | solution.py:554
  10.1 1.3 %collective-permute-start = (f32[32,128]{1,0:T(8,128)S(1)}, f32[32,128]{1,0:T(8,128)S(1)}, u32[]{:S(2)}, u32[]{:S(2)}) collective-permute-start(f32[32,128]{1,0:T(8,128)S(1)} %get-tuple-element.28), channel_id=1, source_target_pairs={{0,32},{2,34},{4,36},{6,38},{8,40},{10,42},{12,44},{14,46},{16,48}... | collective-permute-start | bytes 49160 | tf_op jit(solution)/shard_map/ppermute | solution.py:563
  10.7 0.7 %collective-permute-start.1 = (f32[32,128]{1,0:T(8,128)S(1)}, f32[32,128]{1,0:T(8,128)S(1)}, u32[]{:S(2)}, u32[]{:S(2)}) collective-permute-start(f32[32,128]{1,0:T(8,128)S(1)} %get-tuple-element.29), channel_id=1, source_target_pairs={{32,64},{34,66},{36,68},{38,70},{40,72},{42,74},{44,76},{46,78},{4... | collective-permute-start | bytes 49160 | tf_op jit(solution)/shard_map/ppermute | solution.py:563
  11.4 10.0 %copy-start = (s32[1,1,1,512]{3,2,1,0:T(1,128)S(1)}, s32[1,1,1,512]{3,2,1,0:T(1,128)}, u32[]{:S(2)}) copy-start(s32[1,1,1,512]{3,2,1,0:T(1,128)} %refs_1_.1) | copy-start | bytes 6148
  11.5 10.0 %copy-start.1 = (f32[1,1,1,512]{3,2,1,0:T(1,128)S(1)}, f32[1,1,1,512]{3,2,1,0:T(1,128)}, u32[]{:S(2)}) copy-start(f32[1,1,1,512]{3,2,1,0:T(1,128)} %refs_2_.1) | copy-start | bytes 6148
  11.5 10.0 %copy-start.3 = (s32[1,1,1,32]{3,2,1,0:T(1,128)S(1)}, s32[1,1,1,32]{3,2,1,0:T(1,128)}, u32[]{:S(2)}) copy-start(s32[1,1,1,32]{3,2,1,0:T(1,128)} %refs_0_.1) | copy-start | bytes 388
  14.9 14.7 %collective-permute-start.6 = (f32[12,8,128]{2,1,0:T(8,128)S(1)}, f32[12,8,128]{2,1,0:T(8,128)S(1)}, u32[]{:S(2)}, u32[]{:S(2)}) collective-permute-start(f32[12,8,128]{2,1,0:T(8,128)S(1)} %get-tuple-element.34), channel_id=1, source_target_pairs={{0,1},{2,3},{4,5},{6,7},{8,9},{10,11},{12,13},{14,15},{16,17},{18,... | collective-permute-start | bytes 147464 | tf_op jit(solution)/shard_map/ppermute | solution.py:554
  16.2 18.8 %collective-permute-start.7 = (f32[12,8,128]{2,1,0:T(8,128)S(1)}, f32[12,8,128]{2,1,0:T(8,128)S(1)}, u32[]{:S(2)}, u32[]{:S(2)}) collective-permute-start(f32[12,8,128]{2,1,0:T(8,128)S(1)} %get-tuple-element.35), channel_id=1, source_target_pairs={{2,1},{4,3},{6,5},{8,7},{10,9},{12,11},{14,13},{16,15},{18,17},{20... | collective-permute-start | bytes 147464 | tf_op jit(solution)/shard_map/ppermute | solution.py:554
  17.6 6.1 %collective-permute-start.4 = (f32[32,128]{1,0:T(8,128)S(1)}, f32[32,128]{1,0:T(8,128)S(1)}, u32[]{:S(2)}, u32[]{:S(2)}) collective-permute-start(f32[32,128]{1,0:T(8,128)S(1)} %get-tuple-element.32), channel_id=1, source_target_pairs={{0,32},{1,33},{2,34},{3,35},{4,36},{5,37},{6,38},{7,39},{8,40},{9,... | collective-permute-start | bytes 49160 | tf_op jit(solution)/shard_map/ppermute | solution.py:563
  19.5 5.6 %collective-permute-start.5 = (f32[32,128]{1,0:T(8,128)S(1)}, f32[32,128]{1,0:T(8,128)S(1)}, u32[]{:S(2)}, u32[]{:S(2)}) collective-permute-start(f32[32,128]{1,0:T(8,128)S(1)} %get-tuple-element.33), channel_id=1, source_target_pairs={{32,64},{33,65},{34,66},{35,67},{36,68},{37,69},{38,70},{39,71},{4... | collective-permute-start | bytes 49160 | tf_op jit(solution)/shard_map/ppermute | solution.py:563
  21.6 13.5 %copy-start.2 = (s32[1,1,1,512]{3,2,1,0:T(1,128)S(1)}, s32[1,1,1,512]{3,2,1,0:T(1,128)}, u32[]{:S(2)}) copy-start(s32[1,1,1,512]{3,2,1,0:T(1,128)} %refs_16_.1) | copy-start | bytes 6148
  51.9 13.9 %collective-permute-start.8 = (f32[1,1,1,48,128]{4,3,2,1,0:T(8,128)S(1)}, f32[1,1,1,48,128]{4,3,2,1,0:T(8,128)S(1)}, u32[]{:S(2)}, u32[]{:S(2)}) collective-permute-start(f32[1,1,1,48,128]{4,3,2,1,0:T(8,128)S(1)} %get-tuple-element.43), channel_id=1, source_target_pairs={{0,257},{1,256},{2,259},{3,258},{4,261},{5,260},{6,263},{7,262},{8... | collective-permute-start | bytes 73736 | tf_op jit(solution)/shard_map/ppermute | solution.py:719
  53.8 11.9 %collective-permute-start.9 = (f32[1,1,1,48,128]{4,3,2,1,0:T(8,128)S(1)}, f32[1,1,1,48,128]{4,3,2,1,0:T(8,128)S(1)}, u32[]{:S(2)}, u32[]{:S(2)}) collective-permute-start(f32[1,1,1,48,128]{4,3,2,1,0:T(8,128)S(1)} %get-tuple-element.44), channel_id=1, source_target_pairs={{0,256},{256,0},{1,257},{257,1},{2,258},{258,2},{3,259},{259,3},{4... | collective-permute-start | bytes 73736 | tf_op jit(solution)/shard_map/ppermute | solution.py:720

commit v7 on v6

--- a/solution.py
+++ b/solution.py
@@ -509,18 +509,18 @@
     totals = []
     for half in range(2):
         got = got_ref[:, 8 * half : 8 * half + 8].reshape(rows, CELLS_T)
-        total = jnp.zeros((48, CYCLE), F32)
+        onehots = []
         for start in (0, 64):
             slot = got[:, start + 48 : start + 49].astype(jnp.int32)
-            onehot = (slot == lanes_of((rows, CYCLE))).astype(F32)
-            part = lax.dot_general(
-                got,
-                onehot,
-                (((0,), (0,)), ((), ())),
-                precision=lax.Precision.HIGHEST,
-                preferred_element_type=F32,
-            )
-            total = total + part[start : start + 48]
+            onehots.append((slot == lanes_of((rows, CYCLE))).astype(F32))
+        both = lax.dot_general(
+            got,
+            jnp.concatenate(onehots, axis=1),
+            (((0,), (0,)), ((), ())),
+            precision=lax.Precision.HIGHEST,
+            preferred_element_type=F32,
+        )
+        total = both[0:48, 0:CYCLE] + both[64:112, CYCLE:]
         totals.append(total)
     odd = lax.axis_index("lon") % 2 == 1
     near_ref[0, 0, 0] = jnp.where(odd, totals[1], totals[0])

time: 66.7 us -> 66.8 us (level)
  no operation moved by 1% of the time
where the time goes in v7:
time: 66.8 us; the launch traced here: 66.4 us
  waiting for transfers between devices  23 us (34%)
  starting transfers between devices  21.5 us (32%)
  blocking collectives  14 us (21%)
  Pallas kernels  6.41 us (10%)
  between operations  0.84 us (1%)
    all_to_all x1, blocking collectives, local(): lax.all_to_all(payload.reshape(pairs, 16, CELLS_T), 'lon', split_axis=0,...  14 us
    ppermute x4, waiting for transfers between devices, along_lon(): return lax.ppermute(block, 'lon', pairs)  12.6 us
    ppermute x4, starting transfers between devices, along_lon(): return lax.ppermute(block, 'lon', pairs)  10.3 us
    ppermute x1, waiting for transfers between devices, local(): far = lax.ppermute(far, ('grid', 'lon'), across)  6.9 us
    ppermute x4, starting transfers between devices, between_lat(): return lax.ppermute(block, ('lat', 'lon'), pairs)  5.17 us
    ppermute x1, starting transfers between devices, local(): near = lax.ppermute(near, 'grid', [(0, 1), (1, 0)])  4.12 us
    ppermute x4, waiting for transfers between devices, between_lat(): return lax.ppermute(block, ('lat', 'lon'), pairs)  3.54 us
    pallas_call x1, Pallas kernels, local(): pl.pallas_call(section, in_specs=[VMEM] * 18, out_specs=[VMEM] * 4, out_s...  2.35 us
  transfers between devices with their start and end apart: 10, of which 7 were waited for; matrix products, arithmetic and copies ran while one was open for 0% of the time, Pallas kernels for 3%

profile of v7, /device:TPU:448, one launch (start us, length us, event | category | flops | bytes accessed | tf_op | source)
XLA Modules:
  0.0 66.4 jit_solution(559071649258498306)
XLA Ops:
  0.6 1.7 %edges.1 = (f32[32,128]{1,0:T(8,128)S(1)}, f32[32,128]{1,0:T(8,128)S(1)}, f32[11,8,128]{2,1,0:T(8,128)S(1)}, f32[11,8,128]{2,1,0:T(8,128)S(1)}, f32[32,128]{1,0:...) custom-call(f32[1,3,8,32,128]{4,3,2,1,0:T(8,128)} %vel_ref.1, ...), custom_call_target="tpu_custom_call" | custom-call | tf_op jit(solution)/shard_map/edges/pallas_call | solution.py:565
  2.3 6.4 %collective-permute-start.2 = (f32[11,8,128]{2,1,0:T(8,128)S(1)}, f32[11,8,128]{2,1,0:T(8,128)S(1)}, u32[]{:S(2)}, u32[]{:S(2)}) collective-permute-start(f32[11,8,128]{2,1,0:T(8,128)S(1)} %get-tuple-element.30.last_ref.refs_9_), channel_id=1, source_target_pairs={{1,2},{3,4},{5,6},{7,8},{9,10},{11,12},{13,14},{15,16},{17,18},{19... | collective-permute-start | bytes 135176 | tf_op jit(solution)/shard_map/ppermute | solution.py:554
  8.8 1.3 %collective-permute-start.3 = (f32[11,8,128]{2,1,0:T(8,128)S(1)}, f32[11,8,128]{2,1,0:T(8,128)S(1)}, u32[]{:S(2)}, u32[]{:S(2)}) collective-permute-start(f32[11,8,128]{2,1,0:T(8,128)S(1)} %get-tuple-element.31.first_ref.refs_8_), channel_id=1, source_target_pairs={{1,0},{3,2},{5,4},{7,6},{9,8},{11,10},{13,12},{15,14},{17,16},{19,... | collective-permute-start | bytes 135176 | tf_op jit(solution)/shard_map/ppermute | solution.py:554
  10.1 0.7 collective-permute-start
  10.7 0.7 collective-permute-start.1
  11.4 0.0 collective-permute-done.refs_2_.one_ref.refs_4_
  11.4 0.0 collective-permute-done.1.refs_3_.two_ref.refs_5_
  11.4 0.0 copy-start
  11.5 0.0 copy-start.1
  11.5 0.0 copy-start.3
  11.5 2.6 %collective-permute-done.2.before_ref.refs_10_ = f32[11,8,128]{2,1,0:T(8,128)S(1)} collective-permute-done((f32[11,8,128]{2,1,0:T(8,128)S(1)}, f32[11,8,128]{2,1,0:T(8,128)S(1)}, u32[]{:S(2)}, u32[]{:S(2)}) %collective-permute-start.2) | collective-permute-done | bytes 45088 | tf_op jit(solution)/shard_map/ppermute | solution.py:554
  14.0 0.9 %collective-permute-done.3.after_ref.refs_11_ = f32[11,8,128]{2,1,0:T(8,128)S(1)} collective-permute-done((f32[11,8,128]{2,1,0:T(8,128)S(1)}, f32[11,8,128]{2,1,0:T(8,128)S(1)}, u32[]{:S(2)}, u32[]{:S(2)}) %collective-permute-start.3) | collective-permute-done | bytes 45088 | tf_op jit(solution)/shard_map/ppermute | solution.py:554
  14.9 1.3 %collective-permute-start.6 = (f32[12,8,128]{2,1,0:T(8,128)S(1)}, f32[12,8,128]{2,1,0:T(8,128)S(1)}, u32[]{:S(2)}, u32[]{:S(2)}) collective-permute-start(f32[12,8,128]{2,1,0:T(8,128)S(1)} %get-tuple-element.34), channel_id=1, source_target_pairs={{0,1},{2,3},{4,5},{6,7},{8,9},{10,11},{12,13},{14,15},{16,17},{18,... | collective-permute-start | bytes 147464 | tf_op jit(solution)/shard_map/ppermute | solution.py:554
  16.2 1.3 %collective-permute-start.7 = (f32[12,8,128]{2,1,0:T(8,128)S(1)}, f32[12,8,128]{2,1,0:T(8,128)S(1)}, u32[]{:S(2)}, u32[]{:S(2)}) collective-permute-start(f32[12,8,128]{2,1,0:T(8,128)S(1)} %get-tuple-element.35), channel_id=1, source_target_pairs={{2,1},{4,3},{6,5},{8,7},{10,9},{12,11},{14,13},{16,15},{18,17},{20... | collective-permute-start | bytes 147464 | tf_op jit(solution)/shard_map/ppermute | solution.py:554
  17.6 1.9 %collective-permute-start.4 = (f32[32,128]{1,0:T(8,128)S(1)}, f32[32,128]{1,0:T(8,128)S(1)}, u32[]{:S(2)}, u32[]{:S(2)}) collective-permute-start(f32[32,128]{1,0:T(8,128)S(1)} %get-tuple-element.32), channel_id=1, source_target_pairs={{0,32},{1,33},{2,34},{3,35},{4,36},{5,37},{6,38},{7,39},{8,40},{9,... | collective-permute-start | bytes 49160 | tf_op jit(solution)/shard_map/ppermute | solution.py:563
  19.5 1.9 %collective-permute-start.5 = (f32[32,128]{1,0:T(8,128)S(1)}, f32[32,128]{1,0:T(8,128)S(1)}, u32[]{:S(2)}, u32[]{:S(2)}) collective-permute-start(f32[32,128]{1,0:T(8,128)S(1)} %get-tuple-element.33), channel_id=1, source_target_pairs={{32,64},{33,65},{34,66},{35,67},{36,68},{37,69},{38,70},{39,71},{4... | collective-permute-start | bytes 49160 | tf_op jit(solution)/shard_map/ppermute | solution.py:563
  21.4 0.0 copy-done
  21.5 0.1 donors.1
  21.6 2.0 %collective-permute-done.4.refs_2_.refs_6_ = f32[32,128]{1,0:T(8,128)S(1)} collective-permute-done((f32[32,128]{1,0:T(8,128)S(1)}, f32[32,128]{1,0:T(8,128)S(1)}, u32[]{:S(2)}, u32[]{:S(2)}) %collective-permute-start.4) | collective-permute-done | bytes 16416 | tf_op jit(solution)/shard_map/ppermute | solution.py:563
  23.6 1.5 %collective-permute-done.5.refs_3_.refs_7_ = f32[32,128]{1,0:T(8,128)S(1)} collective-permute-done((f32[32,128]{1,0:T(8,128)S(1)}, f32[32,128]{1,0:T(8,128)S(1)}, u32[]{:S(2)}, u32[]{:S(2)}) %collective-permute-start.5) | collective-permute-done | bytes 16416 | tf_op jit(solution)/shard_map/ppermute | solution.py:563
  25.1 0.8 %flux.3.refs_17_ = f32[9,8,32,128]{3,2,1,0:T(8,128)S(1)} custom-call(f32[1,3,8,32,128]{4,3,2,1,0:T(8,128)S(1)} %get-tuple-element.24.refs_0_, f32[1,3,8,32,128]{4,3,2,1,0:T(8,128)S(1)} %get-tuple-element.25.refs_1_, f32[32,128]{1,0:T(8,128)S(1)} %collective-permute-done.4.refs_2_.refs_6_, ...), custom_call_target="tpu_custom_call", output_to_operand_aliasing={{}: (4, {})} | custom-call | tf_op jit(solution)/shard_map/flux/pallas_call | solution.py:595
  26.0 3.7 %collective-permute-done.6.refs_12_ = f32[12,8,128]{2,1,0:T(8,128)S(1)} collective-permute-done((f32[12,8,128]{2,1,0:T(8,128)S(1)}, f32[12,8,128]{2,1,0:T(8,128)S(1)}, u32[]{:S(2)}, u32[]{:S(2)}) %collective-permute-start.6) | collective-permute-done | bytes 49184 | tf_op jit(solution)/shard_map/ppermute | solution.py:554
  29.7 5.4 %collective-permute-done.7.refs_13_ = f32[12,8,128]{2,1,0:T(8,128)S(1)} collective-permute-done((f32[12,8,128]{2,1,0:T(8,128)S(1)}, f32[12,8,128]{2,1,0:T(8,128)S(1)}, u32[]{:S(2)}, u32[]{:S(2)}) %collective-permute-start.7) | collective-permute-done | bytes 49184 | tf_op jit(solution)/shard_map/ppermute | solution.py:554
  35.1 2.4 %section.1 = (f32[1,3,8,32,128]{4,3,2,1,0:T(8,128)S(1)}, f32[1,3,8,32,128]{4,3,2,1,0:T(8,128)S(1)}, f32[32,8,128]{2,1,0:T(8,128)S(1)}, f32[9,8,32,128]{3,2,1,0:T(8,128)S(1)}) custom-call(f32[1,3,8,32,128]{4,3,2,1,0:T(8,128)S(1)} %get-tuple-element.24.refs_0_, f32[1,3,8,32,128]{4,3,2,1,0:T(8,128)S(1)} %get-tuple-element.25.refs_1_, ...), custom_call_target="tpu_custom_call", output_to_operand_aliasing={{3}: (17, {})} | custom-call | tf_op jit(solution)/shard_map/section/pallas_call | solution.py:648
  37.4 14.0 %all_to_all.5.got_ref = f32[16,16,128]{2,1,0:T(8,128)S(1)} all-to-all(f32[16,16,128]{2,1,0:T(8,128)S(1)} %bitcast.1), channel_id=1, replica_groups={{0,2,4,6,8,10,12,14,16,18,20,22,24,26,28,30},{1,3,5,7,9,11,13,15,17,19,..., dimensions={0} | all-to-all | bytes 262144 | tf_op jit(solution)/shard_map/all_to_all | solution.py:698
  51.4 0.5 collect.1
  51.9 1.9 %collective-permute-start.8 = (f32[1,1,1,48,128]{4,3,2,1,0:T(8,128)S(1)}, f32[1,1,1,48,128]{4,3,2,1,0:T(8,128)S(1)}, u32[]{:S(2)}, u32[]{:S(2)}) collective-permute-start(f32[1,1,1,48,128]{4,3,2,1,0:T(8,128)S(1)} %get-tuple-element.43), channel_id=1, source_target_pairs={{0,257},{1,256},{2,259},{3,258},{4,261},{5,260},{6,263},{7,262},{8... | collective-permute-start | bytes 73736 | tf_op jit(solution)/shard_map/ppermute | solution.py:719
  53.8 4.1 %collective-permute-start.9 = (f32[1,1,1,48,128]{4,3,2,1,0:T(8,128)S(1)}, f32[1,1,1,48,128]{4,3,2,1,0:T(8,128)S(1)}, u32[]{:S(2)}, u32[]{:S(2)}) collective-permute-start(f32[1,1,1,48,128]{4,3,2,1,0:T(8,128)S(1)} %get-tuple-element.44), channel_id=1, source_target_pairs={{0,256},{256,0},{1,257},{257,1},{2,258},{258,2},{3,259},{259,3},{4... | collective-permute-start | bytes 73736 | tf_op jit(solution)/shard_map/ppermute | solution.py:720
  58.0 0.9 %store.1 = (f32[1,3,8,32,128]{4,3,2,1,0:T(8,128)}, f32[1,3,8,32,128]{4,3,2,1,0:T(8,128)}) custom-call(f32[1,3,8,32,128]{4,3,2,1,0:T(8,128)S(1)} %get-tuple-element.38.vel_ref, f32[1,3,8,32,128]{4,3,2,1,0:T(8,128)S(1)} %get-tuple-element.39.mag_ref), custom_call_target="tpu_custom_call" | custom-call | tf_op jit(solution)/shard_map/store/pallas_call | solution.py:687
  58.9 6.9 %collective-permute-done.8 = f32[1,1,1,48,128]{4,3,2,1,0:T(8,128)S(1)} collective-permute-done((f32[1,1,1,48,128]{4,3,2,1,0:T(8,128)S(1)}, f32[1,1,1,48,128]{4,3,2,1,0:T(8,128)S(1)}, u32[]{:S(2)}, u32[]{:S(2)}) %collective-permute-start.8) | collective-permute-done | bytes 24608 | tf_op jit(solution)/shard_map/ppermute | solution.py:719
  65.8 0.0 collective-permute-done.9
  65.8 0.6 add.3
  (7 shorter events, 0.1 us)
Async XLA Ops:
  2.3 11.8 %collective-permute-start.2 = (f32[11,8,128]{2,1,0:T(8,128)S(1)}, f32[11,8,128]{2,1,0:T(8,128)S(1)}, u32[]{:S(2)}, u32[]{:S(2)}) collective-permute-start(f32[11,8,128]{2,1,0:T(8,128)S(1)} %get-tuple-element.30.last_ref.refs_9_), channel_id=1, source_target_pairs={{1,2},{3,4},{5,6},{7,8},{9,10},{11,12},{13,14},{15,16},{17,18},{19... | collective-permute-start | bytes 135176 | tf_op jit(solution)/shard_map/ppermute | solution.py:554
  8.8 6.2 %collective-permute-start.3 = (f32[11,8,128]{2,1,0:T(8,128)S(1)}, f32[11,8,128]{2,1,0:T(8,128)S(1)}, u32[]{:S(2)}, u32[]{:S(2)}) collective-permute-start(f32[11,8,128]{2,1,0:T(8,128)S(1)} %get-tuple-element.31.first_ref.refs_8_), channel_id=1, source_target_pairs={{1,0},{3,2},{5,4},{7,6},{9,8},{11,10},{13,12},{15,14},{17,16},{19,... | collective-permute-start | bytes 135176 | tf_op jit(solution)/shard_map/ppermute | solution.py:554
  10.1 1.3 %collective-permute-start = (f32[32,128]{1,0:T(8,128)S(1)}, f32[32,128]{1,0:T(8,128)S(1)}, u32[]{:S(2)}, u32[]{:S(2)}) collective-permute-start(f32[32,128]{1,0:T(8,128)S(1)} %get-tuple-element.28), channel_id=1, source_target_pairs={{0,32},{2,34},{4,36},{6,38},{8,40},{10,42},{12,44},{14,46},{16,48}... | collective-permute-start | bytes 49160 | tf_op jit(solution)/shard_map/ppermute | solution.py:563
  10.7 0.7 %collective-permute-start.1 = (f32[32,128]{1,0:T(8,128)S(1)}, f32[32,128]{1,0:T(8,128)S(1)}, u32[]{:S(2)}, u32[]{:S(2)}) collective-permute-start(f32[32,128]{1,0:T(8,128)S(1)} %get-tuple-element.29), channel_id=1, source_target_pairs={{32,64},{34,66},{36,68},{38,70},{40,72},{42,74},{44,76},{46,78},{4... | collective-permute-start | bytes 49160 | tf_op jit(solution)/shard_map/ppermute | solution.py:563
  11.4 10.0 %copy-start = (s32[1,1,1,512]{3,2,1,0:T(1,128)S(1)}, s32[1,1,1,512]{3,2,1,0:T(1,128)}, u32[]{:S(2)}) copy-start(s32[1,1,1,512]{3,2,1,0:T(1,128)} %refs_1_.1) | copy-start | bytes 6148
  11.5 10.0 %copy-start.1 = (f32[1,1,1,512]{3,2,1,0:T(1,128)S(1)}, f32[1,1,1,512]{3,2,1,0:T(1,128)}, u32[]{:S(2)}) copy-start(f32[1,1,1,512]{3,2,1,0:T(1,128)} %refs_2_.1) | copy-start | bytes 6148
  11.5 10.0 %copy-start.3 = (s32[1,1,1,32]{3,2,1,0:T(1,128)S(1)}, s32[1,1,1,32]{3,2,1,0:T(1,128)}, u32[]{:S(2)}) copy-start(s32[1,1,1,32]{3,2,1,0:T(1,128)} %refs_0_.1) | copy-start | bytes 388
  14.9 14.7 %collective-permute-start.6 = (f32[12,8,128]{2,1,0:T(8,128)S(1)}, f32[12,8,128]{2,1,0:T(8,128)S(1)}, u32[]{:S(2)}, u32[]{:S(2)}) collective-permute-start(f32[12,8,128]{2,1,0:T(8,128)S(1)} %get-tuple-element.34), channel_id=1, source_target_pairs={{0,1},{2,3},{4,5},{6,7},{8,9},{10,11},{12,13},{14,15},{16,17},{18,... | collective-permute-start | bytes 147464 | tf_op jit(solution)/shard_map/ppermute | solution.py:554
  16.2 18.8 %collective-permute-start.7 = (f32[12,8,128]{2,1,0:T(8,128)S(1)}, f32[12,8,128]{2,1,0:T(8,128)S(1)}, u32[]{:S(2)}, u32[]{:S(2)}) collective-permute-start(f32[12,8,128]{2,1,0:T(8,128)S(1)} %get-tuple-element.35), channel_id=1, source_target_pairs={{2,1},{4,3},{6,5},{8,7},{10,9},{12,11},{14,13},{16,15},{18,17},{20... | collective-permute-start | bytes 147464 | tf_op jit(solution)/shard_map/ppermute | solution.py:554
  17.6 6.1 %collective-permute-start.4 = (f32[32,128]{1,0:T(8,128)S(1)}, f32[32,128]{1,0:T(8,128)S(1)}, u32[]{:S(2)}, u32[]{:S(2)}) collective-permute-start(f32[32,128]{1,0:T(8,128)S(1)} %get-tuple-element.32), channel_id=1, source_target_pairs={{0,32},{1,33},{2,34},{3,35},{4,36},{5,37},{6,38},{7,39},{8,40},{9,... | collective-permute-start | bytes 49160 | tf_op jit(solution)/shard_map/ppermute | solution.py:563
  19.5 5.6 %collective-permute-start.5 = (f32[32,128]{1,0:T(8,128)S(1)}, f32[32,128]{1,0:T(8,128)S(1)}, u32[]{:S(2)}, u32[]{:S(2)}) collective-permute-start(f32[32,128]{1,0:T(8,128)S(1)} %get-tuple-element.33), channel_id=1, source_target_pairs={{32,64},{33,65},{34,66},{35,67},{36,68},{37,69},{38,70},{39,71},{4... | collective-permute-start | bytes 49160 | tf_op jit(solution)/shard_map/ppermute | solution.py:563
  21.6 13.5 %copy-start.2 = (s32[1,1,1,512]{3,2,1,0:T(1,128)S(1)}, s32[1,1,1,512]{3,2,1,0:T(1,128)}, u32[]{:S(2)}) copy-start(s32[1,1,1,512]{3,2,1,0:T(1,128)} %refs_16_.1) | copy-start | bytes 6148
  51.9 13.9 %collective-permute-start.8 = (f32[1,1,1,48,128]{4,3,2,1,0:T(8,128)S(1)}, f32[1,1,1,48,128]{4,3,2,1,0:T(8,128)S(1)}, u32[]{:S(2)}, u32[]{:S(2)}) collective-permute-start(f32[1,1,1,48,128]{4,3,2,1,0:T(8,128)S(1)} %get-tuple-element.43), channel_id=1, source_target_pairs={{0,257},{1,256},{2,259},{3,258},{4,261},{5,260},{6,263},{7,262},{8... | collective-permute-start | bytes 73736 | tf_op jit(solution)/shard_map/ppermute | solution.py:719
  53.8 11.9 %collective-permute-start.9 = (f32[1,1,1,48,128]{4,3,2,1,0:T(8,128)S(1)}, f32[1,1,1,48,128]{4,3,2,1,0:T(8,128)S(1)}, u32[]{:S(2)}, u32[]{:S(2)}) collective-permute-start(f32[1,1,1,48,128]{4,3,2,1,0:T(8,128)S(1)} %get-tuple-element.44), channel_id=1, source_target_pairs={{0,256},{256,0},{1,257},{257,1},{2,258},{258,2},{3,259},{259,3},{4... | collective-permute-start | bytes 73736 | tf_op jit(solution)/shard_map/ppermute | solution.py:720
